TPU v7x, 32 devices: a whole 2x2x4 slice. The times are simulated.
32 devices in a mesh: row: 4 (over y, x), col: 8 (over z, core).
Axes of the slice: x: 2, y: 2, z: 4, core: 2. Of those that a mesh axis runs over, the one named last changes fastest.
Arguments:
- inputs: bfloat16 [2048, 2048], P('row', 'col'), may hold values from -6 to 6
- query_weight: bfloat16 [2048, 2048], P('row', 'col'), may hold values from -4 to 4
- key_weight: bfloat16 [2048, 2048], P('row', 'col'), may hold values from -4 to 4
- value_weight: bfloat16 [2048, 2048], P('row', 'col'), may hold values from -0.125 to 0.125
- output_weight: bfloat16 [2048, 2048], P('row', 'col'), may hold values from -4 to 4
- gate_weight: bfloat16 [2048, 8192], P('row', 'col'), may hold values from -0.125 to 0.125
- up_weight: bfloat16 [2048, 8192], P('row', 'col'), may hold values from -0.125 to 0.125
- down_weight: bfloat16 [2048, 8192], P('row', 'col'), may hold values from -4 to 4
- query_gain: float32 [2048], replicated, may hold values from 0.5 to 4.5
- key_gain: float32 [2048], replicated, may hold values from 0.5 to 4.5
- attn_gain: float32 [2048], replicated, may hold values from 0.25 to 1.75
- mlp_gain: float32 [2048], replicated, may hold values from 0.25 to 1.75
- positions: int32 [2048], P('row'), may hold values from 0 to 511, as said below
- segments: int32 [2048], P('row'), may hold values from 0 to 2047, as said below
- cotangent: bfloat16 [2048, 2048], P('row', 'col'), may hold values from -18 to 18
Outputs:
- layer_out: bfloat16 [2048, 2048], P('row', 'col')
- grad_inputs: float32 [2048, 2048], P('row', 'col')
- grad_query: float32 [2048, 2048], P('row', 'col')
- grad_key: float32 [2048, 2048], P('row', 'col')
- grad_value: float32 [2048, 2048], P('row', 'col')
- grad_output: float32 [2048, 2048], P('row', 'col')
- grad_gate: float32 [2048, 8192], P('row', 'col')
- grad_up: float32 [2048, 8192], P('row', 'col')
- grad_down: float32 [2048, 8192], P('row', 'col')
- grad_query_gain: float32 [2048], P('col')
- grad_key_gain: float32 [2048], P('col')
- grad_attn_gain: float32 [2048], P('col')
- grad_mlp_gain: float32 [2048], P('col')
Inputs may be any that keep to these rules, and one draw needn't show every extreme that they name: `segments`: A token's segment number is the index of its segment's first token, so numbers never fall; every sequence of 512 tokens begins a new segment; the first sequence is one segment; the last token is a segment of its own. `positions`: A token's position is the number of earlier tokens of its segment.
All inputs are finite; a program needn't handle non-finite values.
Results may differ from a plain program's by a relative error of at most 0.015.
Values may be sent and summed in bfloat16 or wider, within the bound.
A program may use at most 192 MiB of HBM per device.

v0:
```python
import math

import jax
import jax.numpy as jnp
from jax import lax
from jax.sharding import PartitionSpec as P

HD = 128
LENGTH = 512


EPS = 1e-06
THETA = 500000.0
MASKED = -1e30


def rope_tables(positions, head_size):
    halfway = head_size // 2
    frequency = jnp.exp(
        jnp.arange(halfway, dtype=jnp.float32) * (-2.0 * math.log(THETA) / head_size)
    )
    angles = positions.astype(jnp.float32)[:, None] * frequency[None, :]
    return (jnp.cos(angles)[:, None, :], jnp.sin(angles)[:, None, :])


def rotate(values, cosine, sine):
    halfway = values.shape[-1] // 2
    first_half = values[..., :halfway]
    second_half = values[..., halfway:]
    return jnp.concatenate(
        [first_half * cosine - second_half * sine, second_half * cosine + first_half * sine],
        axis=-1,
    )


def matmul(left, right):
    return jnp.dot(left, right, preferred_element_type=jnp.float32)


def cross_rows(left, right):
    return lax.dot_general(
        left, right, (((0,), (0,)), ((), ())), preferred_element_type=jnp.float32
    )


def cross_cols(left, right):
    return lax.dot_general(
        left, right, (((1,), (1,)), ((), ())), preferred_element_type=jnp.float32
    )


def visible_pairs(segment_part):
    places = jnp.arange(segment_part.shape[0])
    return (segment_part[:, None] == segment_part[None, :]) & (places[:, None] >= places[None, :])


def on_device(
    inputs,
    query_weight,
    key_weight,
    value_weight,
    output_weight,
    gate_weight,
    up_weight,
    down_weight,
    query_gain,
    key_gain,
    attn_gain,
    mlp_gain,
    positions,
    segments,
    cotangent,
):
    bfloat = jnp.bfloat16
    floats = jnp.float32
    rows = inputs.shape[0]
    local_width = inputs.shape[1]
    width = local_width * lax.axis_size("col")
    offset = lax.axis_index("col") * local_width
    head_size = HD
    heads_here = local_width // head_size
    sequences = rows // LENGTH
    scale = head_size ** (-0.5)
    shape_seq = (sequences, LENGTH, heads_here, head_size)

    def mine(values):
        return lax.dynamic_slice_in_dim(values, offset, local_width, values.ndim - 1)

    query_gain_here = mine(query_gain)
    key_gain_here = mine(key_gain)
    cot_here = cotangent.astype(floats)
    gathered = (
        lax.all_gather(query_weight, "row", axis=0, tiled=True),
        lax.all_gather(key_weight, "row", axis=0, tiled=True),
        lax.all_gather(value_weight, "row", axis=0, tiled=True),
        lax.all_gather(gate_weight, "row", axis=0, tiled=True),
        lax.all_gather(up_weight, "row", axis=0, tiled=True),
        lax.all_gather(output_weight, "row", axis=0, tiled=True),
        lax.all_gather(down_weight, "row", axis=0, tiled=True),
    )
    query_full, key_full, value_full, gate_full, up_full, output_full, down_full = gathered
    whole_in = lax.all_gather(inputs, "col", axis=1, tiled=True)
    query_raw = matmul(whole_in, query_full)
    key_raw = matmul(whole_in, key_full)
    value_raw = matmul(whole_in, value_full)
    query_total, key_total = lax.psum(
        (jnp.sum(query_raw * query_raw, axis=1), jnp.sum(key_raw * key_raw, axis=1)), "col"
    )
    query_scale = lax.rsqrt(query_total / width + EPS)[:, None]
    key_scale = lax.rsqrt(key_total / width + EPS)[:, None]
    query_hat = query_raw * query_scale
    key_hat = key_raw * key_scale
    cosine, sine = rope_tables(positions, head_size)
    query_low = (
        rotate((query_hat * query_gain_here).reshape(rows, heads_here, head_size), cosine, sine)
        * scale
    ).astype(bfloat)
    key_low = rotate(
        (key_hat * key_gain_here).reshape(rows, heads_here, head_size), cosine, sine
    ).astype(bfloat)
    value_low = value_raw.astype(bfloat).reshape(rows, heads_here, head_size)
    query_blocks = query_low.reshape(shape_seq)
    key_blocks = key_low.reshape(shape_seq)
    value_blocks = value_low.reshape(shape_seq)
    segment_blocks = segments.reshape(sequences, LENGTH)

    def attend(block):
        queries, keys_part, values_part, segment_part = block
        scores = jnp.einsum("qhd,khd->hqk", queries, keys_part, preferred_element_type=floats)
        scores = jnp.where(visible_pairs(segment_part)[None], scores, MASKED)
        largest = jnp.max(scores, axis=-1, keepdims=True)
        exponent = jnp.exp(scores - largest)
        totals = jnp.sum(exponent, axis=-1, keepdims=True)
        weights_low = (exponent / totals).astype(bfloat)
        attended_part = jnp.einsum(
            "hqk,khd->qhd", weights_low, values_part, preferred_element_type=floats
        )
        return (attended_part, (largest + jnp.log(totals))[..., 0])

    attended, log_totals = lax.map(attend, (query_blocks, key_blocks, value_blocks, segment_blocks))
    attended_low = attended.reshape(rows, local_width).astype(bfloat)
    branch = lax.psum(cross_cols(attended_low, output_full), "col")
    branch_scale = lax.rsqrt(jnp.mean(branch * branch, axis=1, keepdims=True) + EPS)
    branch_hat = branch * branch_scale
    middle = whole_in.astype(floats) + branch_hat * attn_gain
    middle_low = middle.astype(bfloat)
    middle_here = mine(middle)
    branch_hat_here = mine(branch_hat)
    gate_pre = matmul(middle_low, gate_full)
    up_pre = matmul(middle_low, up_full)
    sigma = jax.nn.sigmoid(gate_pre)
    silu_gate = gate_pre * sigma
    mixed_low = (silu_gate * up_pre).astype(bfloat)
    ffn = lax.psum(cross_cols(mixed_low, down_full), "col")
    ffn_scale = lax.rsqrt(jnp.mean(ffn * ffn, axis=1, keepdims=True) + EPS)
    ffn_hat = ffn * ffn_scale
    ffn_hat_here = mine(ffn_hat)
    grad_top = lax.all_gather(cotangent, "col", axis=1, tiled=True).astype(floats)
    normed_top = grad_top * mlp_gain
    inner_top = jnp.sum(normed_top * ffn_hat, axis=1, keepdims=True)
    grad_ffn_low = (ffn_scale * (normed_top - ffn_hat * inner_top / width)).astype(bfloat)
    layer_out = (middle_here + ffn_hat_here * mine(mlp_gain)).astype(bfloat)
    grad_mlp_gain = jnp.sum(cot_here * ffn_hat_here, axis=0)
    grad_down = cross_rows(grad_ffn_low, mixed_low)
    grad_mixed = matmul(grad_ffn_low, down_full)
    grad_gate_low = (grad_mixed * up_pre * sigma * (1.0 + gate_pre * (1.0 - sigma))).astype(bfloat)
    grad_up_low = (grad_mixed * silu_gate).astype(bfloat)
    grad_middle_part = cross_cols(grad_gate_low, gate_full) + cross_cols(grad_up_low, up_full)
    grad_gate = cross_rows(middle_low, grad_gate_low)
    grad_up = cross_rows(middle_low, grad_up_low)
    grad_middle = grad_top + lax.psum(grad_middle_part, "col")
    grad_middle_here = mine(grad_middle)
    grad_attn_gain = jnp.sum(grad_middle_here * branch_hat_here, axis=0)
    normed_mid = grad_middle * attn_gain
    inner_mid = jnp.sum(normed_mid * branch_hat, axis=1, keepdims=True)
    grad_branch_low = (branch_scale * (normed_mid - branch_hat * inner_mid / width)).astype(bfloat)
    grad_output = cross_rows(grad_branch_low, attended_low)
    grad_attended_low = matmul(grad_branch_low, output_full).astype(bfloat)

    def attend_back(block):
        queries, keys_part, values_part, segment_part, log_part, grad_part = block
        scores = jnp.einsum("qhd,khd->hqk", queries, keys_part, preferred_element_type=floats)
        scores = jnp.where(visible_pairs(segment_part)[None], scores, MASKED)
        probs = jnp.exp(scores - log_part[..., None])
        grad_values = jnp.einsum(
            "hqk,qhd->khd", probs.astype(bfloat), grad_part, preferred_element_type=floats
        )
        grad_probs = jnp.einsum(
            "qhd,khd->hqk", grad_part, values_part, preferred_element_type=floats
        )
        grad_scores = probs * (grad_probs - jnp.sum(probs * grad_probs, axis=-1, keepdims=True))
        scores_low = grad_scores.astype(bfloat)
        grad_queries = jnp.einsum(
            "hqk,khd->qhd", scores_low, keys_part, preferred_element_type=floats
        )
        grad_keys = jnp.einsum("hqk,qhd->khd", scores_low, queries, preferred_element_type=floats)
        return (grad_queries, grad_keys, grad_values.astype(bfloat))

    grad_queries, grad_keys, grad_values = lax.map(
        attend_back,
        (
            query_blocks,
            key_blocks,
            value_blocks,
            segment_blocks,
            log_totals,
            grad_attended_low.reshape(shape_seq),
        ),
    )
    grad_query_norm = rotate(
        grad_queries.reshape(rows, heads_here, head_size) * scale, cosine, -sine
    ).reshape(rows, local_width)
    grad_key_norm = rotate(grad_keys.reshape(rows, heads_here, head_size), cosine, -sine).reshape(
        rows, local_width
    )
    grad_query_gain = jnp.sum(grad_query_norm * query_hat, axis=0)
    grad_key_gain = jnp.sum(grad_key_norm * key_hat, axis=0)
    normed_query = grad_query_norm * query_gain_here
    normed_key = grad_key_norm * key_gain_here
    inner_query, inner_key = lax.psum(
        (jnp.sum(normed_query * query_hat, axis=1), jnp.sum(normed_key * key_hat, axis=1)), "col"
    )
    grad_query_low = (
        query_scale * (normed_query - query_hat * inner_query[:, None] / width)
    ).astype(bfloat)
    grad_key_low = (key_scale * (normed_key - key_hat * inner_key[:, None] / width)).astype(bfloat)
    grad_value_low = grad_values.reshape(rows, local_width)
    grad_in_part = (
        cross_cols(grad_query_low, query_full)
        + cross_cols(grad_key_low, key_full)
        + cross_cols(grad_value_low, value_full)
    )
    grad_inputs = grad_middle_here + lax.psum_scatter(
        grad_in_part, "col", scatter_dimension=1, tiled=True
    )
    grad_query = cross_rows(whole_in, grad_query_low)
    grad_key = cross_rows(whole_in, grad_key_low)
    grad_value = cross_rows(whole_in, grad_value_low)
    summed = (
        lax.psum_scatter(grad_query, "row", scatter_dimension=0, tiled=True),
        lax.psum_scatter(grad_key, "row", scatter_dimension=0, tiled=True),
        lax.psum_scatter(grad_value, "row", scatter_dimension=0, tiled=True),
        lax.psum_scatter(grad_output, "row", scatter_dimension=0, tiled=True),
        lax.psum_scatter(grad_gate, "row", scatter_dimension=0, tiled=True),
        lax.psum_scatter(grad_up, "row", scatter_dimension=0, tiled=True),
        lax.psum_scatter(grad_down, "row", scatter_dimension=0, tiled=True),
    )
    gains = lax.psum((grad_query_gain, grad_key_gain, grad_attn_gain, grad_mlp_gain), "row")
    return (
        layer_out,
        grad_inputs,
        summed[0],
        summed[1],
        summed[2],
        summed[3],
        summed[4],
        summed[5],
        summed[6],
        gains[0],
        gains[1],
        gains[2],
        gains[3],
    )


def solution(mesh):
    in_specs = (
        P("row", "col"),
        P("row", "col"),
        P("row", "col"),
        P("row", "col"),
        P("row", "col"),
        P("row", "col"),
        P("row", "col"),
        P("row", "col"),
        P(),
        P(),
        P(),
        P(),
        P("row"),
        P("row"),
        P("row", "col"),
    )
    out_specs = (
        P("row", "col"),
        P("row", "col"),
        P("row", "col"),
        P("row", "col"),
        P("row", "col"),
        P("row", "col"),
        P("row", "col"),
        P("row", "col"),
        P("row", "col"),
        P("col"),
        P("col"),
        P("col"),
        P("col"),
    )
    return jax.shard_map(
        on_device, mesh=mesh, in_specs=in_specs, out_specs=out_specs, check_vma=False
    )
```

profile of v0, /device:TPU:0, one launch (start us, length us, event | category | flops | bytes accessed | tf_op | source)
XLA Modules:
  0.0 1192.4 jit_solution(15415583480090670992)
XLA Ops:
  15.7 23.5 %all-gather.16.cloned.1.call-done = bf16[2048,256]{1,0:T(8,128)(2,1)} async-done(((bf16[512,256]{1,0:T(8,128)(2,1)}), bf16[2048,256]{1,0:T(8,128)(2,1)}) %all-gather.16.cloned.1.call-update) | async-done | bytes 1048592 | tf_op jit(solution)/shard_map/all_gather | solution.py:94
  39.2 32.5 %all-gather.10.cloned.1.call-done = bf16[512,2048]{1,0:T(8,128)(2,1)} async-done(((bf16[512,256]{1,0:T(8,128)(2,1)}), bf16[512,2048]{1,0:T(8,128)(2,1)}) %all-gather.10.cloned.1.call-update) | async-done | bytes 2097168 | tf_op jit(solution)/shard_map/all_gather | solution.py:102
  74.5 24.8 %all-gather.14.cloned.1.call-done = bf16[2048,256]{1,0:T(8,128)(2,1)} async-done(((bf16[512,256]{1,0:T(8,128)(2,1)}), bf16[2048,256]{1,0:T(8,128)(2,1)}) %all-gather.14.cloned.1.call-update) | async-done | bytes 1048592 | tf_op jit(solution)/shard_map/all_gather | solution.py:93
  101.2 16.4 %all-reduce.1 = (f32[512]{0:T(512)S(1)}, f32[512]{0:T(512)S(1)}) all-reduce(f32[512]{0:T(512)S(1)} %get-tuple-element.121, f32[512]{0:T(512)S(1)} %get-tuple-element.123), channel_id=1, replica_groups=mesh['row'=4,'col'=8] {'col'}, use_global_device_ids=true, to_apply=%region_1.0 | all-reduce | flops 1024 | bytes 8192 | tf_op jit(solution)/shard_map/psum | solution.py:106
  132.4 23.6 %all-gather.18.cloned.1.call-done = bf16[2048,256]{1,0:T(8,128)(2,1)} async-done(((bf16[512,256]{1,0:T(8,128)(2,1)}), bf16[2048,256]{1,0:T(8,128)(2,1)}) %all-gather.18.cloned.1.call-update) | async-done | bytes 1048592 | tf_op jit(solution)/shard_map/all_gather | solution.py:98
  162.8 93.8 %all-reduce.7.cloned.1.call-done = f32[512,2048]{1,0:T(8,128)} async-done(((f32[512,2048]{1,0:T(8,128)}), f32[512,2048]{1,0:T(8,128)}) %all-reduce.7.cloned.1.call-update) | async-done | bytes 4194320 | tf_op jit(solution)/shard_map/psum | solution.py:142
  259.5 8.1 fusion.23
  267.6 43.7 %all-gather.20.cloned.1.call-done = bf16[2048,1024]{1,0:T(8,128)(2,1)} async-done(((bf16[512,1024]{1,0:T(8,128)(2,1)}), bf16[2048,1024]{1,0:T(8,128)(2,1)}) %all-gather.20.cloned.1.call-update) | async-done | bytes 4194320 | tf_op jit(solution)/shard_map/all_gather | solution.py:96
  317.8 48.1 %all-gather.22.cloned.1.call-done = bf16[2048,1024]{1,0:T(8,128)(2,1)} async-done(((bf16[512,1024]{1,0:T(8,128)(2,1)}), bf16[2048,1024]{1,0:T(8,128)(2,1)}) %all-gather.22.cloned.1.call-update) | async-done | bytes 4194320 | tf_op jit(solution)/shard_map/all_gather | solution.py:97
  365.9 7.5 multiply_convert_fusion.4
  373.4 47.1 %all-gather.24.cloned.1.call-done = bf16[2048,1024]{1,0:T(8,128)(2,1)} async-done(((bf16[512,1024]{1,0:T(8,128)(2,1)}), bf16[2048,1024]{1,0:T(8,128)(2,1)}) %all-gather.24.cloned.1.call-update) | async-done | bytes 4194320 | tf_op jit(solution)/shard_map/all_gather | solution.py:99
  420.5 6.8 fusion.28
  428.3 95.7 %all-reduce.9.cloned.1.call-done = f32[512,2048]{1,0:T(8,128)} async-done(((f32[512,2048]{1,0:T(8,128)}), f32[512,2048]{1,0:T(8,128)}) %all-reduce.9.cloned.1.call-update) | async-done | bytes 4194320 | tf_op jit(solution)/shard_map/psum | solution.py:154
  526.6 30.0 %all-gather.26.cloned.1.call-done = bf16[512,2048]{1,0:T(8,128)(2,1)} async-done(((bf16[512,256]{1,0:T(8,128)(2,1)}), bf16[512,2048]{1,0:T(8,128)(2,1)}) %all-gather.26.cloned.1.call-update) | async-done | bytes 2097168 | tf_op jit(solution)/shard_map/all_gather | solution.py:158
  576.7 95.5 %all-reduce.11.cloned.1.call-done = f32[512,2048]{1,0:T(8,128)} async-done(((f32[512,2048]{1,0:T(8,128)}), f32[512,2048]{1,0:T(8,128)}) %all-reduce.11.cloned.1.call-update) | async-done | bytes 4194320 | tf_op jit(solution)/shard_map/psum | solution.py:171
  694.8 15.6 %all-reduce = (f32[512]{0:T(512)S(1)}, f32[512]{0:T(512)S(1)}) all-reduce(f32[512]{0:T(512)S(1)} %get-tuple-element.80, f32[512]{0:T(512)S(1)} %get-tuple-element.78), channel_id=1, replica_groups=mesh['row'=4,'col'=8] {'col'}, use_global_device_ids=true, to_apply=%region_15.16 | all-reduce | flops 1024 | bytes 8192 | tf_op jit(solution)/shard_map/psum | solution.py:220
  760.8 26.9 %reduce-scatter.15.cloned.1.call-done = f32[512,256]{0,1:T(8,128)} async-done(((f32[2048,256]{0,1:T(8,128)}), f32[512,256]{0,1:T(8,128)}) %reduce-scatter.15.cloned.1.call-update) | async-done | bytes 524304 | tf_op jit(solution)/shard_map/reduce_scatter | solution.py:242
  789.8 36.0 %reduce-scatter.13.cloned.1.call-done = f32[512,256]{0,1:T(8,128)} async-done(((f32[2048,256]{0,1:T(8,128)}), f32[512,256]{0,1:T(8,128)}) %reduce-scatter.13.cloned.1.call-update) | async-done | bytes 524304 | tf_op jit(solution)/shard_map/reduce_scatter | solution.py:241
  827.8 50.3 %reduce-scatter.9.cloned.1.call-done = f32[512,256]{1,0:T(8,128)} async-done(((f32[512,2048]{1,0:T(8,128)}), f32[512,256]{1,0:T(8,128)}) %reduce-scatter.9.cloned.1.call-update) | async-done | bytes 524304 | tf_op jit(solution)/shard_map/reduce_scatter | solution.py:233
  880.3 10.5 all-reduce.2
  890.8 24.3 %reduce-scatter.17.cloned.1.call-done = f32[512,256]{1,0:T(8,128)} async-done(((f32[2048,256]{1,0:T(8,128)}), f32[512,256]{1,0:T(8,128)}) %reduce-scatter.17.cloned.1.call-update) | async-done | bytes 524304 | tf_op jit(solution)/shard_map/reduce_scatter | solution.py:243
  915.1 89.9 %reduce-scatter.23.cloned.1.call-done = f32[512,1024]{1,0:T(8,128)} async-done(((f32[2048,1024]{1,0:T(8,128)}), f32[512,1024]{1,0:T(8,128)}) %reduce-scatter.23.cloned.1.call-update) | async-done | bytes 2097168 | tf_op jit(solution)/shard_map/reduce_scatter | solution.py:246
  1005.0 90.4 %reduce-scatter.21.cloned.1.call-done = f32[512,1024]{1,0:T(8,128)} async-done(((f32[2048,1024]{1,0:T(8,128)}), f32[512,1024]{1,0:T(8,128)}) %reduce-scatter.21.cloned.1.call-update) | async-done | bytes 2097168 | tf_op jit(solution)/shard_map/reduce_scatter | solution.py:245
  1095.4 89.9 %reduce-scatter.19.cloned.1.call-done = f32[512,1024]{1,0:T(8,128)} async-done(((f32[2048,1024]{1,0:T(8,128)}), f32[512,1024]{1,0:T(8,128)}) %reduce-scatter.19.cloned.1.call-update) | async-done | bytes 2097168 | tf_op jit(solution)/shard_map/reduce_scatter | solution.py:244
  (210 shorter events, 146.5 us)
Async XLA Ops:
  7.2 32.0 %all-gather.16.cloned.1.call-start = ((), (), s32[]{:S(2)}) async-start(), calls=%async_computation.11 | async-start | bytes 1310720 | tf_op jit(solution)/shard_map/all_gather | solution.py:94
  7.9 63.8 %all-gather.10.cloned.1.call-start = ((), (), s32[]{:S(2)}) async-start(), calls=%async_computation.8 | async-start | bytes 2359296 | tf_op jit(solution)/shard_map/all_gather | solution.py:102
  8.7 90.6 %all-gather.14.cloned.1.call-start = ((), (), s32[]{:S(2)}) async-start(), calls=%async_computation.10 | async-start | bytes 1310720 | tf_op jit(solution)/shard_map/all_gather | solution.py:93
  9.4 118.2 %all-gather.12.cloned.1.call-start = ((), (), s32[]{:S(2)}) async-start(), calls=%async_computation.9 | async-start | bytes 1310720 | tf_op jit(solution)/shard_map/all_gather | solution.py:95
  10.0 146.0 %all-gather.18.cloned.1.call-start = ((), (), s32[]{:S(2)}) async-start(), calls=%async_computation.12 | async-start | bytes 1310720 | tf_op jit(solution)/shard_map/all_gather | solution.py:98
  10.6 246.1 %all-reduce.7.cloned.1.call-start = ((), (), s32[]{:S(2)}) async-start(), calls=%async_computation.13 | async-start | bytes 8388608 | tf_op jit(solution)/shard_map/psum | solution.py:142
  71.7 27.6 %copy-start.1 = (bf16[512,2048]{1,0:T(8,128)(2,1)S(1)}, bf16[512,2048]{1,0:T(8,128)(2,1)}, u32[]{:S(2)}) copy-start(bf16[512,2048]{1,0:T(8,128)(2,1)} %all-gather.10.cloned.1.call-done) | copy-start | bytes 6291460
  160.0 151.3 %all-gather.20.cloned.1.call-start = ((), (), s32[]{:S(2)}) async-start(), calls=%async_computation.14 | async-start | bytes 5242880 | tf_op jit(solution)/shard_map/all_gather | solution.py:96
  160.8 205.1 %all-gather.22.cloned.1.call-start = ((), (), s32[]{:S(2)}) async-start(), calls=%async_computation.15 | async-start | bytes 5242880 | tf_op jit(solution)/shard_map/all_gather | solution.py:97
  161.5 259.0 %all-gather.24.cloned.1.call-start = ((), (), s32[]{:S(2)}) async-start(), calls=%async_computation.16 | async-start | bytes 5242880 | tf_op jit(solution)/shard_map/all_gather | solution.py:99
  162.3 97.1 %copy-start.38 = (f32[2048]{0:T(1024)S(1)}, f32[2048]{0:T(1024)}, u32[]{:S(2)}) copy-start(f32[2048]{0:T(1024)} %param.25) | copy-start | bytes 24580
  162.3 361.8 %all-reduce.9.cloned.1.call-start = ((), (), s32[]{:S(2)}) async-start(), calls=%async_computation.17 | async-start | bytes 8388608 | tf_op jit(solution)/shard_map/psum | solution.py:154
  427.4 129.2 %all-gather.26.cloned.1.call-start = ((), (), s32[]{:S(2)}) async-start(), calls=%async_computation.18 | async-start | bytes 2359296 | tf_op jit(solution)/shard_map/all_gather | solution.py:158
  428.1 128.5 %copy-start.39 = (f32[2048]{0:T(1024)S(1)}, f32[2048]{0:T(1024)}, u32[]{:S(2)}) copy-start(f32[2048]{0:T(1024)} %param.26) | copy-start | bytes 24580
  428.1 244.0 %all-reduce.11.cloned.1.call-start = ((), (), s32[]{:S(2)}) async-start(), calls=%async_computation.19 | async-start | bytes 8388608 | tf_op jit(solution)/shard_map/psum | solution.py:171
  562.5 6.5 copy-start.21
  576.4 182.3 %reduce-scatter.11.cloned.1.call-start = ((), (), s32[]{:S(2)}) async-start(), calls=%async_computation.21 | async-start | bytes 2621440 | tf_op jit(solution)/shard_map/reduce_scatter | solution.py:240
  715.9 71.8 %reduce-scatter.15.cloned.1.call-start = ((), (), s32[]{:S(2)}) async-start(), calls=%async_computation.23 | async-start | bytes 2621440 | tf_op jit(solution)/shard_map/reduce_scatter | solution.py:242
  720.5 105.2 %reduce-scatter.13.cloned.1.call-start = ((), (), s32[]{:S(2)}) async-start(), calls=%async_computation.22 | async-start | bytes 2621440 | tf_op jit(solution)/shard_map/reduce_scatter | solution.py:241
  724.2 153.8 %reduce-scatter.9.cloned.1.call-start = ((), (), s32[]{:S(2)}) async-start(), calls=%async_computation.20 | async-start | bytes 4718592 | tf_op jit(solution)/shard_map/reduce_scatter | solution.py:233
  730.4 184.7 %reduce-scatter.17.cloned.1.call-start = ((), (), s32[]{:S(2)}) async-start(), calls=%async_computation.24 | async-start | bytes 2621440 | tf_op jit(solution)/shard_map/reduce_scatter | solution.py:243
  734.1 270.9 %reduce-scatter.23.cloned.1.call-start = ((), (), s32[]{:S(2)}) async-start(), calls=%async_computation.27 | async-start | bytes 10485760 | tf_op jit(solution)/shard_map/reduce_scatter | solution.py:246
  741.4 354.0 %reduce-scatter.21.cloned.1.call-start = ((), (), s32[]{:S(2)}) async-start(), calls=%async_computation.26 | async-start | bytes 10485760 | tf_op jit(solution)/shard_map/reduce_scatter | solution.py:245
  748.9 436.4 %reduce-scatter.19.cloned.1.call-start = ((), (), s32[]{:S(2)}) async-start(), calls=%async_computation.25 | async-start | bytes 10485760 | tf_op jit(solution)/shard_map/reduce_scatter | solution.py:244
  (46 other events, 95.2 us)
Sparse Core Ops, SparseCore 0:
  9.9 29.3 all-gather.15
  40.8 30.8 all-gather.9
  73.5 25.6 all-gather.13
  100.9 26.6 all-gather.11
  129.3 26.6 all-gather.17
  160.1 96.4 all-reduce.6
  258.5 52.7 all-gather.19
  313.2 52.6 all-gather.21
  367.7 52.6 all-gather.23
  427.5 96.5 all-reduce.8
  525.6 30.8 all-gather.25
  576.5 95.5 all-reduce.10
  716.0 33.3 reduce-scatter.10
  752.5 35.1 reduce-scatter.14
  790.5 35.1 reduce-scatter.12
  828.0 49.9 reduce-scatter.8
  881.7 33.3 reduce-scatter.16
  918.6 86.3 reduce-scatter.22
  1009.0 86.3 reduce-scatter.20
  1098.9 86.3 reduce-scatter.18
where the time goes:
time: 1200 us; the launch traced here: 1190 us
  waiting for transfers between devices  974 us (81%)
  matrix products  78.5 us (7%)
  other arithmetic  42.7 us (4%)
  blocking collectives  42.4 us (4%)
  local copies, waits for them, and re-layouts  37.8 us (3%)
  between operations  15.2 us (1%)
    psum x1, waiting for transfers between devices, on_device(): ffn = lax.psum(cross_cols(mixed_low, down_full), 'col')  95.7 us
    psum x1, waiting for transfers between devices, on_device(): grad_middle = grad_top + lax.psum(grad_middle_part, 'col')  95.5 us
    psum x1, waiting for transfers between devices, on_device(): branch = lax.psum(cross_cols(attended_low, output_full), 'col')  93.8 us
    reduce_scatter x1, waiting for transfers between devices, on_device(): lax.psum_scatter(grad_up, 'row', scatter_dimension=0, tiled=True)  90.4 us
    reduce_scatter x1, waiting for transfers between devices, on_device(): lax.psum_scatter(grad_down, 'row', scatter_dimension=0, tiled=True)  89.9 us
    reduce_scatter x1, waiting for transfers between devices, on_device(): lax.psum_scatter(grad_gate, 'row', scatter_dimension=0, tiled=True)  89.9 us
    reduce_scatter x1, waiting for transfers between devices, on_device(): lax.psum_scatter(grad_in_part, 'col', scatter_dimension=1, tiled=True)  50.3 us
    all_gather x1, waiting for transfers between devices, on_device(): lax.all_gather(up_weight, 'row', axis=0, tiled=True)  48.1 us
  transfers between devices with their start and end apart: 20, of which 19 were waited for; matrix products, arithmetic and copies ran while one was open for 7% of the time, Pallas kernels for 0%

commit v1 on v0

--- a/solution.py
+++ b/solution.py
@@ -3,6 +3,8 @@
 import jax
 import jax.numpy as jnp
 from jax import lax
+from jax.experimental import pallas as pl
+from jax.experimental.pallas import tpu as pltpu
 from jax.sharding import PartitionSpec as P
 
 HD = 128
@@ -263,6 +265,789 @@
     )
 
 
+BF = jnp.bfloat16
+F32 = jnp.float32
+MESH_ID = pl.DeviceIdType.MESH
+T = 512
+DC = 256
+DR = 512
+D = 2048
+FH = 512
+LAYER_STAGES = 5
+EXACT = lax.Precision.HIGHEST
+
+
+def dot_nn(a, b):
+    return jnp.dot(a, b, preferred_element_type=F32)
+
+
+def dot_nt(a, b, precision=None):
+    return lax.dot_general(
+        a, b, (((1,), (1,)), ((), ())), precision=precision, preferred_element_type=F32
+    )
+
+
+def dot_tn(a, b, precision=None):
+    return lax.dot_general(
+        a, b, (((0,), (0,)), ((), ())), precision=precision, preferred_element_type=F32
+    )
+
+
+def aligned(start, size):
+    return pl.ds(pl.multiple_of(start, size), size)
+
+
+class Counter:
+    def __init__(self):
+        self.used = 0
+
+    def take(self, count=1):
+        first = self.used
+        self.used += count
+        return first
+
+
+def block_kernel(
+    x_hbm,
+    wq_hbm,
+    wk_hbm,
+    wv_hbm,
+    wo_hbm,
+    wg_hbm,
+    wu_hbm,
+    wd_hbm,
+    cot_hbm,
+    gains_ref,
+    pos_ref,
+    layer_out,
+    grad_in,
+    gains_out,
+    land_down,
+    land_gu,
+    land_o,
+    land_qkv,
+    wqkv,
+    wo,
+    wgu,
+    wd,
+    x_full,
+    mid_full,
+    gf_full,
+    gb_full,
+    gu_s,
+    mixed_s,
+    ggu_s,
+    probs_s,
+    hat_s,
+    low_s,
+    cos_s,
+    sin_s,
+    cot_s,
+    middle_s,
+    bhat_s,
+    work_s,
+    att_s,
+    ga_s,
+    gqkv_s,
+    gs_s,
+    pl_s,
+    gqk_s,
+    own_s,
+    stage_c,
+    land_c,
+    stage_y,
+    land_y,
+    stage_z,
+    land_z,
+    scal_s,
+    gain_s,
+    stage_down,
+    stage_gu,
+    out_lo,
+    send_sem,
+    recv_sem,
+    local_sem,
+):
+    row = lax.axis_index("row")
+    col = lax.axis_index("col")
+    x_at = lax.rem(row, 2)
+    y_at = lax.div(row, 2)
+    core = lax.rem(col, 2)
+    z_at = lax.div(col, 2)
+    row_x = row + 1 - 2 * x_at
+    row_y = lax.rem(row + 2, 4)
+    row_d = row_y + 1 - 2 * x_at
+    sib = col + 1 - 2 * core
+    dev_x = (row_x, col)
+    dev_y = (row_y, col)
+    dev_d = (row_d, col)
+    dev_c = (row, sib)
+
+    def dev_z(step):
+        return (row, lax.rem(col + 2 * step, 8))
+
+    def col_from(step):
+        return lax.rem(col + 8 - 2 * step, 8)
+
+    def sib_from(step):
+        return lax.rem(sib + 8 - 2 * step, 8)
+
+    counter = Counter()
+    locals_used = Counter()
+    pending = []
+
+    def copy_of(index, src, dst, device):
+        return pltpu.make_async_remote_copy(
+            src_ref=src,
+            dst_ref=dst,
+            send_sem=send_sem.at[index],
+            recv_sem=recv_sem.at[index],
+            device_id=device,
+            device_id_type=MESH_ID,
+        )
+
+    def send(index, src, dst, device):
+        copy = copy_of(index, src, dst, device)
+        copy.start()
+        pending.append(copy)
+        return copy
+
+    def arrived(index, dst):
+        copy_of(index, dst, dst, dev_c).wait_recv()
+
+    def sent(copy):
+        copy.wait_send()
+        pending[:] = [other for other in pending if other is not copy]
+
+    def local(src, dst):
+        copy = pltpu.make_async_copy(src, dst, local_sem.at[locals_used.take()])
+        copy.start()
+        return copy
+
+    barrier = pltpu.get_barrier_semaphore()
+    partners = [dev_x, dev_y, dev_d] + [(row, lax.rem(col + step, 8)) for step in range(1, 8)]
+    for device in partners:
+        pl.semaphore_signal(barrier, inc=1, device_id=device, device_id_type=MESH_ID)
+    local_copies = []
+    for index, ref in enumerate((wq_hbm, wk_hbm, wv_hbm)):
+        local_copies.append(local(ref, wqkv.at[aligned(row * DR, DR), pl.ds(index * DC, DC)]))
+    local_copies.append(local(wo_hbm, wo.at[aligned(row * DR, DR), :]))
+    half_mine = aligned(y_at * FH, FH)
+    half_other = aligned((1 - y_at) * FH, FH)
+    local_copies.append(local(wg_hbm.at[:, half_mine], wgu.at[aligned(row * DR, DR), pl.ds(0, FH)]))
+    local_copies.append(local(wu_hbm.at[:, half_mine], wgu.at[aligned(row * DR, DR), pl.ds(FH, FH)]))
+    local_copies.append(local(wd_hbm.at[:, half_mine], wd.at[aligned(row * DR, DR), :]))
+    local_copies.append(local(x_hbm, x_full.at[:, aligned(col * DC, DC)]))
+    local_copies.append(local(cot_hbm, cot_s))
+    pl.semaphore_wait(barrier, len(partners))
+
+    def gather_block(buf, rows, at):
+        return buf.at[rows, aligned(at * DC, DC)]
+
+    class Gather:
+        def __init__(self, buf, plane):
+            self.buf = buf
+            self.plane = plane
+            self.base_z = counter.take(3)
+            self.base_c = counter.take(4)
+            if plane:
+                self.base_y = counter.take(4)
+                self.base_cy = counter.take(4)
+                self.rows = aligned(y_at * T, T)
+                self.rows_other = aligned((1 - y_at) * T, T)
+            else:
+                self.rows = pl.ds(0, T)
+
+        def start(self, source=None):
+            own = gather_block(self.buf, self.rows, col)
+            src = own if source is None else source
+            for step in (1, 2, 3):
+                send(self.base_z + step - 1, src, own, dev_z(step))
+            if self.plane:
+                send(self.base_y, src, own, dev_y)
+            send(self.base_c, src, own, dev_c)
+
+        def finish(self):
+            for step in (1, 2, 3):
+                block = gather_block(self.buf, self.rows, col_from(step))
+                arrived(self.base_z + step - 1, block)
+                if self.plane:
+                    send(self.base_y + step, block, block, dev_y)
+                send(self.base_c + step, block, block, dev_c)
+            if self.plane:
+                for step in range(4):
+                    block = gather_block(self.buf, self.rows_other, col_from(step))
+                    arrived(self.base_y + step, block)
+                    send(self.base_cy + step, block, block, dev_c)
+            for step in range(4):
+                arrived(self.base_c + step, gather_block(self.buf, self.rows, sib_from(step)))
+                if self.plane:
+                    arrived(
+                        self.base_cy + step, gather_block(self.buf, self.rows_other, sib_from(step))
+                    )
+
+    class Reduce:
+        ORDER = (1, 2, 3, 0)
+
+        def __init__(self, partial, plane):
+            self.partial = partial
+            self.plane = plane
+            self.count = 2 * T if plane else T
+            self.base_c = counter.take(4)
+            self.base_z = counter.take(3)
+            if plane:
+                self.base_y = counter.take(4)
+                self.rows = aligned(y_at * T, T)
+                self.rows_other = aligned((1 - y_at) * T, T)
+            else:
+                self.rows = pl.ds(0, T)
+            self.sent = []
+
+        def start(self):
+            count = self.count
+            for slot, step in enumerate(self.ORDER):
+                target = lax.rem(z_at + step, 4)
+                start = pl.multiple_of((2 * target + 1 - core) * DC, DC)
+                stage_c[slot, :count, :] = self.partial(start).astype(BF)
+                self.sent.append(
+                    send(
+                        self.base_c + slot,
+                        stage_c.at[slot, pl.ds(0, count), :],
+                        land_c.at[slot, pl.ds(0, count), :],
+                        dev_c,
+                    )
+                )
+                start = pl.multiple_of((2 * target + core) * DC, DC)
+                own_s[slot, :count, :] = self.partial(start)
+
+        def cores(self):
+            count = self.count
+            for slot, step in enumerate(self.ORDER):
+                arrived(self.base_c + slot, land_c.at[slot, pl.ds(0, count), :])
+                if self.plane:
+                    rows = self.rows_other
+                    stage_y[slot] = (
+                        own_s[slot, rows, :] + land_c[slot, rows, :].astype(F32)
+                    ).astype(BF)
+                    self.sent.append(
+                        send(self.base_y + slot, stage_y.at[slot], land_y.at[slot], dev_y)
+                    )
+                    rows = self.rows
+                    own_s[slot, rows, :] = own_s[slot, rows, :] + land_c[slot, rows, :].astype(F32)
+                else:
+                    self.pass_on(slot, step, land_c.at[slot, pl.ds(0, T), :])
+
+        def pass_on(self, slot, step, landed):
+            total = own_s[slot, self.rows, :] + landed[...].astype(F32)
+            if step == 0:
+                own_s[slot, self.rows, :] = total
+            else:
+                stage_z[slot] = total.astype(BF)
+                self.sent.append(
+                    send(self.base_z + slot, stage_z.at[slot], land_z.at[slot], dev_z(step))
+                )
+
+        def planes(self):
+            if self.plane:
+                for slot, step in enumerate(self.ORDER):
+                    arrived(self.base_y + slot, land_y.at[slot])
+                    self.pass_on(slot, step, land_y.at[slot])
+
+        def finish(self):
+            for slot in range(3):
+                arrived(self.base_z + slot, land_z.at[slot])
+            total = own_s[3, self.rows, :]
+            for slot in range(3):
+                total = total + land_z[slot].astype(F32)
+            for copy in self.sent:
+                sent(copy)
+            return total
+
+    pick = lax.broadcasted_iota(jnp.int32, (8, DC), 0)
+    lane = lax.broadcasted_iota(jnp.int32, (8, DC), 1)
+    first_row = (pick == 0).astype(F32)
+    second_row = (pick == 1).astype(F32)
+    spread = ((pick == 0) & (lane < 128)).astype(F32) + ((pick == 1) & (lane >= 128)).astype(F32)
+
+    def sums_over_col(stage, first, second):
+        base = counter.take(7)
+        mine = dot_nt(first_row, first, EXACT)
+        if second is not None:
+            mine = mine + dot_nt(second_row, second, EXACT)
+        scal_s[stage, col] = mine
+        for step in range(1, 8):
+            send(
+                base + step - 1,
+                scal_s.at[stage, col],
+                scal_s.at[stage, col],
+                (row, lax.rem(col + step, 8)),
+            )
+        for step in range(1, 8):
+            arrived(base + step - 1, scal_s.at[stage, lax.rem(col + 8 - step, 8)])
+        total = scal_s[stage, 0]
+        for index in range(1, 8):
+            total = total + scal_s[stage, index]
+        both = dot_tn(total, spread, EXACT)
+        return both[:, :128], both[:, 128:]
+
+    def wide(values):
+        return jnp.concatenate([values, values], axis=1)
+
+    x_gather = Gather(x_full, False)
+    attn_base = counter.take(16)
+
+    def attn_place(index, owner, part=None):
+        if part is None:
+            rows = aligned(owner * DR, DR)
+        else:
+            rows = aligned(owner * DR + part * (DR // 2), DR // 2)
+        if index < 3:
+            return wqkv.at[rows, pl.ds(index * DC, DC)]
+        return wo.at[rows, :]
+
+    attn_hbm = (wq_hbm, wk_hbm, wv_hbm, wo_hbm)
+
+    def attn_send(index):
+        send(attn_base + index, attn_hbm[index], attn_place(index, row), dev_x)
+        send(attn_base + 4 + index, attn_hbm[index], attn_place(index, row), dev_y)
+
+    def attn_relay(index):
+        arrived(attn_base + index, attn_place(index, row_x))
+        part = attn_place(index, row_x, 0)
+        send(attn_base + 8 + index, part, part, dev_y)
+        arrived(attn_base + 4 + index, attn_place(index, row_y))
+        part = attn_place(index, row_y, 1)
+        send(attn_base + 12 + index, part, part, dev_x)
+
+    def attn_ready(index):
+        arrived(attn_base + 8 + index, attn_place(index, row_d, 0))
+        arrived(attn_base + 12 + index, attn_place(index, row_d, 1))
+
+    mlp_base = counter.take(9)
+    mlp_hbm = (wg_hbm, wu_hbm, wd_hbm)
+
+    def mlp_place(index, owner):
+        rows = aligned(owner * DR, DR)
+        if index < 2:
+            return wgu.at[rows, pl.ds(index * FH, FH)]
+        return wd.at[rows, :]
+
+    def mlp_send(index):
+        send(mlp_base + index, mlp_hbm[index].at[:, half_mine], mlp_place(index, row), dev_x)
+        send(mlp_base + 3 + index, mlp_hbm[index].at[:, half_other], mlp_place(index, row), dev_y)
+
+    def mlp_relay(index):
+        place = mlp_place(index, row_y)
+        arrived(mlp_base + 3 + index, place)
+        send(mlp_base + 6 + index, place, place, dev_x)
+
+    def mlp_ready(index):
+        arrived(mlp_base + index, mlp_place(index, row_x))
+        arrived(mlp_base + 6 + index, mlp_place(index, row_d))
+
+    for index in range(3):
+        attn_send(index)
+    x_gather.start(x_hbm)
+
+    lane_at = lax.broadcasted_iota(jnp.int32, (1, HD), 1)
+    within = lax.rem(lane_at, HD // 2).astype(F32)
+    frequency = jnp.exp(within * (-2.0 * math.log(THETA) / HD))
+    angles = pos_ref[...].astype(F32) * frequency
+    cos_s[...] = jnp.cos(angles)
+    sine = jnp.sin(angles)
+    sin_s[...] = jnp.where(lane_at < HD // 2, -sine, sine)
+
+    for index in range(3):
+        attn_relay(index)
+    attn_send(3)
+    for copy in local_copies:
+        copy.wait()
+    x_gather.finish()
+    for index in range(3):
+        attn_ready(index)
+
+    gains = gains_ref[:, aligned(col * DC, DC)]
+    raw = []
+    for index in range(3):
+        raw.append(dot_nn(x_full[...], wqkv[:, pl.ds(index * DC, DC)]))
+    low_s[2] = raw[2].astype(BF)
+    hat_s[0] = raw[0]
+    hat_s[1] = raw[1]
+    attn_relay(3)
+    for index in range(3):
+        mlp_send(index)
+    totals = sums_over_col(0, raw[0] * raw[0], raw[1] * raw[1])
+    scales = [lax.rsqrt(total / D + EPS) for total in totals]
+    work_s[0] = jnp.concatenate(scales, axis=1)
+    for index in range(2):
+        hat = hat_s[index] * wide(scales[index])
+        hat_s[index] = hat
+        normed = hat * gains[index : index + 1, :]
+        for head in range(2):
+            part = normed[:, head * HD : (head + 1) * HD]
+            turned = part * cos_s[...] + pltpu.roll(part, HD // 2, 1) * sin_s[...]
+            if index == 0:
+                turned = turned * (HD**-0.5)
+            low_s[index, :, pl.ds(head * HD, HD)] = turned.astype(BF)
+
+    chunk = 128
+
+    def visible(at):
+        query = at * chunk + lax.broadcasted_iota(jnp.int32, (chunk, T), 0)
+        key = lax.broadcasted_iota(jnp.int32, (chunk, T), 1)
+        oldest = query - pos_ref[aligned(at * chunk, chunk), :]
+        return (key <= query) & (key >= oldest)
+
+    def attend_chunk(at, carry):
+        rows = aligned(at * chunk, chunk)
+        allowed = visible(at)
+        for head in range(2):
+            lanes = pl.ds(head * HD, HD)
+            scores = dot_nt(low_s[0, rows, lanes], low_s[1, :, lanes])
+            scores = jnp.where(allowed, scores, MASKED)
+            exponent = jnp.exp(scores - jnp.max(scores, axis=1, keepdims=True))
+            probs = exponent / jnp.sum(exponent, axis=1, keepdims=True)
+            probs_s[head, rows, :] = probs
+            att_s[rows, lanes] = dot_nn(probs.astype(BF), low_s[2, :, lanes]).astype(BF)
+        return carry
+
+    lax.fori_loop(0, T // chunk, attend_chunk, 0)
+
+    attn_ready(3)
+    branch_sum = Reduce(lambda start: dot_nt(att_s[...], wo[pl.ds(start, DC), :]), False)
+    branch_sum.start()
+    branch_sum.cores()
+    mlp_relay(0)
+    branch = branch_sum.finish()
+    work_s[1] = branch
+    mlp_relay(1)
+    total, _ = sums_over_col(1, branch * branch, None)
+    branch_scale = lax.rsqrt(total / D + EPS)
+    work_s[2, :, :128] = branch_scale
+    branch_hat = work_s[1] * wide(branch_scale)
+    bhat_s[...] = branch_hat
+    middle = x_hbm_slice(x_full, col) + branch_hat * gains[2:3, :]
+    middle_s[...] = middle
+    mid_full[aligned(y_at * T, T), aligned(col * DC, DC)] = middle.astype(BF)
+    mid_gather = Gather(mid_full, True)
+    mid_gather.start()
+    mlp_relay(2)
+    mid_gather.finish()
+    mlp_ready(0)
+    mlp_ready(1)
+
+    tile = 256
+
+    def forward_tile(at, carry):
+        rows = aligned(lax.div(at, 2) * T, T)
+        lane_start = lax.rem(at, 2) * tile
+        lanes = aligned(lane_start, tile)
+        lanes_up = aligned(lane_start + FH, tile)
+        gate = dot_nn(mid_full[rows, :], wgu[:, lanes])
+        up = dot_nn(mid_full[rows, :], wgu[:, lanes_up])
+        gu_s[rows, lanes] = gate
+        gu_s[rows, lanes_up] = up
+        mixed_s[rows, lanes] = (gate * jax.nn.sigmoid(gate) * up).astype(BF)
+        return carry
+
+    lax.fori_loop(0, 4, forward_tile, 0)
+    mlp_ready(2)
+    ffn_sum = Reduce(lambda start: dot_nt(mixed_s[...], wd[pl.ds(start, DC), :]), True)
+    ffn_sum.start()
+    ffn_sum.cores()
+    ffn_sum.planes()
+    ffn = ffn_sum.finish()
+    work_s[1] = ffn
+    cot_gain = cot_s[...].astype(F32) * gains[3:4, :]
+    total, inner = sums_over_col(2, ffn * ffn, cot_gain * ffn)
+    ffn_scale = lax.rsqrt(total / D + EPS)
+    ffn_hat = work_s[1] * wide(ffn_scale)
+    cot = cot_s[...].astype(F32)
+    out_lo[...] = (middle_s[...] + ffn_hat * gains[3:4, :]).astype(BF)
+    lo_copy = local(out_lo, layer_out)
+    gain_s[row, 3:4, :] = jnp.sum(cot * ffn_hat, axis=0, keepdims=True)
+    inner = wide(inner * ffn_scale / D)
+    grad_ffn = wide(ffn_scale) * (cot * gains[3:4, :] - ffn_hat * inner)
+    gf_full[aligned(y_at * T, T), aligned(col * DC, DC)] = grad_ffn.astype(BF)
+    gf_gather = Gather(gf_full, True)
+    gf_gather.start()
+    gf_gather.finish()
+
+    def backward_tile(at, carry):
+        rows = aligned(lax.div(at, 2) * T, T)
+        lane_start = lax.rem(at, 2) * tile
+        lanes = aligned(lane_start, tile)
+        lanes_up = aligned(lane_start + FH, tile)
+        grad_mixed = dot_nn(gf_full[rows, :], wd[:, lanes])
+        gate = gu_s[rows, lanes]
+        up = gu_s[rows, lanes_up]
+        sigma = jax.nn.sigmoid(gate)
+        ggu_s[rows, lanes] = (grad_mixed * up * sigma * (1.0 + gate * (1.0 - sigma))).astype(BF)
+        ggu_s[rows, lanes_up] = (grad_mixed * gate * sigma).astype(BF)
+        return carry
+
+    lax.fori_loop(0, 4, backward_tile, 0)
+    mid_sum = Reduce(lambda start: dot_nt(ggu_s[...], wgu[pl.ds(start, DC), :]), True)
+    mid_sum.start()
+    mid_sum.cores()
+
+    order = ((row_x, dev_x), (row_y, dev_y), (row_d, dev_d), (row, None))
+
+    def push(stage, slot, land, base, device):
+        if device is None:
+            return local(stage.at[slot], land.at[row])
+        return send(base + slot, stage.at[slot], land.at[row], device)
+
+    pushes = []
+    down_base = counter.take(3)
+    for slot, (owner, device) in enumerate(order):
+        lanes = aligned(owner * DR, DR)
+        stage_down[slot] = dot_tn(gf_full[:, lanes], mixed_s[...]).astype(BF)
+        pushes.append(push(stage_down, slot, land_down, down_base, device))
+    mid_sum.planes()
+    gu_base = counter.take(3)
+    gu_pushes = []
+    for slot, (owner, device) in enumerate(order):
+        lanes = aligned(owner * DR, DR)
+        for part in range(2):
+            half = pl.ds(part * FH, FH)
+            stage_gu[slot, :, half] = dot_tn(mid_full[:, lanes], ggu_s[:, half]).astype(BF)
+        gu_pushes.append(push(stage_gu, slot, land_gu, gu_base, device))
+    grad_middle = cot_s[...].astype(F32) + mid_sum.finish()
+    middle_s[...] = grad_middle
+    gain_s[row, 2:3, :] = jnp.sum(grad_middle * bhat_s[...], axis=0, keepdims=True)
+    inner, _ = sums_over_col(3, grad_middle * gains[2:3, :] * bhat_s[...], None)
+    branch_scale = wide(work_s[2, :, :128])
+    grad_branch = branch_scale * (
+        middle_s[...] * gains[2:3, :] - bhat_s[...] * wide(inner / D)
+    )
+    gb_full[:, aligned(col * DC, DC)] = grad_branch.astype(BF)
+    gb_gather = Gather(gb_full, False)
+    gb_gather.start()
+    gb_gather.finish()
+
+    ga_s[...] = dot_nn(gb_full[...], wo[...]).astype(BF)
+
+    def attend_back_chunk(at, carry):
+        rows = aligned(at * chunk, chunk)
+        for head in range(2):
+            lanes = pl.ds(head * HD, HD)
+            grad_probs = dot_nt(ga_s[rows, lanes], low_s[2, :, lanes])
+            probs = probs_s[head, rows, :]
+            weighted = probs * grad_probs
+            inner = jnp.sum(weighted, axis=1, keepdims=True)
+            grad_scores = (probs * (grad_probs - inner)).astype(BF)
+            gs_s[head, rows, :] = grad_scores
+            pl_s[head, rows, :] = probs.astype(BF)
+            gqk_s[0, rows, lanes] = dot_nn(grad_scores, low_s[1, :, lanes])
+        return carry
+
+    lax.fori_loop(0, T // chunk, attend_back_chunk, 0)
+    for head in range(2):
+        lanes = pl.ds(head * HD, HD)
+        gqk_s[1, :, lanes] = dot_tn(gs_s[head], low_s[0, :, lanes])
+        gqkv_s[:, pl.ds(2 * DC + head * HD, HD)] = dot_tn(pl_s[head], ga_s[:, lanes]).astype(BF)
+    inners = []
+    for index in range(2):
+        for head in range(2):
+            lanes = pl.ds(head * HD, HD)
+            part = gqk_s[index, :, lanes]
+            turned = part * cos_s[...] - pltpu.roll(part, HD // 2, 1) * sin_s[...]
+            if index == 0:
+                turned = turned * (HD**-0.5)
+            gqk_s[index, :, lanes] = turned
+        weighted = gqk_s[index] * hat_s[index]
+        gain_s[row, index : index + 1, :] = jnp.sum(weighted, axis=0, keepdims=True)
+        inners.append(weighted * gains[index : index + 1, :])
+    gain_base = counter.take(3)
+    for slot, (_, device) in enumerate(order[:3]):
+        send(gain_base + slot, gain_s.at[row], gain_s.at[row], device)
+    totals = sums_over_col(4, inners[0], inners[1])
+    for index in range(2):
+        scale = wide(work_s[0, :, index * 128 : (index + 1) * 128])
+        gqkv_s[:, pl.ds(index * DC, DC)] = (
+            scale
+            * (
+                gqk_s[index] * gains[index : index + 1, :]
+                - hat_s[index] * wide(totals[index] / D)
+            )
+        ).astype(BF)
+
+    for group in (pushes, gu_pushes):
+        for copy in group[:3]:
+            sent(copy)
+        group[3].wait()
+    in_sum = Reduce(lambda start: dot_nt(gqkv_s[...], wqkv[pl.ds(start, DC), :]), False)
+    in_sum.start()
+    in_sum.cores()
+    o_base = counter.take(3)
+    qkv_base = counter.take(3)
+    late = []
+    for slot, (owner, device) in enumerate(order):
+        lanes = aligned(owner * DR, DR)
+        stage_gu[slot, :, pl.ds(0, 3 * DC)] = dot_tn(x_full[:, lanes], gqkv_s[...]).astype(BF)
+        source = stage_gu.at[slot, :, pl.ds(0, 3 * DC)]
+        if device is None:
+            late.append(local(source, land_qkv.at[row]))
+        else:
+            send(qkv_base + slot, source, land_qkv.at[row], device)
+        stage_down[slot, :, pl.ds(0, DC)] = dot_tn(gb_full[:, lanes], att_s[...]).astype(BF)
+        source = stage_down.at[slot, :, pl.ds(0, DC)]
+        if device is None:
+            late.append(local(source, land_o.at[row]))
+        else:
+            send(o_base + slot, source, land_o.at[row], device)
+    work_s[1] = middle_s[...] + in_sum.finish()
+    late.append(local(work_s.at[1], grad_in))
+    late.append(lo_copy)
+
+    sources = (row_x, row_y, row_d)
+    for slot, owner in enumerate(sources):
+        arrived(gain_base + slot, gain_s.at[owner])
+    gains_out[...] = gain_s[0] + gain_s[1] + gain_s[2] + gain_s[3]
+    for slot, owner in enumerate(sources):
+        arrived(down_base + slot, land_down.at[owner])
+        arrived(gu_base + slot, land_gu.at[owner])
+        arrived(o_base + slot, land_o.at[owner])
+        arrived(qkv_base + slot, land_qkv.at[owner])
+    for copy in late:
+        copy.wait()
+    for copy in pending:
+        copy.wait_send()
+
+
+def x_hbm_slice(x_full, col):
+    return x_full[:, aligned(col * DC, DC)].astype(F32)
+
+
+MIB = 1 << 20
+
+
+def on_device_kernel(
+    inputs,
+    query_weight,
+    key_weight,
+    value_weight,
+    output_weight,
+    gate_weight,
+    up_weight,
+    down_weight,
+    query_gain,
+    key_gain,
+    attn_gain,
+    mlp_gain,
+    positions,
+    segments,
+    cotangent,
+):
+    gains = jnp.stack([query_gain, key_gain, attn_gain, mlp_gain])
+    gains = jnp.concatenate([gains, jnp.zeros_like(gains)], axis=0)
+    hbm = pl.BlockSpec(memory_space=pl.ANY)
+    vmem = pl.BlockSpec(memory_space=pltpu.VMEM)
+    sds = jax.ShapeDtypeStruct
+    copies = 230
+    results = pl.pallas_call(
+        block_kernel,
+        out_shape=[
+            sds((T, DC), BF),
+            sds((T, DC), F32),
+            sds((8, DC), F32),
+            sds((4, DR, FH), BF),
+            sds((4, DR, 2 * FH), BF),
+            sds((4, DR, DC), BF),
+            sds((4, DR, 3 * DC), BF),
+        ],
+        in_specs=[hbm] * 9 + [vmem, vmem],
+        out_specs=[hbm, hbm, vmem, hbm, hbm, hbm, hbm],
+        scratch_shapes=[
+            pltpu.VMEM((D, 3 * DC), BF),
+            pltpu.VMEM((D, DC), BF),
+            pltpu.VMEM((D, 2 * FH), BF),
+            pltpu.VMEM((D, FH), BF),
+            pltpu.VMEM((T, D), BF),
+            pltpu.VMEM((2 * T, D), BF),
+            pltpu.VMEM((2 * T, D), BF),
+            pltpu.VMEM((T, D), BF),
+            pltpu.VMEM((2 * T, 2 * FH), F32),
+            pltpu.VMEM((2 * T, FH), BF),
+            pltpu.VMEM((2 * T, 2 * FH), BF),
+            pltpu.VMEM((2, T, T), F32),
+            pltpu.VMEM((2, T, DC), F32),
+            pltpu.VMEM((3, T, DC), BF),
+            pltpu.VMEM((T, HD), F32),
+            pltpu.VMEM((T, HD), F32),
+            pltpu.VMEM((T, DC), BF),
+            pltpu.VMEM((T, DC), F32),
+            pltpu.VMEM((T, DC), F32),
+            pltpu.VMEM((3, T, DC), F32),
+            pltpu.VMEM((T, DC), BF),
+            pltpu.VMEM((T, DC), BF),
+            pltpu.VMEM((T, 3 * DC), BF),
+            pltpu.VMEM((2, T, T), BF),
+            pltpu.VMEM((2, T, T), BF),
+            pltpu.VMEM((2, T, DC), F32),
+            pltpu.VMEM((4, 2 * T, DC), F32),
+            pltpu.VMEM((4, 2 * T, DC), BF),
+            pltpu.VMEM((4, 2 * T, DC), BF),
+            pltpu.VMEM((4, T, DC), BF),
+            pltpu.VMEM((4, T, DC), BF),
+            pltpu.VMEM((3, T, DC), BF),
+            pltpu.VMEM((3, T, DC), BF),
+            pltpu.VMEM((LAYER_STAGES, 8, 8, T), F32),
+            pltpu.VMEM((4, 8, DC), F32),
+            pltpu.VMEM((4, DR, FH), BF),
+            pltpu.VMEM((4, DR, 2 * FH), BF),
+            pltpu.VMEM((T, DC), BF),
+            pltpu.SemaphoreType.DMA((copies,)),
+            pltpu.SemaphoreType.DMA((copies,)),
+            pltpu.SemaphoreType.DMA((32,)),
+        ],
+        compiler_params=pltpu.CompilerParams(
+            collective_id=0, has_side_effects=True, vmem_limit_bytes=64 * MIB
+        ),
+        cost_estimate=pl.CostEstimate(
+            flops=26_800_000_000, bytes_accessed=16_000_000, transcendentals=2_000_000
+        ),
+    )(
+        inputs,
+        query_weight,
+        key_weight,
+        value_weight,
+        output_weight,
+        gate_weight,
+        up_weight,
+        down_weight,
+        cotangent,
+        gains,
+        positions[:, None],
+    )
+    layer_out, grad_in, gains_out, land_down, land_gu, land_o, land_qkv = results
+
+    def halves(landed):
+        landed = landed.astype(F32)
+        return jnp.concatenate([landed[0] + landed[1], landed[2] + landed[3]], axis=1)
+
+    def total(landed):
+        landed = landed.astype(F32)
+        return landed[0] + landed[1] + landed[2] + landed[3]
+
+    return (
+        layer_out,
+        grad_in,
+        total(land_qkv[:, :, :DC]),
+        total(land_qkv[:, :, DC : 2 * DC]),
+        total(land_qkv[:, :, 2 * DC :]),
+        total(land_o),
+        halves(land_gu[:, :, :FH]),
+        halves(land_gu[:, :, FH:]),
+        halves(land_down),
+        gains_out[0],
+        gains_out[1],
+        gains_out[2],
+        gains_out[3],
+    )
+
+
 def solution(mesh):
     in_specs = (
         P("row", "col"),
@@ -296,6 +1081,8 @@
         P("col"),
         P("col"),
     )
+    sizes = (mesh.shape["row"], mesh.shape["col"])
+    body = on_device_kernel if sizes == (4, 8) else on_device
     return jax.shard_map(
-        on_device, mesh=mesh, in_specs=in_specs, out_specs=out_specs, check_vma=False
-    )
+        body, mesh=mesh, in_specs=in_specs, out_specs=out_specs, check_vma=False
+    )

time: 1200 us -> 384 us (0.32)
  waiting for transfers between devices: 974 us -> 0 us
  Pallas kernels: 0 us -> 355 us
  matrix products: 78.5 us -> 0 us
  blocking collectives: 42.4 us -> 0 us
  other arithmetic: 42.7 us -> 12.2 us
  local copies, waits for them, and re-layouts: 37.8 us -> 8.47 us
  between operations: 15.2 us -> 1.18 us
    reduce_scatter x8 -> x0, waiting for transfers between devices: 408 us -> none  [the longest x1 90.4 us: on_device(): lax.psum_scatter(grad_up, 'row', scatter_dimension=0, tiled=True)]
    pallas_call x0 -> x1, Pallas kernels: none -> 355 us  [on_device_kernel(): pl.pallas_call(block_kernel, out_shape=[sds((T, DC), BF), sds((T, DC), F3...]
    psum x3 -> x0, waiting for transfers between devices: 285 us -> none  [the longest x1 95.7 us: on_device(): ffn = lax.psum(cross_cols(mixed_low, down_full), 'col')]
    all_gather x9 -> x0, waiting for transfers between devices: 275 us -> none  [the longest x1 48.1 us: on_device(): lax.all_gather(up_weight, 'row', axis=0, tiled=True)]
    dot_general x27 -> x0, matrix products: 78.5 us -> none  [the longest x7 26.9 us: cross_rows(): lax.dot_general(left, right, (((0,), (0,)), ((), ())), preferred_element_...]
    psum x3 -> x0, blocking collectives: 42.4 us -> none  [the longest x1 16.4 us: on_device(): lax.psum((jnp.sum(query_raw * query_raw, axis=1), jnp.sum(key_raw * key_r...]
    unnamed x107 -> x12, local copies, waits for them, and re-layouts: 31.3 us -> 4.02 us
    reduce_sum x9 -> x0, other arithmetic: 21 us -> none  [the longest x1 4.95 us: on_device(): inner_mid = jnp.sum(normed_mid * branch_hat, axis=1, keepdims=True)]
  transfers between devices with their start and end apart: 20 -> 0, of which waited for: 19 -> 0; matrix products, arithmetic and copies ran while one was open for 7% -> 0% of each run, Pallas kernels for 0% -> 0%
where the time goes in v1:
time: 384 us; the launch traced here: 377 us
  Pallas kernels  355 us (92%)
  other arithmetic  12.2 us (3%)
  local copies, waits for them, and re-layouts  8.47 us (2%)
    pallas_call x1, Pallas kernels, on_device_kernel(): pl.pallas_call(block_kernel, out_shape=[sds((T, DC), BF), sds((T, DC), F3...  355 us

profile of v1, /device:TPU:0, one launch (start us, length us, event | category | flops | bytes accessed | tf_op | source)
XLA Modules:
  0.0 376.8 jit_solution(5763126823879607672)
XLA Ops:
  0.7 1.4 concatenate.12.gains_ref
  2.1 1.5 copy.27.pos_ref
  3.6 355.0 %shard_map.237 = (bf16[512,256]{1,0:T(8,128)(2,1)}, f32[512,256]{1,0:T(8,128)}, f32[8,256]{1,0:T(8,128)}, bf16[4,512,512]{2,1,0:T(8,128)(2,1)}, bf16[4,512,1024]...) custom-call(bf16[512,256]{1,0:T(8,128)(2,1)} %x_hbm.1, bf16[512,256]{1,0:T(8,128)(2,1)} %wq_hbm.1, ...), custom_call_target="tpu_custom_call" | custom-call | flops 26800001024 | bytes 16000000 | tf_op jit(solution)/shard_map/pallas_call | solution.py:949
  358.6 0.0 copy-start.2
  358.6 1.5 fusion.10
  360.1 1.4 convert_element_type.24
  361.5 0.0 copy-done.2
  361.5 0.6 convert_element_type.27
  362.1 0.5 fusion.1
  362.6 0.0 copy-start.1
  362.6 1.5 pad_maximum_fusion.2
  364.1 1.2 copy-done.1
  365.2 0.6 slice_convert_fusion.2
  365.9 1.2 fusion.6
  367.1 1.2 fusion.7
  368.3 1.3 copy-done
  369.7 1.3 slice_convert_fusion
  370.9 1.0 fusion.3
  372.0 1.5 pad_maximum_fusion.1
  373.4 1.5 pad_maximum_fusion
  374.9 0.0 copy-done.4
  374.9 0.7 copy.30
  375.6 0.0 copy-done.3
  375.6 0.8 copy.31
  (4 shorter events, 0.0 us)
Async XLA Ops:
  358.6 2.9 copy-start.2
  362.6 2.6 copy-start.1
  367.1 2.6 copy-start
  373.4 1.5 copy-start.4
  373.4 2.2 copy-start.3

commit v2 on v1

--- a/solution.py
+++ b/solution.py
@@ -317,15 +317,16 @@
     wu_hbm,
     wd_hbm,
     cot_hbm,
-    gains_ref,
+    query_gain_ref,
+    key_gain_ref,
+    attn_gain_ref,
+    mlp_gain_ref,
     pos_ref,
     layer_out,
     grad_in,
     gains_out,
-    land_down,
-    land_gu,
-    land_o,
-    land_qkv,
+    land_mlp,
+    land_attn,
     wqkv,
     wo,
     wgu,
@@ -336,13 +337,15 @@
     gb_full,
     gu_s,
     mixed_s,
-    ggu_s,
     probs_s,
     hat_s,
     low_s,
     cos_s,
     sin_s,
-    cot_s,
+    pos_s,
+    cot_z,
+    braw_s,
+    raw_s,
     middle_s,
     bhat_s,
     work_s,
@@ -350,7 +353,6 @@
     ga_s,
     gqkv_s,
     gs_s,
-    pl_s,
     gqk_s,
     own_s,
     stage_c,
@@ -363,6 +365,8 @@
     gain_s,
     stage_down,
     stage_gu,
+    rel_mlp,
+    rel_attn,
     out_lo,
     send_sem,
     recv_sem,
@@ -382,15 +386,13 @@
     dev_y = (row_y, col)
     dev_d = (row_d, col)
     dev_c = (row, sib)
-
-    def dev_z(step):
-        return (row, lax.rem(col + 2 * step, 8))
-
-    def col_from(step):
-        return lax.rem(col + 8 - 2 * step, 8)
-
-    def sib_from(step):
-        return lax.rem(sib + 8 - 2 * step, 8)
+    z_pair = {
+        0: z_at,
+        1: z_at + 1 - 2 * lax.rem(z_at, 2),
+        2: lax.rem(z_at + 2, 4),
+        3: 3 - z_at,
+    }
+    dev_z = {pair: (row, 2 * z_pair[pair] + core) for pair in (1, 2, 3)}
 
     counter = Counter()
     locals_used = Counter()
@@ -428,66 +430,74 @@
     partners = [dev_x, dev_y, dev_d] + [(row, lax.rem(col + step, 8)) for step in range(1, 8)]
     for device in partners:
         pl.semaphore_signal(barrier, inc=1, device_id=device, device_id_type=MESH_ID)
-    local_copies = []
-    for index, ref in enumerate((wq_hbm, wk_hbm, wv_hbm)):
-        local_copies.append(local(ref, wqkv.at[aligned(row * DR, DR), pl.ds(index * DC, DC)]))
-    local_copies.append(local(wo_hbm, wo.at[aligned(row * DR, DR), :]))
     half_mine = aligned(y_at * FH, FH)
     half_other = aligned((1 - y_at) * FH, FH)
-    local_copies.append(local(wg_hbm.at[:, half_mine], wgu.at[aligned(row * DR, DR), pl.ds(0, FH)]))
-    local_copies.append(local(wu_hbm.at[:, half_mine], wgu.at[aligned(row * DR, DR), pl.ds(FH, FH)]))
-    local_copies.append(local(wd_hbm.at[:, half_mine], wd.at[aligned(row * DR, DR), :]))
-    local_copies.append(local(x_hbm, x_full.at[:, aligned(col * DC, DC)]))
-    local_copies.append(local(cot_hbm, cot_s))
+    rows_mine = aligned(row * DR, DR)
+    local_copies = [local(x_hbm, x_full.at[:, aligned(col * DC, DC)]), local(cot_hbm, cot_z.at[z_at])]
+    for index, ref in enumerate((wq_hbm, wk_hbm, wv_hbm)):
+        local_copies.append(local(ref, wqkv.at[rows_mine, pl.ds(index * DC, DC)]))
+    local_copies.append(local(wo_hbm, wo.at[rows_mine, :]))
+    local_copies.append(local(wg_hbm.at[:, half_mine], wgu.at[rows_mine, pl.ds(0, FH)]))
+    local_copies.append(local(wu_hbm.at[:, half_mine], wgu.at[rows_mine, pl.ds(FH, FH)]))
+    local_copies.append(local(wd_hbm.at[:, half_mine], wd.at[rows_mine, :]))
     pl.semaphore_wait(barrier, len(partners))
 
-    def gather_block(buf, rows, at):
-        return buf.at[rows, aligned(at * DC, DC)]
-
     class Gather:
-        def __init__(self, buf, plane):
+        def __init__(self, buf, plane, raw, process):
             self.buf = buf
             self.plane = plane
+            self.raw = raw
+            self.process = process
             self.base_z = counter.take(3)
             self.base_c = counter.take(4)
+            self.rows = pl.ds(0, T)
             if plane:
                 self.base_y = counter.take(4)
                 self.base_cy = counter.take(4)
                 self.rows = aligned(y_at * T, T)
                 self.rows_other = aligned((1 - y_at) * T, T)
-            else:
-                self.rows = pl.ds(0, T)
-
-        def start(self, source=None):
-            own = gather_block(self.buf, self.rows, col)
-            src = own if source is None else source
-            for step in (1, 2, 3):
-                send(self.base_z + step - 1, src, own, dev_z(step))
-            if self.plane:
-                send(self.base_y, src, own, dev_y)
-            send(self.base_c, src, own, dev_c)
-
-        def finish(self):
-            for step in (1, 2, 3):
-                block = gather_block(self.buf, self.rows, col_from(step))
-                arrived(self.base_z + step - 1, block)
+
+        def block(self, rows, place, parity=None):
+            at = 2 * place + (core if parity is None else parity)
+            return rows, aligned(at * DC, DC)
+
+        def start(self):
+            self.raw_sends = []
+            for pair in (2, 3, 1):
+                own = self.raw.at[z_at]
+                self.raw_sends.append(send(self.base_z + pair - 1, own, own, dev_z[pair]))
+
+        def finish_own(self):
+            for pair in (0, 1, 2, 3):
+                place = z_pair[pair]
+                if pair:
+                    arrived(self.base_z + pair - 1, self.raw.at[place])
+                where = self.block(self.rows, place)
+                self.buf[where] = self.process(pair, place)
+                block = self.buf.at[where]
                 if self.plane:
-                    send(self.base_y + step, block, block, dev_y)
-                send(self.base_c + step, block, block, dev_c)
-            if self.plane:
-                for step in range(4):
-                    block = gather_block(self.buf, self.rows_other, col_from(step))
-                    arrived(self.base_y + step, block)
-                    send(self.base_cy + step, block, block, dev_c)
-            for step in range(4):
-                arrived(self.base_c + step, gather_block(self.buf, self.rows, sib_from(step)))
-                if self.plane:
-                    arrived(
-                        self.base_cy + step, gather_block(self.buf, self.rows_other, sib_from(step))
-                    )
+                    send(self.base_y + pair, block, block, dev_y)
+                send(self.base_c + pair, block, block, dev_c)
+            for pair in range(4):
+                arrived(
+                    self.base_c + pair, self.buf.at[self.block(self.rows, z_pair[pair], 1 - core)]
+                )
+
+        def finish_other(self):
+            for pair in range(4):
+                block = self.buf.at[self.block(self.rows_other, z_pair[pair])]
+                arrived(self.base_y + pair, block)
+                send(self.base_cy + pair, block, block, dev_c)
+            for pair in range(4):
+                arrived(
+                    self.base_cy + pair,
+                    self.buf.at[self.block(self.rows_other, z_pair[pair], 1 - core)],
+                )
+
+    stage_sends = []
 
     class Reduce:
-        ORDER = (1, 2, 3, 0)
+        ORDER = (2, 3, 1, 0)
 
         def __init__(self, partial, plane):
             self.partial = partial
@@ -495,21 +505,22 @@
             self.count = 2 * T if plane else T
             self.base_c = counter.take(4)
             self.base_z = counter.take(3)
+            self.rows = pl.ds(0, T)
             if plane:
                 self.base_y = counter.take(4)
                 self.rows = aligned(y_at * T, T)
                 self.rows_other = aligned((1 - y_at) * T, T)
-            else:
-                self.rows = pl.ds(0, T)
-            self.sent = []
 
         def start(self):
+            for copy in stage_sends:
+                sent(copy)
+            stage_sends.clear()
             count = self.count
-            for slot, step in enumerate(self.ORDER):
-                target = lax.rem(z_at + step, 4)
+            for slot, pair in enumerate(self.ORDER):
+                target = z_pair[pair]
                 start = pl.multiple_of((2 * target + 1 - core) * DC, DC)
                 stage_c[slot, :count, :] = self.partial(start).astype(BF)
-                self.sent.append(
+                stage_sends.append(
                     send(
                         self.base_c + slot,
                         stage_c.at[slot, pl.ds(0, count), :],
@@ -519,39 +530,39 @@
                 )
                 start = pl.multiple_of((2 * target + core) * DC, DC)
                 own_s[slot, :count, :] = self.partial(start)
-
-        def cores(self):
+                if slot:
+                    self.cores(slot - 1)
+            self.cores(3)
+
+        def cores(self, slot):
             count = self.count
-            for slot, step in enumerate(self.ORDER):
-                arrived(self.base_c + slot, land_c.at[slot, pl.ds(0, count), :])
-                if self.plane:
-                    rows = self.rows_other
-                    stage_y[slot] = (
-                        own_s[slot, rows, :] + land_c[slot, rows, :].astype(F32)
-                    ).astype(BF)
-                    self.sent.append(
-                        send(self.base_y + slot, stage_y.at[slot], land_y.at[slot], dev_y)
-                    )
-                    rows = self.rows
-                    own_s[slot, rows, :] = own_s[slot, rows, :] + land_c[slot, rows, :].astype(F32)
-                else:
-                    self.pass_on(slot, step, land_c.at[slot, pl.ds(0, T), :])
-
-        def pass_on(self, slot, step, landed):
+            arrived(self.base_c + slot, land_c.at[slot, pl.ds(0, count), :])
+            if self.plane:
+                rows = self.rows_other
+                stage_y[slot] = (own_s[slot, rows, :] + land_c[slot, rows, :].astype(F32)).astype(BF)
+                stage_sends.append(
+                    send(self.base_y + slot, stage_y.at[slot], land_y.at[slot], dev_y)
+                )
+                rows = self.rows
+                own_s[slot, rows, :] = own_s[slot, rows, :] + land_c[slot, rows, :].astype(F32)
+            else:
+                self.pass_on(slot, land_c.at[slot, pl.ds(0, T), :])
+
+        def pass_on(self, slot, landed):
+            pair = self.ORDER[slot]
             total = own_s[slot, self.rows, :] + landed[...].astype(F32)
-            if step == 0:
+            if pair == 0:
                 own_s[slot, self.rows, :] = total
             else:
                 stage_z[slot] = total.astype(BF)
-                self.sent.append(
-                    send(self.base_z + slot, stage_z.at[slot], land_z.at[slot], dev_z(step))
+                stage_sends.append(
+                    send(self.base_z + slot, stage_z.at[slot], land_z.at[slot], dev_z[pair])
                 )
 
         def planes(self):
-            if self.plane:
-                for slot, step in enumerate(self.ORDER):
-                    arrived(self.base_y + slot, land_y.at[slot])
-                    self.pass_on(slot, step, land_y.at[slot])
+            for slot in range(4):
+                arrived(self.base_y + slot, land_y.at[slot])
+                self.pass_on(slot, land_y.at[slot])
 
         def finish(self):
             for slot in range(3):
@@ -559,8 +570,6 @@
             total = own_s[3, self.rows, :]
             for slot in range(3):
                 total = total + land_z[slot].astype(F32)
-            for copy in self.sent:
-                sent(copy)
             return total
 
     pick = lax.broadcasted_iota(jnp.int32, (8, DC), 0)
@@ -568,22 +577,26 @@
     first_row = (pick == 0).astype(F32)
     second_row = (pick == 1).astype(F32)
     spread = ((pick == 0) & (lane < 128)).astype(F32) + ((pick == 1) & (lane >= 128)).astype(F32)
-
-    def sums_over_col(stage, first, second):
-        base = counter.take(7)
+    scal_base = counter.take(7 * LAYER_STAGES)
+
+    def scal_send(stage, first, second=None):
         mine = dot_nt(first_row, first, EXACT)
         if second is not None:
             mine = mine + dot_nt(second_row, second, EXACT)
         scal_s[stage, col] = mine
         for step in range(1, 8):
             send(
-                base + step - 1,
+                scal_base + 7 * stage + step - 1,
                 scal_s.at[stage, col],
                 scal_s.at[stage, col],
                 (row, lax.rem(col + step, 8)),
             )
+
+    def scal_get(stage):
         for step in range(1, 8):
-            arrived(base + step - 1, scal_s.at[stage, lax.rem(col + 8 - step, 8)])
+            arrived(
+                scal_base + 7 * stage + step - 1, scal_s.at[stage, lax.rem(col + 8 - step, 8)]
+            )
         total = scal_s[stage, 0]
         for index in range(1, 8):
             total = total + scal_s[stage, index]
@@ -593,8 +606,8 @@
     def wide(values):
         return jnp.concatenate([values, values], axis=1)
 
-    x_gather = Gather(x_full, False)
     attn_base = counter.take(16)
+    attn_hbm = (wq_hbm, wk_hbm, wv_hbm, wo_hbm)
 
     def attn_place(index, owner, part=None):
         if part is None:
@@ -605,8 +618,6 @@
             return wqkv.at[rows, pl.ds(index * DC, DC)]
         return wo.at[rows, :]
 
-    attn_hbm = (wq_hbm, wk_hbm, wv_hbm, wo_hbm)
-
     def attn_send(index):
         send(attn_base + index, attn_hbm[index], attn_place(index, row), dev_x)
         send(attn_base + 4 + index, attn_hbm[index], attn_place(index, row), dev_y)
@@ -647,12 +658,24 @@
 
     for index in range(3):
         attn_send(index)
-    x_gather.start(x_hbm)
-
+
+    x_base = counter.take(7)
+    cot_base = counter.take(3)
+
+    def x_block(place, parity):
+        return x_full.at[:, aligned((2 * place + parity) * DC, DC)]
+
+    for pair in (2, 3, 1):
+        send(x_base + pair - 1, x_hbm, x_block(z_at, core), dev_z[pair])
+    send(x_base + 3, x_hbm, x_block(z_at, core), dev_c)
+
+    position_rows = jnp.broadcast_to(pos_ref[...].astype(F32), (8, T))
+    position = dot_tn(position_rows, first_row[:, :HD], EXACT)
+    pos_s[...] = position.astype(jnp.int32)
     lane_at = lax.broadcasted_iota(jnp.int32, (1, HD), 1)
     within = lax.rem(lane_at, HD // 2).astype(F32)
     frequency = jnp.exp(within * (-2.0 * math.log(THETA) / HD))
-    angles = pos_ref[...].astype(F32) * frequency
+    angles = position * frequency
     cos_s[...] = jnp.cos(angles)
     sine = jnp.sin(angles)
     sin_s[...] = jnp.where(lane_at < HD // 2, -sine, sine)
@@ -660,29 +683,37 @@
     for index in range(3):
         attn_relay(index)
     attn_send(3)
+    for pair in (1, 2, 3):
+        block = x_block(z_pair[pair], core)
+        arrived(x_base + pair - 1, block)
+        send(x_base + 3 + pair, block, block, dev_c)
     for copy in local_copies:
         copy.wait()
-    x_gather.finish()
-    for index in range(3):
-        attn_ready(index)
-
-    gains = gains_ref[:, aligned(col * DC, DC)]
-    raw = []
-    for index in range(3):
-        raw.append(dot_nn(x_full[...], wqkv[:, pl.ds(index * DC, DC)]))
-    low_s[2] = raw[2].astype(BF)
-    hat_s[0] = raw[0]
-    hat_s[1] = raw[1]
+    for pair in (2, 3, 1):
+        send(cot_base + pair - 1, cot_z.at[z_at], cot_z.at[z_at], dev_z[pair])
+    for pair in range(4):
+        arrived(x_base + 3 + pair, x_block(z_pair[pair], 1 - core))
+    attn_ready(0)
+    attn_ready(1)
+
+    def gain_at(ref, at):
+        return ref[:, aligned(at * DC, DC)]
+
+    qk_gain = (gain_at(query_gain_ref, col), gain_at(key_gain_ref, col))
+    for index in range(2):
+        hat_s[index] = dot_nn(x_full[...], wqkv[:, pl.ds(index * DC, DC)])
+    scal_send(0, hat_s[0] * hat_s[0], hat_s[1] * hat_s[1])
     attn_relay(3)
     for index in range(3):
         mlp_send(index)
-    totals = sums_over_col(0, raw[0] * raw[0], raw[1] * raw[1])
-    scales = [lax.rsqrt(total / D + EPS) for total in totals]
+    attn_ready(2)
+    low_s[2] = dot_nn(x_full[...], wqkv[:, pl.ds(2 * DC, DC)]).astype(BF)
+    scales = [lax.rsqrt(total / D + EPS) for total in scal_get(0)]
     work_s[0] = jnp.concatenate(scales, axis=1)
     for index in range(2):
         hat = hat_s[index] * wide(scales[index])
         hat_s[index] = hat
-        normed = hat * gains[index : index + 1, :]
+        normed = hat * qk_gain[index]
         for head in range(2):
             part = normed[:, head * HD : (head + 1) * HD]
             turned = part * cos_s[...] + pltpu.roll(part, HD // 2, 1) * sin_s[...]
@@ -695,7 +726,7 @@
     def visible(at):
         query = at * chunk + lax.broadcasted_iota(jnp.int32, (chunk, T), 0)
         key = lax.broadcasted_iota(jnp.int32, (chunk, T), 1)
-        oldest = query - pos_ref[aligned(at * chunk, chunk), :]
+        oldest = query - pos_s[aligned(at * chunk, chunk), :1]
         return (key <= query) & (key >= oldest)
 
     def attend_chunk(at, carry):
@@ -716,117 +747,224 @@
     attn_ready(3)
     branch_sum = Reduce(lambda start: dot_nt(att_s[...], wo[pl.ds(start, DC), :]), False)
     branch_sum.start()
-    branch_sum.cores()
     mlp_relay(0)
     branch = branch_sum.finish()
+    scal_send(1, branch * branch)
     work_s[1] = branch
+    braw_s[z_at] = branch.astype(BF)
+
+    def middle_block(pair, place):
+        at = 2 * place + core
+        raw = work_s[1] if pair == 0 else braw_s[place].astype(F32)
+        hat = raw * wide(work_s[2, :, :128])
+        inputs = x_full[:, aligned(at * DC, DC)].astype(F32)
+        middle = inputs + hat * gain_at(attn_gain_ref, at)
+        if pair == 0:
+            bhat_s[...] = hat
+            middle_s[...] = middle
+        return middle.astype(BF)
+
+    mid_gather = Gather(mid_full, True, braw_s, middle_block)
+    mid_gather.start()
+    total, _ = scal_get(1)
+    work_s[2, :, :128] = lax.rsqrt(total / D + EPS)
     mlp_relay(1)
-    total, _ = sums_over_col(1, branch * branch, None)
-    branch_scale = lax.rsqrt(total / D + EPS)
-    work_s[2, :, :128] = branch_scale
-    branch_hat = work_s[1] * wide(branch_scale)
-    bhat_s[...] = branch_hat
-    middle = x_hbm_slice(x_full, col) + branch_hat * gains[2:3, :]
-    middle_s[...] = middle
-    mid_full[aligned(y_at * T, T), aligned(col * DC, DC)] = middle.astype(BF)
-    mid_gather = Gather(mid_full, True)
-    mid_gather.start()
     mlp_relay(2)
-    mid_gather.finish()
+    mid_gather.finish_own()
     mlp_ready(0)
     mlp_ready(1)
 
     tile = 256
 
-    def forward_tile(at, carry):
-        rows = aligned(lax.div(at, 2) * T, T)
-        lane_start = lax.rem(at, 2) * tile
-        lanes = aligned(lane_start, tile)
-        lanes_up = aligned(lane_start + FH, tile)
-        gate = dot_nn(mid_full[rows, :], wgu[:, lanes])
-        up = dot_nn(mid_full[rows, :], wgu[:, lanes_up])
-        gu_s[rows, lanes] = gate
-        gu_s[rows, lanes_up] = up
-        mixed_s[rows, lanes] = (gate * jax.nn.sigmoid(gate) * up).astype(BF)
-        return carry
-
-    lax.fori_loop(0, 4, forward_tile, 0)
+    def forward_tiles(rows):
+        def forward_tile(at, carry):
+            lanes = aligned(at * tile, tile)
+            lanes_up = aligned(at * tile + FH, tile)
+            gate = dot_nn(mid_full[rows, :], wgu[:, lanes])
+            up = dot_nn(mid_full[rows, :], wgu[:, lanes_up])
+            gu_s[rows, lanes] = gate.astype(BF)
+            gu_s[rows, lanes_up] = up.astype(BF)
+            mixed_s[rows, lanes] = (gate * jax.nn.sigmoid(gate) * up).astype(BF)
+            return carry
+
+        lax.fori_loop(0, FH // tile, forward_tile, 0)
+
+    forward_tiles(mid_gather.rows)
+    mid_gather.finish_other()
+    forward_tiles(mid_gather.rows_other)
     mlp_ready(2)
     ffn_sum = Reduce(lambda start: dot_nt(mixed_s[...], wd[pl.ds(start, DC), :]), True)
     ffn_sum.start()
-    ffn_sum.cores()
     ffn_sum.planes()
     ffn = ffn_sum.finish()
+    cot = cot_z[z_at].astype(F32)
+    mlp_gain = gain_at(mlp_gain_ref, col)
+    scal_send(2, ffn * ffn, cot * mlp_gain * ffn)
     work_s[1] = ffn
-    cot_gain = cot_s[...].astype(F32) * gains[3:4, :]
-    total, inner = sums_over_col(2, ffn * ffn, cot_gain * ffn)
+    raw_s[z_at] = ffn.astype(BF)
+
+    def grad_ffn_block(pair, place):
+        at = 2 * place + core
+        raw = work_s[1] if pair == 0 else raw_s[place].astype(F32)
+        scale = wide(work_s[2, :, 128:])
+        grad = cot_z[place].astype(F32) * gain_at(mlp_gain_ref, at)
+        return (scale * (grad - raw * scale * wide(own_s[0, pl.ds(0, T), :128]))).astype(BF)
+
+    gf_gather = Gather(gf_full, True, raw_s, grad_ffn_block)
+    gf_gather.start()
+    for pair in (1, 2, 3):
+        arrived(cot_base + pair - 1, cot_z.at[z_pair[pair]])
+    total, inner = scal_get(2)
     ffn_scale = lax.rsqrt(total / D + EPS)
+    work_s[2, :, 128:] = ffn_scale
+    own_s[0, pl.ds(0, T), :128] = inner * ffn_scale / D
     ffn_hat = work_s[1] * wide(ffn_scale)
-    cot = cot_s[...].astype(F32)
-    out_lo[...] = (middle_s[...] + ffn_hat * gains[3:4, :]).astype(BF)
+    out_lo[...] = (middle_s[...] + ffn_hat * mlp_gain).astype(BF)
     lo_copy = local(out_lo, layer_out)
     gain_s[row, 3:4, :] = jnp.sum(cot * ffn_hat, axis=0, keepdims=True)
-    inner = wide(inner * ffn_scale / D)
-    grad_ffn = wide(ffn_scale) * (cot * gains[3:4, :] - ffn_hat * inner)
-    gf_full[aligned(y_at * T, T), aligned(col * DC, DC)] = grad_ffn.astype(BF)
-    gf_gather = Gather(gf_full, True)
-    gf_gather.start()
-    gf_gather.finish()
-
-    def backward_tile(at, carry):
-        rows = aligned(lax.div(at, 2) * T, T)
-        lane_start = lax.rem(at, 2) * tile
-        lanes = aligned(lane_start, tile)
-        lanes_up = aligned(lane_start + FH, tile)
-        grad_mixed = dot_nn(gf_full[rows, :], wd[:, lanes])
-        gate = gu_s[rows, lanes]
-        up = gu_s[rows, lanes_up]
-        sigma = jax.nn.sigmoid(gate)
-        ggu_s[rows, lanes] = (grad_mixed * up * sigma * (1.0 + gate * (1.0 - sigma))).astype(BF)
-        ggu_s[rows, lanes_up] = (grad_mixed * gate * sigma).astype(BF)
-        return carry
-
-    lax.fori_loop(0, 4, backward_tile, 0)
-    mid_sum = Reduce(lambda start: dot_nt(ggu_s[...], wgu[pl.ds(start, DC), :]), True)
+    gf_gather.finish_own()
+
+    def backward_tiles(rows):
+        def backward_tile(at, carry):
+            lanes = aligned(at * tile, tile)
+            lanes_up = aligned(at * tile + FH, tile)
+            grad_mixed = dot_nn(gf_full[rows, :], wd[:, lanes])
+            gate = gu_s[rows, lanes].astype(F32)
+            up = gu_s[rows, lanes_up].astype(F32)
+            sigma = jax.nn.sigmoid(gate)
+            gu_s[rows, lanes] = (grad_mixed * up * sigma * (1.0 + gate * (1.0 - sigma))).astype(BF)
+            gu_s[rows, lanes_up] = (grad_mixed * gate * sigma).astype(BF)
+            return carry
+
+        lax.fori_loop(0, FH // tile, backward_tile, 0)
+
+    backward_tiles(gf_gather.rows)
+    gf_gather.finish_other()
+    backward_tiles(gf_gather.rows_other)
+
+    def lanes_of(owner):
+        return aligned(owner * DR, DR)
+
+    GU = pl.ds(0, 2 * FH)
+    DOWN = pl.ds(2 * FH, FH)
+
+    def down_piece(owner):
+        return dot_tn(gf_full[:, lanes_of(owner)], mixed_s[...])
+
+    def gu_piece(owner, part):
+        return dot_tn(mid_full[:, lanes_of(owner)], gu_s[:, pl.ds(part * FH, FH)])
+
+    def gu_stage(slot, owner):
+        for part in range(2):
+            stage_gu[slot, :, pl.ds(part * FH, FH)] = gu_piece(owner, part).astype(BF)
+
+    grad_base = counter.take(6)
+    stage_down[0] = down_piece(row_d).astype(BF)
+    down_sends = [send(grad_base, stage_down.at[0], rel_mlp.at[:, DOWN], dev_x)]
+    mid_sum = Reduce(lambda start: dot_nt(gu_s[...], wgu[pl.ds(start, DC), :]), True)
     mid_sum.start()
-    mid_sum.cores()
-
-    order = ((row_x, dev_x), (row_y, dev_y), (row_d, dev_d), (row, None))
-
-    def push(stage, slot, land, base, device):
-        if device is None:
-            return local(stage.at[slot], land.at[row])
-        return send(base + slot, stage.at[slot], land.at[row], device)
-
-    pushes = []
-    down_base = counter.take(3)
-    for slot, (owner, device) in enumerate(order):
-        lanes = aligned(owner * DR, DR)
-        stage_down[slot] = dot_tn(gf_full[:, lanes], mixed_s[...]).astype(BF)
-        pushes.append(push(stage_down, slot, land_down, down_base, device))
+    gu_stage(0, row_d)
+    gu_sends = [send(grad_base + 1, stage_gu.at[0], rel_mlp.at[:, GU], dev_x)]
+    stage_down[1] = down_piece(row_x).astype(BF)
+    down_sends.append(send(grad_base + 2, stage_down.at[1], land_mlp.at[1, :, DOWN], dev_x))
     mid_sum.planes()
-    gu_base = counter.take(3)
-    gu_pushes = []
-    for slot, (owner, device) in enumerate(order):
-        lanes = aligned(owner * DR, DR)
-        for part in range(2):
-            half = pl.ds(part * FH, FH)
-            stage_gu[slot, :, half] = dot_tn(mid_full[:, lanes], ggu_s[:, half]).astype(BF)
-        gu_pushes.append(push(stage_gu, slot, land_gu, gu_base, device))
-    grad_middle = cot_s[...].astype(F32) + mid_sum.finish()
+    arrived(grad_base, rel_mlp.at[:, DOWN])
+    stage_down[2] = (down_piece(row_y) + rel_mlp[:, DOWN].astype(F32)).astype(BF)
+    down_sends.append(send(grad_base + 4, stage_down.at[2], land_mlp.at[2, :, DOWN], dev_y))
+    gu_stage(1, row_x)
+    gu_sends.append(send(grad_base + 3, stage_gu.at[1], land_mlp.at[1, :, GU], dev_x))
+    grad_middle = cot_z[z_at].astype(F32) + mid_sum.finish()
+    attn_gain = gain_at(attn_gain_ref, col)
+    scal_send(3, grad_middle * attn_gain * bhat_s[...])
     middle_s[...] = grad_middle
-    gain_s[row, 2:3, :] = jnp.sum(grad_middle * bhat_s[...], axis=0, keepdims=True)
-    inner, _ = sums_over_col(3, grad_middle * gains[2:3, :] * bhat_s[...], None)
-    branch_scale = wide(work_s[2, :, :128])
-    grad_branch = branch_scale * (
-        middle_s[...] * gains[2:3, :] - bhat_s[...] * wide(inner / D)
-    )
-    gb_full[:, aligned(col * DC, DC)] = grad_branch.astype(BF)
-    gb_gather = Gather(gb_full, False)
+    for copy in gf_gather.raw_sends:
+        sent(copy)
+    raw_s[z_at] = grad_middle.astype(BF)
+
+    def grad_branch_block(pair, place):
+        at = 2 * place + core
+        scale = wide(work_s[2, :, :128])
+        raw = middle_s[...] if pair == 0 else raw_s[place].astype(F32)
+        hat = bhat_s[...] if pair == 0 else braw_s[place].astype(F32) * scale
+        inner = wide(own_s[0, pl.ds(0, T), :128])
+        return (scale * (raw * gain_at(attn_gain_ref, at) - hat * inner)).astype(BF)
+
+    gb_gather = Gather(gb_full, False, raw_s, grad_branch_block)
     gb_gather.start()
-    gb_gather.finish()
+    gain_s[row, 2:3, :] = jnp.sum(middle_s[...] * bhat_s[...], axis=0, keepdims=True)
+    inner, _ = scal_get(3)
+    own_s[0, pl.ds(0, T), :128] = inner / D
+    arrived(grad_base + 1, rel_mlp.at[:, GU])
+    for part in range(2):
+        half = pl.ds(part * FH, FH)
+        stage_gu[2, :, half] = (gu_piece(row_y, part) + rel_mlp[:, half].astype(F32)).astype(BF)
+    gu_sends.append(send(grad_base + 5, stage_gu.at[2], land_mlp.at[2, :, GU], dev_y))
+    gb_gather.finish_own()
 
     ga_s[...] = dot_nn(gb_full[...], wo[...]).astype(BF)
+
+    upper = pl.ds(0, DR // 2)
+    lower = pl.ds(DR // 2, DR // 2)
+    attn_grad_base = counter.take(3 * 6)
+    late = []
+
+    class AttnGrad:
+        def __init__(self, order, left, right, stage, stage_lanes, lanes):
+            self.base = attn_grad_base + 6 * order
+            self.left, self.right = left, right
+            self.stage, self.stage_lanes, self.lanes = stage, stage_lanes, lanes
+
+        def at(self, slot, rows):
+            return self.stage.at[slot, rows, self.stage_lanes]
+
+        def start(self):
+            for slot, owner in enumerate((row_d, row_x, row_y, row)):
+                self.stage[slot, :, self.stage_lanes] = dot_tn(
+                    self.left[:, lanes_of(owner)], self.right()
+                ).astype(BF)
+                if slot == 0:
+                    send(self.base, self.at(0, upper), rel_attn.at[upper, self.lanes], dev_x)
+                    send(self.base + 1, self.at(0, lower), rel_attn.at[lower, self.lanes], dev_y)
+                elif slot == 1:
+                    landing = land_attn.at[1, upper, self.lanes]
+                    send(self.base + 2, self.at(1, upper), landing, dev_x)
+                elif slot == 2:
+                    landing = land_attn.at[2, lower, self.lanes]
+                    send(self.base + 3, self.at(2, lower), landing, dev_y)
+                else:
+                    whole = self.at(3, pl.ds(0, DR))
+                    late.append(local(whole, land_attn.at[0, :, self.lanes]))
+
+        def relay(self):
+            for step, (slot, rows, device) in enumerate(((2, upper, dev_y), (1, lower, dev_x))):
+                arrived(self.base + step, rel_attn.at[rows, self.lanes])
+                self.stage[slot, rows, self.stage_lanes] = (
+                    self.stage[slot, rows, self.stage_lanes].astype(F32)
+                    + rel_attn[rows, self.lanes].astype(F32)
+                ).astype(BF)
+                send(
+                    self.base + 4 + step,
+                    self.at(slot, rows),
+                    land_attn.at[slot, rows, self.lanes],
+                    device,
+                )
+
+        def finish(self):
+            arrived(self.base + 2, land_attn.at[1, upper, self.lanes])
+            arrived(self.base + 3, land_attn.at[2, lower, self.lanes])
+            arrived(self.base + 4, land_attn.at[2, upper, self.lanes])
+            arrived(self.base + 5, land_attn.at[1, lower, self.lanes])
+
+    stage_down[3] = down_piece(row).astype(BF)
+    own_copies = [local(stage_down.at[3], land_mlp.at[0, :, DOWN])]
+    for copy in down_sends:
+        sent(copy)
+    own_copies[0].wait()
+    first_lanes = pl.ds(0, DC)
+    o_grad = AttnGrad(
+        0, gb_full, lambda: att_s[...], stage_down, first_lanes, pl.ds(3 * DC, DC)
+    )
+    o_grad.start()
 
     def attend_back_chunk(at, carry):
         rows = aligned(at * chunk, chunk)
@@ -834,11 +972,9 @@
             lanes = pl.ds(head * HD, HD)
             grad_probs = dot_nt(ga_s[rows, lanes], low_s[2, :, lanes])
             probs = probs_s[head, rows, :]
-            weighted = probs * grad_probs
-            inner = jnp.sum(weighted, axis=1, keepdims=True)
+            inner = jnp.sum(probs * grad_probs, axis=1, keepdims=True)
             grad_scores = (probs * (grad_probs - inner)).astype(BF)
             gs_s[head, rows, :] = grad_scores
-            pl_s[head, rows, :] = probs.astype(BF)
             gqk_s[0, rows, lanes] = dot_nn(grad_scores, low_s[1, :, lanes])
         return carry
 
@@ -846,7 +982,6 @@
     for head in range(2):
         lanes = pl.ds(head * HD, HD)
         gqk_s[1, :, lanes] = dot_tn(gs_s[head], low_s[0, :, lanes])
-        gqkv_s[:, pl.ds(2 * DC + head * HD, HD)] = dot_tn(pl_s[head], ga_s[:, lanes]).astype(BF)
     inners = []
     for index in range(2):
         for head in range(2):
@@ -858,66 +993,80 @@
             gqk_s[index, :, lanes] = turned
         weighted = gqk_s[index] * hat_s[index]
         gain_s[row, index : index + 1, :] = jnp.sum(weighted, axis=0, keepdims=True)
-        inners.append(weighted * gains[index : index + 1, :])
+        inners.append(weighted * qk_gain[index])
+    scal_send(4, inners[0], inners[1])
     gain_base = counter.take(3)
-    for slot, (_, device) in enumerate(order[:3]):
+    for slot, device in enumerate((dev_x, dev_y, dev_d)):
         send(gain_base + slot, gain_s.at[row], gain_s.at[row], device)
-    totals = sums_over_col(4, inners[0], inners[1])
+    for head in range(2):
+        lanes = pl.ds(head * HD, HD)
+        gqkv_s[:, pl.ds(2 * DC + head * HD, HD)] = dot_tn(
+            probs_s[head].astype(BF), ga_s[:, lanes]
+        ).astype(BF)
+    v_grad = AttnGrad(
+        1,
+        x_full,
+        lambda: gqkv_s[:, 2 * DC :],
+        stage_down,
+        pl.ds(DC, DC),
+        pl.ds(2 * DC, DC),
+    )
+    v_grad.start()
+    totals = scal_get(4)
     for index in range(2):
         scale = wide(work_s[0, :, index * 128 : (index + 1) * 128])
         gqkv_s[:, pl.ds(index * DC, DC)] = (
-            scale
-            * (
-                gqk_s[index] * gains[index : index + 1, :]
-                - hat_s[index] * wide(totals[index] / D)
-            )
+            scale * (gqk_s[index] * qk_gain[index] - hat_s[index] * wide(totals[index] / D))
         ).astype(BF)
-
-    for group in (pushes, gu_pushes):
-        for copy in group[:3]:
-            sent(copy)
-        group[3].wait()
     in_sum = Reduce(lambda start: dot_nt(gqkv_s[...], wqkv[pl.ds(start, DC), :]), False)
     in_sum.start()
-    in_sum.cores()
-    o_base = counter.take(3)
-    qkv_base = counter.take(3)
-    late = []
-    for slot, (owner, device) in enumerate(order):
-        lanes = aligned(owner * DR, DR)
-        stage_gu[slot, :, pl.ds(0, 3 * DC)] = dot_tn(x_full[:, lanes], gqkv_s[...]).astype(BF)
-        source = stage_gu.at[slot, :, pl.ds(0, 3 * DC)]
-        if device is None:
-            late.append(local(source, land_qkv.at[row]))
-        else:
-            send(qkv_base + slot, source, land_qkv.at[row], device)
-        stage_down[slot, :, pl.ds(0, DC)] = dot_tn(gb_full[:, lanes], att_s[...]).astype(BF)
-        source = stage_down.at[slot, :, pl.ds(0, DC)]
-        if device is None:
-            late.append(local(source, land_o.at[row]))
-        else:
-            send(o_base + slot, source, land_o.at[row], device)
+    o_grad.relay()
+    gu_stage(3, row)
+    own_copies.append(local(stage_gu.at[3], land_mlp.at[0, :, GU]))
+    for copy in gu_sends:
+        sent(copy)
+    own_copies[1].wait()
+    both_lanes = pl.ds(0, 2 * DC)
+    qk_grad = AttnGrad(
+        2, x_full, lambda: gqkv_s[:, : 2 * DC], stage_gu, both_lanes, both_lanes
+    )
+    qk_grad.start()
+    v_grad.relay()
     work_s[1] = middle_s[...] + in_sum.finish()
     late.append(local(work_s.at[1], grad_in))
     late.append(lo_copy)
-
-    sources = (row_x, row_y, row_d)
-    for slot, owner in enumerate(sources):
+    qk_grad.relay()
+
+    for slot, owner in enumerate((row_x, row_y, row_d)):
         arrived(gain_base + slot, gain_s.at[owner])
     gains_out[...] = gain_s[0] + gain_s[1] + gain_s[2] + gain_s[3]
-    for slot, owner in enumerate(sources):
-        arrived(down_base + slot, land_down.at[owner])
-        arrived(gu_base + slot, land_gu.at[owner])
-        arrived(o_base + slot, land_o.at[owner])
-        arrived(qkv_base + slot, land_qkv.at[owner])
+    for index, (slot, lanes) in enumerate(((1, DOWN), (1, GU), (2, DOWN), (2, GU))):
+        arrived(grad_base + 2 + index, land_mlp.at[slot, :, lanes])
+    for grad in (o_grad, v_grad, qk_grad):
+        grad.finish()
     for copy in late:
         copy.wait()
     for copy in pending:
         copy.wait_send()
 
 
-def x_hbm_slice(x_full, col):
-    return x_full[:, aligned(col * DC, DC)].astype(F32)
+def total_kernel(
+    lo_ref, gin_ref, gains_ref, mlp_ref, attn_ref, lo_out, gin_out, *outs
+):
+    y_at = lax.div(lax.axis_index("row"), 2)
+    lo_out[...] = lo_ref[...]
+    gin_out[...] = gin_ref[...]
+    attn = attn_ref[0].astype(F32) + attn_ref[1].astype(F32) + attn_ref[2].astype(F32)
+    for index in range(4):
+        outs[index][...] = attn[:, index * DC : (index + 1) * DC]
+    mine = mlp_ref[0].astype(F32) + mlp_ref[1].astype(F32)
+    other = mlp_ref[2].astype(F32)
+    for index in range(3):
+        lanes = slice(index * FH, (index + 1) * FH)
+        outs[4 + index][:, aligned(y_at * FH, FH)] = mine[:, lanes]
+        outs[4 + index][:, aligned((1 - y_at) * FH, FH)] = other[:, lanes]
+    for index in range(4):
+        outs[7 + index][...] = gains_ref[index : index + 1, :]
 
 
 MIB = 1 << 20
@@ -940,25 +1089,21 @@
     segments,
     cotangent,
 ):
-    gains = jnp.stack([query_gain, key_gain, attn_gain, mlp_gain])
-    gains = jnp.concatenate([gains, jnp.zeros_like(gains)], axis=0)
     hbm = pl.BlockSpec(memory_space=pl.ANY)
     vmem = pl.BlockSpec(memory_space=pltpu.VMEM)
     sds = jax.ShapeDtypeStruct
-    copies = 230
-    results = pl.pallas_call(
+    copies = 240
+    landed = pl.pallas_call(
         block_kernel,
         out_shape=[
             sds((T, DC), BF),
             sds((T, DC), F32),
             sds((8, DC), F32),
-            sds((4, DR, FH), BF),
-            sds((4, DR, 2 * FH), BF),
-            sds((4, DR, DC), BF),
-            sds((4, DR, 3 * DC), BF),
+            sds((3, DR, 3 * FH), BF),
+            sds((3, DR, 4 * DC), BF),
         ],
-        in_specs=[hbm] * 9 + [vmem, vmem],
-        out_specs=[hbm, hbm, vmem, hbm, hbm, hbm, hbm],
+        in_specs=[hbm] * 9 + [vmem] * 5,
+        out_specs=[hbm, hbm, vmem, hbm, hbm],
         scratch_shapes=[
             pltpu.VMEM((D, 3 * DC), BF),
             pltpu.VMEM((D, DC), BF),
@@ -968,22 +1113,23 @@
             pltpu.VMEM((2 * T, D), BF),
             pltpu.VMEM((2 * T, D), BF),
             pltpu.VMEM((T, D), BF),
-            pltpu.VMEM((2 * T, 2 * FH), F32),
+            pltpu.VMEM((2 * T, 2 * FH), BF),
             pltpu.VMEM((2 * T, FH), BF),
-            pltpu.VMEM((2 * T, 2 * FH), BF),
             pltpu.VMEM((2, T, T), F32),
             pltpu.VMEM((2, T, DC), F32),
             pltpu.VMEM((3, T, DC), BF),
             pltpu.VMEM((T, HD), F32),
             pltpu.VMEM((T, HD), F32),
-            pltpu.VMEM((T, DC), BF),
+            pltpu.VMEM((T, HD), jnp.int32),
+            pltpu.VMEM((4, T, DC), BF),
+            pltpu.VMEM((4, T, DC), BF),
+            pltpu.VMEM((4, T, DC), BF),
             pltpu.VMEM((T, DC), F32),
             pltpu.VMEM((T, DC), F32),
             pltpu.VMEM((3, T, DC), F32),
             pltpu.VMEM((T, DC), BF),
             pltpu.VMEM((T, DC), BF),
             pltpu.VMEM((T, 3 * DC), BF),
-            pltpu.VMEM((2, T, T), BF),
             pltpu.VMEM((2, T, T), BF),
             pltpu.VMEM((2, T, DC), F32),
             pltpu.VMEM((4, 2 * T, DC), F32),
@@ -997,6 +1143,8 @@
             pltpu.VMEM((4, 8, DC), F32),
             pltpu.VMEM((4, DR, FH), BF),
             pltpu.VMEM((4, DR, 2 * FH), BF),
+            pltpu.VMEM((DR, 3 * FH), BF),
+            pltpu.VMEM((DR, 4 * DC), BF),
             pltpu.VMEM((T, DC), BF),
             pltpu.SemaphoreType.DMA((copies,)),
             pltpu.SemaphoreType.DMA((copies,)),
@@ -1018,34 +1166,35 @@
         up_weight,
         down_weight,
         cotangent,
-        gains,
-        positions[:, None],
-    )
-    layer_out, grad_in, gains_out, land_down, land_gu, land_o, land_qkv = results
-
-    def halves(landed):
-        landed = landed.astype(F32)
-        return jnp.concatenate([landed[0] + landed[1], landed[2] + landed[3]], axis=1)
-
-    def total(landed):
-        landed = landed.astype(F32)
-        return landed[0] + landed[1] + landed[2] + landed[3]
-
-    return (
-        layer_out,
-        grad_in,
-        total(land_qkv[:, :, :DC]),
-        total(land_qkv[:, :, DC : 2 * DC]),
-        total(land_qkv[:, :, 2 * DC :]),
-        total(land_o),
-        halves(land_gu[:, :, :FH]),
-        halves(land_gu[:, :, FH:]),
-        halves(land_down),
-        gains_out[0],
-        gains_out[1],
-        gains_out[2],
-        gains_out[3],
-    )
+        query_gain[None, :],
+        key_gain[None, :],
+        attn_gain[None, :],
+        mlp_gain[None, :],
+        positions[None, :],
+    )
+    step = 64
+
+    def rows_of(width):
+        return pl.BlockSpec((step, width), lambda at: (at, 0))
+
+    gain_spec = pl.BlockSpec((1, DC), lambda at: (0, 0))
+    results = pl.pallas_call(
+        total_kernel,
+        grid=(DR // step,),
+        out_shape=[sds((T, DC), BF), sds((T, DC), F32)]
+        + [sds((DR, DC), F32)] * 4
+        + [sds((DR, 2 * FH), F32)] * 3
+        + [sds((1, DC), F32)] * 4,
+        in_specs=[
+            rows_of(DC),
+            rows_of(DC),
+            pl.BlockSpec((8, DC), lambda at: (0, 0)),
+            pl.BlockSpec((3, step, 3 * FH), lambda at: (0, at, 0)),
+            pl.BlockSpec((3, step, 4 * DC), lambda at: (0, at, 0)),
+        ],
+        out_specs=[rows_of(DC)] * 6 + [rows_of(2 * FH)] * 3 + [gain_spec] * 4,
+    )(*landed)
+    return (*results[:9], *[gain[0] for gain in results[9:]])
 
 
 def solution(mesh):

time: 384 us -> 351 us (0.914)
  other arithmetic: 12.2 us -> 0 us
  Pallas kernels: 355 us -> 346 us
  local copies, waits for them, and re-layouts: 8.47 us -> 0 us
    pallas_call x1, Pallas kernels: 355 us -> 337 us  [on_device_kernel(): pl.pallas_call(block_kernel, out_shape=[sds((T, DC), BF), sds((T, DC), F3...]
    pallas_call x0 -> x1, Pallas kernels: none -> 9.13 us  [on_device_kernel(): pl.pallas_call(total_kernel, grid=(DR // step,), out_shape=[sds((T, DC),...]
    concatenate x3 -> x0, other arithmetic: 4.37 us -> none  [halves(): jnp.concatenate([landed[0] + landed[1], landed[2] + landed[3]], axis=1)]
    unnamed x12 -> x0, local copies, waits for them, and re-layouts: 4.02 us -> none
    add x4 -> x0, other arithmetic: 3.96 us -> none  [the longest x2 2.46 us: total(): return landed[0] + landed[1] + landed[2] + landed[3]]
    convert_element_type x4 -> x0, other arithmetic: 3.87 us -> none  [the longest x2 2 us: total(): landed = landed.astype(F32)]
where the time goes in v2:
time: 351 us; the launch traced here: 347 us
  Pallas kernels  346 us (99%)
    pallas_call x1, Pallas kernels, on_device_kernel(): pl.pallas_call(block_kernel, out_shape=[sds((T, DC), BF), sds((T, DC), F3...  337 us
    pallas_call x1, Pallas kernels, on_device_kernel(): pl.pallas_call(total_kernel, grid=(DR // step,), out_shape=[sds((T, DC),...  9.13 us

profile of v2, /device:TPU:0, one launch (start us, length us, event | category | flops | bytes accessed | tf_op | source)
XLA Modules:
  0.0 346.9 jit_solution(8008227600301404040)
XLA Ops:
  0.7 336.9 %shard_map.237 = (bf16[512,256]{1,0:T(8,128)(2,1)}, f32[512,256]{1,0:T(8,128)}, f32[8,256]{1,0:T(8,128)}, bf16[3,512,1536]{2,1,0:T(8,128)(2,1)}, bf16[3,512,1024]{2,1,0:T(8,128)(2,1)}) custom-call(bf16[512,256]{1,0:T(8,128)(2,1)} %x_hbm.1, bf16[512,256]{1,0:T(8,128)(2,1)} %wq_hbm.1, bf16[512,256]{1,0:T(8,128)(2,1)} %wk_hbm.1, bf16[512,256]{1,0:T(8,128)(2,1)} %wv_hbm.1, ...), custom_call_target="tpu_custom_call" | custom-call | flops 26800001024 | bytes 16000000 | tf_op jit(solution)/shard_map/pallas_call | solution.py:1096
  337.6 9.1 %shard_map.238 = (bf16[512,256]{1,0:T(8,128)(2,1)}, f32[512,256]{1,0:T(8,128)}, f32[512,256]{1,0:T(8,128)}, f32[512,256]{1,0:T(8,128)}, f32[512,256]{1,0:T(8,128...) custom-call(bf16[512,256]{1,0:T(8,128)(2,1)} %get-tuple-element.31.l, ...), custom_call_target="tpu_custom_call" | custom-call | tf_op jit(solution)/shard_map/pallas_call | solution.py:1181

commit v3 on v2

--- a/solution.py
+++ b/solution.py
@@ -273,6 +273,7 @@
 DR = 512
 D = 2048
 FH = 512
+HT = 256
 LAYER_STAGES = 5
 EXACT = lax.Precision.HIGHEST
 
@@ -349,6 +350,7 @@
     middle_s,
     bhat_s,
     work_s,
+    inner_s,
     att_s,
     ga_s,
     gqkv_s,
@@ -361,6 +363,7 @@
     land_y,
     stage_z,
     land_z,
+    land_r,
     scal_s,
     gain_s,
     stage_down,
@@ -392,34 +395,47 @@
         2: lax.rem(z_at + 2, 4),
         3: 3 - z_at,
     }
+    middle = (z_at == 1) | (z_at == 2)
+    at_end = (z_at == 0) | (z_at == 3)
     dev_z = {pair: (row, 2 * z_pair[pair] + core) for pair in (1, 2, 3)}
 
     counter = Counter()
     locals_used = Counter()
     pending = []
 
-    def copy_of(index, src, dst, device):
+    def copy_of(index, src, dst, device, send_index=None):
         return pltpu.make_async_remote_copy(
             src_ref=src,
             dst_ref=dst,
-            send_sem=send_sem.at[index],
+            send_sem=send_sem.at[index if send_index is None else send_index],
             recv_sem=recv_sem.at[index],
             device_id=device,
             device_id_type=MESH_ID,
         )
 
-    def send(index, src, dst, device):
-        copy = copy_of(index, src, dst, device)
-        copy.start()
-        pending.append(copy)
-        return copy
-
-    def arrived(index, dst):
-        copy_of(index, dst, dst, dev_c).wait_recv()
-
-    def sent(copy):
-        copy.wait_send()
-        pending[:] = [other for other in pending if other is not copy]
+    def send(index, src, dst, device, send_index=None, when=None):
+        copy = copy_of(index, src, dst, device, send_index)
+        if when is None:
+            copy.start()
+        else:
+            pl.when(when)(copy.start)
+        pending.append((copy, when))
+        return copy, when
+
+    def arrived(index, dst, when=None):
+        copy = copy_of(index, dst, dst, dev_c)
+        if when is None:
+            copy.wait_recv()
+        else:
+            pl.when(when)(copy.wait_recv)
+
+    def sent(started):
+        copy, when = started
+        if when is None:
+            copy.wait_send()
+        else:
+            pl.when(when)(copy.wait_send)
+        pending[:] = [other for other in pending if other[0] is not copy]
 
     def local(src, dst):
         copy = pltpu.make_async_copy(src, dst, local_sem.at[locals_used.take()])
@@ -430,6 +446,12 @@
     partners = [dev_x, dev_y, dev_d] + [(row, lax.rem(col + step, 8)) for step in range(1, 8)]
     for device in partners:
         pl.semaphore_signal(barrier, inc=1, device_id=device, device_id_type=MESH_ID)
+
+    @pl.when(at_end)
+    def _():
+        land_r[...] = jnp.zeros_like(land_r)
+        land_z[0] = jnp.zeros_like(land_z[0])
+
     half_mine = aligned(y_at * FH, FH)
     half_other = aligned((1 - y_at) * FH, FH)
     rows_mine = aligned(row * DR, DR)
@@ -442,20 +464,36 @@
     local_copies.append(local(wd_hbm.at[:, half_mine], wd.at[rows_mine, :]))
     pl.semaphore_wait(barrier, len(partners))
 
+    def own_rows(half, plane):
+        if plane:
+            return aligned(half * 2 * HT + y_at * HT, HT)
+        return pl.ds(half * HT, HT)
+
+    def other_rows(half):
+        return aligned(half * 2 * HT + (1 - y_at) * HT, HT)
+
+    def half_rows(half, plane):
+        count = 2 * HT if plane else HT
+        return pl.ds(half * count, count)
+
+    def tokens(half):
+        return pl.ds(half * HT, HT)
+
     class Gather:
-        def __init__(self, buf, plane, raw, process):
+        def __init__(self, buf, plane, raw, process, half):
             self.buf = buf
             self.plane = plane
             self.raw = raw
             self.process = process
+            self.half = half
             self.base_z = counter.take(3)
+            self.relay = counter.take()
             self.base_c = counter.take(4)
-            self.rows = pl.ds(0, T)
+            self.rows = own_rows(half, plane)
             if plane:
                 self.base_y = counter.take(4)
                 self.base_cy = counter.take(4)
-                self.rows = aligned(y_at * T, T)
-                self.rows_other = aligned((1 - y_at) * T, T)
+                self.rows_other = other_rows(half)
 
         def block(self, rows, place, parity=None):
             at = 2 * place + (core if parity is None else parity)
@@ -463,17 +501,25 @@
 
         def start(self):
             self.raw_sends = []
+            own = self.raw.at[z_at, tokens(self.half)]
             for pair in (2, 3, 1):
-                own = self.raw.at[z_at]
-                self.raw_sends.append(send(self.base_z + pair - 1, own, own, dev_z[pair]))
+                when = middle if pair == 3 else None
+                self.raw_sends.append(
+                    send(self.base_z + pair - 1, own, own, dev_z[pair], when=when)
+                )
 
         def finish_own(self):
-            for pair in (0, 1, 2, 3):
+            for pair in (0, 2, 1, 3):
                 place = z_pair[pair]
                 if pair:
-                    arrived(self.base_z + pair - 1, self.raw.at[place])
+                    raw = self.raw.at[place, tokens(self.half)]
+                    arrived(self.base_z + pair - 1, raw)
+                if pair == 2:
+                    self.raw_sends.append(
+                        send(self.base_z + 2, raw, raw, dev_z[1], self.relay, middle)
+                    )
                 where = self.block(self.rows, place)
-                self.buf[where] = self.process(pair, place)
+                self.buf[where] = self.process(pair, place, self.half)
                 block = self.buf.at[where]
                 if self.plane:
                     send(self.base_y + pair, block, block, dev_y)
@@ -482,6 +528,10 @@
                 arrived(
                     self.base_c + pair, self.buf.at[self.block(self.rows, z_pair[pair], 1 - core)]
                 )
+
+        def finish_raw(self):
+            for copy in self.raw_sends:
+                sent(copy)
 
         def finish_other(self):
             for pair in range(4):
@@ -494,82 +544,96 @@
                     self.buf.at[self.block(self.rows_other, z_pair[pair], 1 - core)],
                 )
 
-    stage_sends = []
+    stage_sends = ([], [])
 
     class Reduce:
-        ORDER = (2, 3, 1, 0)
-
-        def __init__(self, partial, plane):
+        ORDER = (3, 1, 2, 0)
+
+        def __init__(self, partial, plane, half):
             self.partial = partial
             self.plane = plane
-            self.count = 2 * T if plane else T
+            self.half = half
             self.base_c = counter.take(4)
             self.base_z = counter.take(3)
-            self.rows = pl.ds(0, T)
+            self.relay = counter.take()
+            self.left = half_rows(half, plane)
+            self.all_rows = pl.ds(half * 2 * HT, 2 * HT if plane else HT)
+            self.rows = own_rows(half, True) if plane else self.all_rows
+            self.tokens = tokens(half)
             if plane:
                 self.base_y = counter.take(4)
-                self.rows = aligned(y_at * T, T)
-                self.rows_other = aligned((1 - y_at) * T, T)
+                self.rows_other = other_rows(half)
 
         def start(self):
-            for copy in stage_sends:
+            for copy in stage_sends[self.half]:
                 sent(copy)
-            stage_sends.clear()
-            count = self.count
+            stage_sends[self.half].clear()
+            rows = self.all_rows
             for slot, pair in enumerate(self.ORDER):
                 target = z_pair[pair]
                 start = pl.multiple_of((2 * target + 1 - core) * DC, DC)
-                stage_c[slot, :count, :] = self.partial(start).astype(BF)
-                stage_sends.append(
-                    send(
-                        self.base_c + slot,
-                        stage_c.at[slot, pl.ds(0, count), :],
-                        land_c.at[slot, pl.ds(0, count), :],
-                        dev_c,
-                    )
+                stage_c[slot, rows, :] = self.partial(self.left, start).astype(BF)
+                self.send(
+                    self.base_c + slot, stage_c.at[slot, rows, :], land_c.at[slot, rows, :], dev_c
                 )
                 start = pl.multiple_of((2 * target + core) * DC, DC)
-                own_s[slot, :count, :] = self.partial(start)
+                own_s[slot, rows, :] = self.partial(self.left, start)
                 if slot:
                     self.cores(slot - 1)
             self.cores(3)
 
+        def send(self, *copy):
+            stage_sends[self.half].append(send(*copy))
+
         def cores(self, slot):
-            count = self.count
-            arrived(self.base_c + slot, land_c.at[slot, pl.ds(0, count), :])
+            arrived(self.base_c + slot, land_c.at[slot, self.all_rows, :])
             if self.plane:
                 rows = self.rows_other
-                stage_y[slot] = (own_s[slot, rows, :] + land_c[slot, rows, :].astype(F32)).astype(BF)
-                stage_sends.append(
-                    send(self.base_y + slot, stage_y.at[slot], land_y.at[slot], dev_y)
+                stage_y[slot, self.tokens, :] = (
+                    own_s[slot, rows, :] + land_c[slot, rows, :].astype(F32)
+                ).astype(BF)
+                self.send(
+                    self.base_y + slot,
+                    stage_y.at[slot, self.tokens],
+                    land_y.at[slot, self.tokens],
+                    dev_y,
                 )
                 rows = self.rows
                 own_s[slot, rows, :] = own_s[slot, rows, :] + land_c[slot, rows, :].astype(F32)
             else:
-                self.pass_on(slot, land_c.at[slot, pl.ds(0, T), :])
+                self.pass_on(slot, land_c.at[slot, self.rows, :])
 
         def pass_on(self, slot, landed):
             pair = self.ORDER[slot]
             total = own_s[slot, self.rows, :] + landed[...].astype(F32)
             if pair == 0:
                 own_s[slot, self.rows, :] = total
+                return
+            if pair == 2:
+                arrived(self.relay, land_r.at[self.tokens], middle)
+                total = total + land_r[self.tokens, :].astype(F32)
+            stage_z[slot, self.tokens, :] = total.astype(BF)
+            stage, land = stage_z.at[slot, self.tokens], land_z.at[slot, self.tokens]
+            if pair == 3:
+                index = self.base_z + slot
+                self.send(index, stage, land, dev_z[3], None, middle)
+                self.send(self.relay, stage, land_r.at[self.tokens], dev_z[1], None, at_end)
             else:
-                stage_z[slot] = total.astype(BF)
-                stage_sends.append(
-                    send(self.base_z + slot, stage_z.at[slot], land_z.at[slot], dev_z[pair])
-                )
+                self.send(self.base_z + slot, stage, land, dev_z[pair])
 
         def planes(self):
             for slot in range(4):
-                arrived(self.base_y + slot, land_y.at[slot])
-                self.pass_on(slot, land_y.at[slot])
+                landed = land_y.at[slot, self.tokens]
+                arrived(self.base_y + slot, landed)
+                self.pass_on(slot, landed)
 
         def finish(self):
             for slot in range(3):
-                arrived(self.base_z + slot, land_z.at[slot])
+                when = middle if self.ORDER[slot] == 3 else None
+                arrived(self.base_z + slot, land_z.at[slot, self.tokens], when)
             total = own_s[3, self.rows, :]
             for slot in range(3):
-                total = total + land_z[slot].astype(F32)
+                total = total + land_z[slot, self.tokens, :].astype(F32)
             return total
 
     pick = lax.broadcasted_iota(jnp.int32, (8, DC), 0)
@@ -577,31 +641,29 @@
     first_row = (pick == 0).astype(F32)
     second_row = (pick == 1).astype(F32)
     spread = ((pick == 0) & (lane < 128)).astype(F32) + ((pick == 1) & (lane >= 128)).astype(F32)
-    scal_base = counter.take(7 * LAYER_STAGES)
-
-    def scal_send(stage, first, second=None):
+    scal_base = counter.take(7 * 2 * LAYER_STAGES)
+
+    def scal_send(stage, half, first, second=None):
         mine = dot_nt(first_row, first, EXACT)
         if second is not None:
             mine = mine + dot_nt(second_row, second, EXACT)
-        scal_s[stage, col] = mine
+        place = scal_s.at[stage, half, col]
+        place[...] = mine
         for step in range(1, 8):
-            send(
-                scal_base + 7 * stage + step - 1,
-                scal_s.at[stage, col],
-                scal_s.at[stage, col],
-                (row, lax.rem(col + step, 8)),
-            )
-
-    def scal_get(stage):
+            index = scal_base + 7 * (2 * stage + half) + step - 1
+            send(index, place, place, (row, lax.rem(col + step, 8)))
+
+    def scal_get(stage, half):
         for step in range(1, 8):
-            arrived(
-                scal_base + 7 * stage + step - 1, scal_s.at[stage, lax.rem(col + 8 - step, 8)]
-            )
-        total = scal_s[stage, 0]
+            index = scal_base + 7 * (2 * stage + half) + step - 1
+            arrived(index, scal_s.at[stage, half, lax.rem(col + 8 - step, 8)])
+        total = scal_s[stage, half, 0]
         for index in range(1, 8):
-            total = total + scal_s[stage, index]
+            total = total + scal_s[stage, half, index]
         both = dot_tn(total, spread, EXACT)
         return both[:, :128], both[:, 128:]
+
+    HALVES = (0, 1)
 
     def wide(values):
         return jnp.concatenate([values, values], axis=1)
@@ -689,8 +751,6 @@
         send(x_base + 3 + pair, block, block, dev_c)
     for copy in local_copies:
         copy.wait()
-    for pair in (2, 3, 1):
-        send(cot_base + pair - 1, cot_z.at[z_at], cot_z.at[z_at], dev_z[pair])
     for pair in range(4):
         arrived(x_base + 3 + pair, x_block(z_pair[pair], 1 - core))
     attn_ready(0)
@@ -702,81 +762,112 @@
     qk_gain = (gain_at(query_gain_ref, col), gain_at(key_gain_ref, col))
     for index in range(2):
         hat_s[index] = dot_nn(x_full[...], wqkv[:, pl.ds(index * DC, DC)])
-    scal_send(0, hat_s[0] * hat_s[0], hat_s[1] * hat_s[1])
+    for half in HALVES:
+        query, key = hat_s[0, tokens(half), :], hat_s[1, tokens(half), :]
+        scal_send(0, half, query * query, key * key)
     attn_relay(3)
     for index in range(3):
         mlp_send(index)
     attn_ready(2)
     low_s[2] = dot_nn(x_full[...], wqkv[:, pl.ds(2 * DC, DC)]).astype(BF)
-    scales = [lax.rsqrt(total / D + EPS) for total in scal_get(0)]
-    work_s[0] = jnp.concatenate(scales, axis=1)
-    for index in range(2):
-        hat = hat_s[index] * wide(scales[index])
-        hat_s[index] = hat
-        normed = hat * qk_gain[index]
-        for head in range(2):
-            part = normed[:, head * HD : (head + 1) * HD]
-            turned = part * cos_s[...] + pltpu.roll(part, HD // 2, 1) * sin_s[...]
-            if index == 0:
-                turned = turned * (HD**-0.5)
-            low_s[index, :, pl.ds(head * HD, HD)] = turned.astype(BF)
+    for half in HALVES:
+        scales = [lax.rsqrt(total / D + EPS) for total in scal_get(0, half)]
+        rows = tokens(half)
+        work_s[0, rows, :] = jnp.concatenate(scales, axis=1)
+        for index in range(2):
+            hat = hat_s[index, rows, :] * wide(scales[index])
+            hat_s[index, rows, :] = hat
+            normed = hat * qk_gain[index]
+            for head in range(2):
+                part = normed[:, head * HD : (head + 1) * HD]
+                turned = part * cos_s[rows, :] + pltpu.roll(part, HD // 2, 1) * sin_s[rows, :]
+                if index == 0:
+                    turned = turned * (HD**-0.5)
+                low_s[index, rows, pl.ds(head * HD, HD)] = turned.astype(BF)
 
     chunk = 128
 
-    def visible(at):
-        query = at * chunk + lax.broadcasted_iota(jnp.int32, (chunk, T), 0)
-        key = lax.broadcasted_iota(jnp.int32, (chunk, T), 1)
-        oldest = query - pos_s[aligned(at * chunk, chunk), :1]
-        return (key <= query) & (key >= oldest)
-
-    def attend_chunk(at, carry):
-        rows = aligned(at * chunk, chunk)
-        allowed = visible(at)
-        for head in range(2):
-            lanes = pl.ds(head * HD, HD)
-            scores = dot_nt(low_s[0, rows, lanes], low_s[1, :, lanes])
-            scores = jnp.where(allowed, scores, MASKED)
-            exponent = jnp.exp(scores - jnp.max(scores, axis=1, keepdims=True))
-            probs = exponent / jnp.sum(exponent, axis=1, keepdims=True)
-            probs_s[head, rows, :] = probs
-            att_s[rows, lanes] = dot_nn(probs.astype(BF), low_s[2, :, lanes]).astype(BF)
-        return carry
-
-    lax.fori_loop(0, T // chunk, attend_chunk, 0)
-
-    attn_ready(3)
-    branch_sum = Reduce(lambda start: dot_nt(att_s[...], wo[pl.ds(start, DC), :]), False)
-    branch_sum.start()
-    mlp_relay(0)
-    branch = branch_sum.finish()
-    scal_send(1, branch * branch)
-    work_s[1] = branch
-    braw_s[z_at] = branch.astype(BF)
-
-    def middle_block(pair, place):
+    def attend(half):
+        count = (half + 1) * HT
+        keys = pl.ds(0, count)
+
+        def attend_chunk(at, carry):
+            rows = aligned(at * chunk, chunk)
+            query = at * chunk + lax.broadcasted_iota(jnp.int32, (chunk, count), 0)
+            key = lax.broadcasted_iota(jnp.int32, (chunk, count), 1)
+            oldest = query - pos_s[rows, :1]
+            allowed = (key <= query) & (key >= oldest)
+            for head in range(2):
+                lanes = pl.ds(head * HD, HD)
+                scores = dot_nt(low_s[0, rows, lanes], low_s[1, keys, lanes])
+                scores = jnp.where(allowed, scores, MASKED)
+                exponent = jnp.exp(scores - jnp.max(scores, axis=1, keepdims=True))
+                probs = exponent / jnp.sum(exponent, axis=1, keepdims=True)
+                probs_s[head, rows, keys] = probs
+                att_s[rows, lanes] = dot_nn(probs.astype(BF), low_s[2, keys, lanes]).astype(BF)
+            return carry
+
+        first = half * (HT // chunk)
+        lax.fori_loop(first, first + HT // chunk, attend_chunk, 0)
+
+    branch_sums = [
+        Reduce(
+            lambda rows, start: dot_nt(att_s[rows, :], wo[pl.ds(start, DC), :]), False, half
+        )
+        for half in HALVES
+    ]
+
+    def middle_block(pair, place, half):
+        rows = tokens(half)
         at = 2 * place + core
-        raw = work_s[1] if pair == 0 else braw_s[place].astype(F32)
-        hat = raw * wide(work_s[2, :, :128])
-        inputs = x_full[:, aligned(at * DC, DC)].astype(F32)
+        raw = work_s[1, rows, :] if pair == 0 else braw_s[place, rows, :].astype(F32)
+        hat = raw * wide(work_s[2, rows, :128])
+        inputs = x_full[rows, aligned(at * DC, DC)].astype(F32)
         middle = inputs + hat * gain_at(attn_gain_ref, at)
         if pair == 0:
-            bhat_s[...] = hat
-            middle_s[...] = middle
+            bhat_s[rows, :] = hat
+            middle_s[rows, :] = middle
         return middle.astype(BF)
 
-    mid_gather = Gather(mid_full, True, braw_s, middle_block)
-    mid_gather.start()
-    total, _ = scal_get(1)
-    work_s[2, :, :128] = lax.rsqrt(total / D + EPS)
+    mid_gathers = [Gather(mid_full, True, braw_s, middle_block, half) for half in HALVES]
+
+    def branch_done(half):
+        rows = tokens(half)
+        branch = branch_sums[half].finish()
+        scal_send(1, half, branch * branch)
+        work_s[1, rows, :] = branch
+        braw_s[z_at, rows, :] = branch.astype(BF)
+        mid_gathers[half].start()
+
+    def branch_scaled(half):
+        total, _ = scal_get(1, half)
+        work_s[2, tokens(half), :128] = lax.rsqrt(total / D + EPS)
+
+    attend(0)
+    attn_ready(3)
+    branch_sums[0].start()
+    attend(1)
+    branch_sums[1].start()
+    mlp_relay(0)
+    branch_done(0)
     mlp_relay(1)
+    branch_scaled(0)
+    branch_done(1)
+    mid_gathers[0].finish_own()
+    branch_scaled(1)
     mlp_relay(2)
-    mid_gather.finish_own()
+    mid_gathers[1].finish_own()
+    for pair in (2, 3, 1):
+        send(cot_base + pair - 1, cot_z.at[z_at], cot_z.at[z_at], dev_z[pair])
+    mid_gathers[0].finish_other()
     mlp_ready(0)
     mlp_ready(1)
 
     tile = 256
 
-    def forward_tiles(rows):
+    def forward_tiles(half):
+        rows = half_rows(half, True)
+
         def forward_tile(at, carry):
             lanes = aligned(at * tile, tile)
             lanes_up = aligned(at * tile + FH, tile)
@@ -789,42 +880,66 @@
 
         lax.fori_loop(0, FH // tile, forward_tile, 0)
 
-    forward_tiles(mid_gather.rows)
-    mid_gather.finish_other()
-    forward_tiles(mid_gather.rows_other)
+    ffn_sums = [
+        Reduce(
+            lambda rows, start: dot_nt(mixed_s[rows, :], wd[pl.ds(start, DC), :]), True, half
+        )
+        for half in HALVES
+    ]
+    mlp_gain = gain_at(mlp_gain_ref, col)
+
+    def grad_ffn_block(pair, place, half):
+        rows = tokens(half)
+        at = 2 * place + core
+        raw = work_s[1, rows, :] if pair == 0 else raw_s[place, rows, :].astype(F32)
+        scale = wide(work_s[2, rows, 128:])
+        grad = cot_z[place, rows, :].astype(F32) * gain_at(mlp_gain_ref, at)
+        return (scale * (grad - raw * scale * wide(inner_s[rows, :]))).astype(BF)
+
+    gf_gathers = [Gather(gf_full, True, raw_s, grad_ffn_block, half) for half in HALVES]
+
+    def ffn_done(half):
+        rows = tokens(half)
+        ffn = ffn_sums[half].finish()
+        cot = cot_z[z_at, rows, :].astype(F32)
+        scal_send(2, half, ffn * ffn, cot * mlp_gain * ffn)
+        work_s[1, rows, :] = ffn
+        raw_s[z_at, rows, :] = ffn.astype(BF)
+        gf_gathers[half].start()
+
+    def ffn_scaled(half):
+        rows = tokens(half)
+        total, inner = scal_get(2, half)
+        scale = lax.rsqrt(total / D + EPS)
+        work_s[2, rows, 128:] = scale
+        inner_s[rows, :] = inner * scale / D
+        ffn_hat = work_s[1, rows, :] * wide(scale)
+        out_lo[rows, :] = (middle_s[rows, :] + ffn_hat * mlp_gain).astype(BF)
+        cot = cot_z[z_at, rows, :].astype(F32)
+        return jnp.sum(cot * ffn_hat, axis=0, keepdims=True)
+
+    forward_tiles(0)
     mlp_ready(2)
-    ffn_sum = Reduce(lambda start: dot_nt(mixed_s[...], wd[pl.ds(start, DC), :]), True)
-    ffn_sum.start()
-    ffn_sum.planes()
-    ffn = ffn_sum.finish()
-    cot = cot_z[z_at].astype(F32)
-    mlp_gain = gain_at(mlp_gain_ref, col)
-    scal_send(2, ffn * ffn, cot * mlp_gain * ffn)
-    work_s[1] = ffn
-    raw_s[z_at] = ffn.astype(BF)
-
-    def grad_ffn_block(pair, place):
-        at = 2 * place + core
-        raw = work_s[1] if pair == 0 else raw_s[place].astype(F32)
-        scale = wide(work_s[2, :, 128:])
-        grad = cot_z[place].astype(F32) * gain_at(mlp_gain_ref, at)
-        return (scale * (grad - raw * scale * wide(own_s[0, pl.ds(0, T), :128]))).astype(BF)
-
-    gf_gather = Gather(gf_full, True, raw_s, grad_ffn_block)
-    gf_gather.start()
+    ffn_sums[0].start()
+    mid_gathers[1].finish_other()
+    forward_tiles(1)
+    ffn_sums[1].start()
+    ffn_sums[0].planes()
+    ffn_sums[1].planes()
+    ffn_done(0)
     for pair in (1, 2, 3):
         arrived(cot_base + pair - 1, cot_z.at[z_pair[pair]])
-    total, inner = scal_get(2)
-    ffn_scale = lax.rsqrt(total / D + EPS)
-    work_s[2, :, 128:] = ffn_scale
-    own_s[0, pl.ds(0, T), :128] = inner * ffn_scale / D
-    ffn_hat = work_s[1] * wide(ffn_scale)
-    out_lo[...] = (middle_s[...] + ffn_hat * mlp_gain).astype(BF)
+    mlp_gain_part = ffn_scaled(0)
+    ffn_done(1)
+    gf_gathers[0].finish_own()
+    gain_s[row, 3:4, :] = mlp_gain_part + ffn_scaled(1)
     lo_copy = local(out_lo, layer_out)
-    gain_s[row, 3:4, :] = jnp.sum(cot * ffn_hat, axis=0, keepdims=True)
-    gf_gather.finish_own()
-
-    def backward_tiles(rows):
+    gf_gathers[1].finish_own()
+    gf_gathers[0].finish_other()
+
+    def backward_tiles(half):
+        rows = half_rows(half, True)
+
         def backward_tile(at, carry):
             lanes = aligned(at * tile, tile)
             lanes_up = aligned(at * tile + FH, tile)
@@ -838,10 +953,6 @@
 
         lax.fori_loop(0, FH // tile, backward_tile, 0)
 
-    backward_tiles(gf_gather.rows)
-    gf_gather.finish_other()
-    backward_tiles(gf_gather.rows_other)
-
     def lanes_of(owner):
         return aligned(owner * DR, DR)
 
@@ -858,48 +969,70 @@
         for part in range(2):
             stage_gu[slot, :, pl.ds(part * FH, FH)] = gu_piece(owner, part).astype(BF)
 
+    mid_sums = [
+        Reduce(lambda rows, start: dot_nt(gu_s[rows, :], wgu[pl.ds(start, DC), :]), True, half)
+        for half in HALVES
+    ]
+    attn_gain = gain_at(attn_gain_ref, col)
+
+    def grad_branch_block(pair, place, half):
+        rows = tokens(half)
+        at = 2 * place + core
+        scale = wide(work_s[2, rows, :128])
+        raw = middle_s[rows, :] if pair == 0 else raw_s[place, rows, :].astype(F32)
+        hat = bhat_s[rows, :] if pair == 0 else braw_s[place, rows, :].astype(F32) * scale
+        inner = wide(inner_s[rows, :])
+        return (scale * (raw * gain_at(attn_gain_ref, at) - hat * inner)).astype(BF)
+
+    gb_gathers = [Gather(gb_full, False, raw_s, grad_branch_block, half) for half in HALVES]
+
+    def mid_done(half):
+        rows = tokens(half)
+        grad_middle = cot_z[z_at, rows, :].astype(F32) + mid_sums[half].finish()
+        scal_send(3, half, grad_middle * attn_gain * bhat_s[rows, :])
+        middle_s[rows, :] = grad_middle
+        raw_s[z_at, rows, :] = grad_middle.astype(BF)
+        gb_gathers[half].start()
+
+    def mid_scaled(half):
+        inner, _ = scal_get(3, half)
+        inner_s[tokens(half), :] = inner / D
+
     grad_base = counter.take(6)
+    backward_tiles(0)
+    gf_gathers[0].finish_raw()
+    mid_sums[0].start()
+    gf_gathers[1].finish_other()
     stage_down[0] = down_piece(row_d).astype(BF)
     down_sends = [send(grad_base, stage_down.at[0], rel_mlp.at[:, DOWN], dev_x)]
-    mid_sum = Reduce(lambda start: dot_nt(gu_s[...], wgu[pl.ds(start, DC), :]), True)
-    mid_sum.start()
+    backward_tiles(1)
+    gf_gathers[1].finish_raw()
+    mid_sums[1].start()
     gu_stage(0, row_d)
     gu_sends = [send(grad_base + 1, stage_gu.at[0], rel_mlp.at[:, GU], dev_x)]
+    mid_sums[0].planes()
+    mid_sums[1].planes()
     stage_down[1] = down_piece(row_x).astype(BF)
     down_sends.append(send(grad_base + 2, stage_down.at[1], land_mlp.at[1, :, DOWN], dev_x))
-    mid_sum.planes()
+    mid_done(0)
     arrived(grad_base, rel_mlp.at[:, DOWN])
     stage_down[2] = (down_piece(row_y) + rel_mlp[:, DOWN].astype(F32)).astype(BF)
     down_sends.append(send(grad_base + 4, stage_down.at[2], land_mlp.at[2, :, DOWN], dev_y))
     gu_stage(1, row_x)
     gu_sends.append(send(grad_base + 3, stage_gu.at[1], land_mlp.at[1, :, GU], dev_x))
-    grad_middle = cot_z[z_at].astype(F32) + mid_sum.finish()
-    attn_gain = gain_at(attn_gain_ref, col)
-    scal_send(3, grad_middle * attn_gain * bhat_s[...])
-    middle_s[...] = grad_middle
-    for copy in gf_gather.raw_sends:
-        sent(copy)
-    raw_s[z_at] = grad_middle.astype(BF)
-
-    def grad_branch_block(pair, place):
-        at = 2 * place + core
-        scale = wide(work_s[2, :, :128])
-        raw = middle_s[...] if pair == 0 else raw_s[place].astype(F32)
-        hat = bhat_s[...] if pair == 0 else braw_s[place].astype(F32) * scale
-        inner = wide(own_s[0, pl.ds(0, T), :128])
-        return (scale * (raw * gain_at(attn_gain_ref, at) - hat * inner)).astype(BF)
-
-    gb_gather = Gather(gb_full, False, raw_s, grad_branch_block)
-    gb_gather.start()
+    mid_scaled(0)
+    mid_done(1)
+    gb_gathers[0].finish_own()
     gain_s[row, 2:3, :] = jnp.sum(middle_s[...] * bhat_s[...], axis=0, keepdims=True)
-    inner, _ = scal_get(3)
-    own_s[0, pl.ds(0, T), :128] = inner / D
+    mid_scaled(1)
     arrived(grad_base + 1, rel_mlp.at[:, GU])
     for part in range(2):
-        half = pl.ds(part * FH, FH)
-        stage_gu[2, :, half] = (gu_piece(row_y, part) + rel_mlp[:, half].astype(F32)).astype(BF)
+        half_lanes = pl.ds(part * FH, FH)
+        stage_gu[2, :, half_lanes] = (
+            gu_piece(row_y, part) + rel_mlp[:, half_lanes].astype(F32)
+        ).astype(BF)
     gu_sends.append(send(grad_base + 5, stage_gu.at[2], land_mlp.at[2, :, GU], dev_y))
-    gb_gather.finish_own()
+    gb_gathers[1].finish_own()
 
     ga_s[...] = dot_nn(gb_full[...], wo[...]).astype(BF)
 
@@ -966,22 +1099,32 @@
     )
     o_grad.start()
 
-    def attend_back_chunk(at, carry):
-        rows = aligned(at * chunk, chunk)
-        for head in range(2):
-            lanes = pl.ds(head * HD, HD)
-            grad_probs = dot_nt(ga_s[rows, lanes], low_s[2, :, lanes])
-            probs = probs_s[head, rows, :]
-            inner = jnp.sum(probs * grad_probs, axis=1, keepdims=True)
-            grad_scores = (probs * (grad_probs - inner)).astype(BF)
-            gs_s[head, rows, :] = grad_scores
-            gqk_s[0, rows, lanes] = dot_nn(grad_scores, low_s[1, :, lanes])
-        return carry
-
-    lax.fori_loop(0, T // chunk, attend_back_chunk, 0)
+    def attend_back(half):
+        count = (half + 1) * HT
+        keys = pl.ds(0, count)
+
+        def attend_back_chunk(at, carry):
+            rows = aligned(at * chunk, chunk)
+            for head in range(2):
+                lanes = pl.ds(head * HD, HD)
+                grad_probs = dot_nt(ga_s[rows, lanes], low_s[2, keys, lanes])
+                probs = probs_s[head, rows, keys]
+                inner = jnp.sum(probs * grad_probs, axis=1, keepdims=True)
+                grad_scores = (probs * (grad_probs - inner)).astype(BF)
+                gs_s[head, rows, keys] = grad_scores
+                gqk_s[0, rows, lanes] = dot_nn(grad_scores, low_s[1, keys, lanes])
+            return carry
+
+        first = half * (HT // chunk)
+        lax.fori_loop(first, first + HT // chunk, attend_back_chunk, 0)
+
+    for half in HALVES:
+        attend_back(half)
+    early, last = pl.ds(0, HT), pl.ds(HT, HT)
     for head in range(2):
         lanes = pl.ds(head * HD, HD)
-        gqk_s[1, :, lanes] = dot_tn(gs_s[head], low_s[0, :, lanes])
+        gqk_s[1, early, lanes] = dot_tn(gs_s[head, :, early], low_s[0, :, lanes])
+        gqk_s[1, last, lanes] = dot_tn(gs_s[head, last, last], low_s[0, last, lanes])
     inners = []
     for index in range(2):
         for head in range(2):
@@ -994,14 +1137,20 @@
         weighted = gqk_s[index] * hat_s[index]
         gain_s[row, index : index + 1, :] = jnp.sum(weighted, axis=0, keepdims=True)
         inners.append(weighted * qk_gain[index])
-    scal_send(4, inners[0], inners[1])
+    for half in HALVES:
+        part = slice(half * HT, (half + 1) * HT)
+        scal_send(4, half, inners[0][part], inners[1][part])
     gain_base = counter.take(3)
     for slot, device in enumerate((dev_x, dev_y, dev_d)):
         send(gain_base + slot, gain_s.at[row], gain_s.at[row], device)
     for head in range(2):
         lanes = pl.ds(head * HD, HD)
-        gqkv_s[:, pl.ds(2 * DC + head * HD, HD)] = dot_tn(
-            probs_s[head].astype(BF), ga_s[:, lanes]
+        out_lanes = pl.ds(2 * DC + head * HD, HD)
+        gqkv_s[early, out_lanes] = dot_tn(
+            probs_s[head, :, early].astype(BF), ga_s[:, lanes]
+        ).astype(BF)
+        gqkv_s[last, out_lanes] = dot_tn(
+            probs_s[head, last, last].astype(BF), ga_s[last, lanes]
         ).astype(BF)
     v_grad = AttnGrad(
         1,
@@ -1012,14 +1161,26 @@
         pl.ds(2 * DC, DC),
     )
     v_grad.start()
-    totals = scal_get(4)
-    for index in range(2):
-        scale = wide(work_s[0, :, index * 128 : (index + 1) * 128])
-        gqkv_s[:, pl.ds(index * DC, DC)] = (
-            scale * (gqk_s[index] * qk_gain[index] - hat_s[index] * wide(totals[index] / D))
-        ).astype(BF)
-    in_sum = Reduce(lambda start: dot_nt(gqkv_s[...], wqkv[pl.ds(start, DC), :]), False)
-    in_sum.start()
+    for half in HALVES:
+        rows = tokens(half)
+        totals = scal_get(4, half)
+        for index in range(2):
+            scale = wide(work_s[0, rows, index * 128 : (index + 1) * 128])
+            gqkv_s[rows, pl.ds(index * DC, DC)] = (
+                scale
+                * (
+                    gqk_s[index, rows, :] * qk_gain[index]
+                    - hat_s[index, rows, :] * wide(totals[index] / D)
+                )
+            ).astype(BF)
+    in_sums = [
+        Reduce(
+            lambda rows, start: dot_nt(gqkv_s[rows, :], wqkv[pl.ds(start, DC), :]), False, half
+        )
+        for half in HALVES
+    ]
+    for half in HALVES:
+        in_sums[half].start()
     o_grad.relay()
     gu_stage(3, row)
     own_copies.append(local(stage_gu.at[3], land_mlp.at[0, :, GU]))
@@ -1032,7 +1193,9 @@
     )
     qk_grad.start()
     v_grad.relay()
-    work_s[1] = middle_s[...] + in_sum.finish()
+    for half in HALVES:
+        rows = tokens(half)
+        work_s[1, rows, :] = middle_s[rows, :] + in_sums[half].finish()
     late.append(local(work_s.at[1], grad_in))
     late.append(lo_copy)
     qk_grad.relay()
@@ -1046,8 +1209,8 @@
         grad.finish()
     for copy in late:
         copy.wait()
-    for copy in pending:
-        copy.wait_send()
+    for copy in list(pending):
+        sent(copy)
 
 
 def total_kernel(
@@ -1092,7 +1255,7 @@
     hbm = pl.BlockSpec(memory_space=pl.ANY)
     vmem = pl.BlockSpec(memory_space=pltpu.VMEM)
     sds = jax.ShapeDtypeStruct
-    copies = 240
+    copies = 320
     landed = pl.pallas_call(
         block_kernel,
         out_shape=[
@@ -1127,6 +1290,7 @@
             pltpu.VMEM((T, DC), F32),
             pltpu.VMEM((T, DC), F32),
             pltpu.VMEM((3, T, DC), F32),
+            pltpu.VMEM((T, HD), F32),
             pltpu.VMEM((T, DC), BF),
             pltpu.VMEM((T, DC), BF),
             pltpu.VMEM((T, 3 * DC), BF),
@@ -1139,7 +1303,8 @@
             pltpu.VMEM((4, T, DC), BF),
             pltpu.VMEM((3, T, DC), BF),
             pltpu.VMEM((3, T, DC), BF),
-            pltpu.VMEM((LAYER_STAGES, 8, 8, T), F32),
+            pltpu.VMEM((T, DC), BF),
+            pltpu.VMEM((LAYER_STAGES, 2, 8, 8, HT), F32),
             pltpu.VMEM((4, 8, DC), F32),
             pltpu.VMEM((4, DR, FH), BF),
             pltpu.VMEM((4, DR, 2 * FH), BF),

time: 351 us -> 312 us (0.89)
  Pallas kernels: 346 us -> 306 us
    pallas_call x1, Pallas kernels: 337 us -> 297 us  [on_device_kernel(): pl.pallas_call(block_kernel, out_shape=[sds((T, DC), BF), sds((T, DC), F3...]
where the time goes in v3:
time: 312 us; the launch traced here: 307 us
  Pallas kernels  306 us (98%)
    pallas_call x1, Pallas kernels, on_device_kernel(): pl.pallas_call(block_kernel, out_shape=[sds((T, DC), BF), sds((T, DC), F3...  297 us
    pallas_call x1, Pallas kernels, on_device_kernel(): pl.pallas_call(total_kernel, grid=(DR // step,), out_shape=[sds((T, DC),...  9.13 us

profile of v3, /device:TPU:0, one launch (start us, length us, event | category | flops | bytes accessed | tf_op | source)
XLA Modules:
  0.0 307.2 jit_solution(4979031850685868160)
XLA Ops:
  0.7 296.9 %shard_map.237 = (bf16[512,256]{1,0:T(8,128)(2,1)}, f32[512,256]{1,0:T(8,128)}, f32[8,256]{1,0:T(8,128)}, bf16[3,512,1536]{2,1,0:T(8,128)(2,1)}, bf16[3,512,1024]{2,1,0:T(8,128)(2,1)}) custom-call(bf16[512,256]{1,0:T(8,128)(2,1)} %x_hbm.1, bf16[512,256]{1,0:T(8,128)(2,1)} %wq_hbm.1, bf16[512,256]{1,0:T(8,128)(2,1)} %wk_hbm.1, bf16[512,256]{1,0:T(8,128)(2,1)} %wv_hbm.1, ...), custom_call_target="tpu_custom_call" | custom-call | flops 26800001024 | bytes 16000000 | tf_op jit(solution)/shard_map/pallas_call | solution.py:1259
  297.6 9.1 %shard_map.238 = (bf16[512,256]{1,0:T(8,128)(2,1)}, f32[512,256]{1,0:T(8,128)}, f32[512,256]{1,0:T(8,128)}, f32[512,256]{1,0:T(8,128)}, f32[512,256]{1,0:T(8,128...) custom-call(bf16[512,256]{1,0:T(8,128)(2,1)} %get-tuple-element.31.l, ...), custom_call_target="tpu_custom_call" | custom-call | tf_op jit(solution)/shard_map/pallas_call | solution.py:1346

commit v4 on v3

--- a/solution.py
+++ b/solution.py
@@ -318,11 +318,11 @@
     wu_hbm,
     wd_hbm,
     cot_hbm,
-    query_gain_ref,
-    key_gain_ref,
-    attn_gain_ref,
-    mlp_gain_ref,
-    pos_ref,
+    query_gain_hbm,
+    key_gain_hbm,
+    attn_gain_hbm,
+    mlp_gain_hbm,
+    pos_hbm,
     layer_out,
     grad_in,
     gains_out,
@@ -371,6 +371,11 @@
     rel_mlp,
     rel_attn,
     out_lo,
+    query_gain_ref,
+    key_gain_ref,
+    attn_gain_ref,
+    mlp_gain_ref,
+    pos_ref,
     send_sem,
     recv_sem,
     local_sem,
@@ -452,6 +457,13 @@
         land_r[...] = jnp.zeros_like(land_r)
         land_z[0] = jnp.zeros_like(land_z[0])
 
+    small_copies = [
+        local(query_gain_hbm, query_gain_ref),
+        local(key_gain_hbm, key_gain_ref),
+        local(attn_gain_hbm, attn_gain_ref),
+        local(mlp_gain_hbm, mlp_gain_ref),
+    ]
+    pos_copy = local(pos_hbm, pos_ref)
     half_mine = aligned(y_at * FH, FH)
     half_other = aligned((1 - y_at) * FH, FH)
     rows_mine = aligned(row * DR, DR)
@@ -479,6 +491,9 @@
     def tokens(half):
         return pl.ds(half * HT, HT)
 
+    gather_base = counter.take(2 * 16)
+    gather_sends = ([], [])
+
     class Gather:
         def __init__(self, buf, plane, raw, process, half):
             self.buf = buf
@@ -486,13 +501,13 @@
             self.raw = raw
             self.process = process
             self.half = half
-            self.base_z = counter.take(3)
-            self.relay = counter.take()
-            self.base_c = counter.take(4)
+            self.base_z = gather_base + 16 * half
+            self.relay = self.base_z + 3
+            self.base_c = self.base_z + 4
+            self.base_y = self.base_z + 8
+            self.base_cy = self.base_z + 12
             self.rows = own_rows(half, plane)
             if plane:
-                self.base_y = counter.take(4)
-                self.base_cy = counter.take(4)
                 self.rows_other = other_rows(half)
 
         def block(self, rows, place, parity=None):
@@ -500,50 +515,53 @@
             return rows, aligned(at * DC, DC)
 
         def start(self):
-            self.raw_sends = []
+            self.finish_sends()
             own = self.raw.at[z_at, tokens(self.half)]
             for pair in (2, 3, 1):
                 when = middle if pair == 3 else None
-                self.raw_sends.append(
-                    send(self.base_z + pair - 1, own, own, dev_z[pair], when=when)
-                )
-
-        def finish_own(self):
-            for pair in (0, 2, 1, 3):
+                self.send(self.base_z + pair - 1, own, own, dev_z[pair], None, when)
+
+        def send(self, *copy):
+            gather_sends[self.half].append(send(*copy))
+
+        def pass_on(self, *pairs):
+            for pair in pairs:
                 place = z_pair[pair]
                 if pair:
                     raw = self.raw.at[place, tokens(self.half)]
                     arrived(self.base_z + pair - 1, raw)
                 if pair == 2:
-                    self.raw_sends.append(
-                        send(self.base_z + 2, raw, raw, dev_z[1], self.relay, middle)
-                    )
+                    self.send(self.base_z + 2, raw, raw, dev_z[1], self.relay, middle)
                 where = self.block(self.rows, place)
                 self.buf[where] = self.process(pair, place, self.half)
                 block = self.buf.at[where]
                 if self.plane:
-                    send(self.base_y + pair, block, block, dev_y)
-                send(self.base_c + pair, block, block, dev_c)
+                    self.send(self.base_y + pair, block, block, dev_y)
+                self.send(self.base_c + pair, block, block, dev_c)
+
+        def finish_own(self):
             for pair in range(4):
                 arrived(
                     self.base_c + pair, self.buf.at[self.block(self.rows, z_pair[pair], 1 - core)]
                 )
 
-        def finish_raw(self):
-            for copy in self.raw_sends:
+        def finish_sends(self):
+            for copy in gather_sends[self.half]:
                 sent(copy)
+            gather_sends[self.half].clear()
 
         def finish_other(self):
             for pair in range(4):
                 block = self.buf.at[self.block(self.rows_other, z_pair[pair])]
                 arrived(self.base_y + pair, block)
-                send(self.base_cy + pair, block, block, dev_c)
+                self.send(self.base_cy + pair, block, block, dev_c)
             for pair in range(4):
                 arrived(
                     self.base_cy + pair,
                     self.buf.at[self.block(self.rows_other, z_pair[pair], 1 - core)],
                 )
 
+    reduce_base = counter.take(2 * 12)
     stage_sends = ([], [])
 
     class Reduce:
@@ -553,15 +571,15 @@
             self.partial = partial
             self.plane = plane
             self.half = half
-            self.base_c = counter.take(4)
-            self.base_z = counter.take(3)
-            self.relay = counter.take()
+            self.base_c = reduce_base + 12 * half
+            self.base_z = self.base_c + 4
+            self.relay = self.base_c + 7
+            self.base_y = self.base_c + 8
             self.left = half_rows(half, plane)
             self.all_rows = pl.ds(half * 2 * HT, 2 * HT if plane else HT)
             self.rows = own_rows(half, True) if plane else self.all_rows
             self.tokens = tokens(half)
             if plane:
-                self.base_y = counter.take(4)
                 self.rows_other = other_rows(half)
 
         def start(self):
@@ -621,8 +639,8 @@
             else:
                 self.send(self.base_z + slot, stage, land, dev_z[pair])
 
-        def planes(self):
-            for slot in range(4):
+        def planes(self, *slots):
+            for slot in slots:
                 landed = land_y.at[slot, self.tokens]
                 arrived(self.base_y + slot, landed)
                 self.pass_on(slot, landed)
@@ -641,7 +659,8 @@
     first_row = (pick == 0).astype(F32)
     second_row = (pick == 1).astype(F32)
     spread = ((pick == 0) & (lane < 128)).astype(F32) + ((pick == 1) & (lane >= 128)).astype(F32)
-    scal_base = counter.take(7 * 2 * LAYER_STAGES)
+    scal_base = counter.take(4 * 7)
+    scal_sends = ([], [], [], [])
 
     def scal_send(stage, half, first, second=None):
         mine = dot_nt(first_row, first, EXACT)
@@ -649,13 +668,17 @@
             mine = mine + dot_nt(second_row, second, EXACT)
         place = scal_s.at[stage, half, col]
         place[...] = mine
+        turn = 2 * half + stage % 2
+        for copy in scal_sends[turn]:
+            sent(copy)
+        scal_sends[turn].clear()
         for step in range(1, 8):
-            index = scal_base + 7 * (2 * stage + half) + step - 1
-            send(index, place, place, (row, lax.rem(col + step, 8)))
+            index = scal_base + 7 * turn + step - 1
+            scal_sends[turn].append(send(index, place, place, (row, lax.rem(col + step, 8))))
 
     def scal_get(stage, half):
         for step in range(1, 8):
-            index = scal_base + 7 * (2 * stage + half) + step - 1
+            index = scal_base + 7 * (2 * half + stage % 2) + step - 1
             arrived(index, scal_s.at[stage, half, lax.rem(col + 8 - step, 8)])
         total = scal_s[stage, half, 0]
         for index in range(1, 8):
@@ -669,6 +692,7 @@
         return jnp.concatenate([values, values], axis=1)
 
     attn_base = counter.take(16)
+    weight_sends = []
     attn_hbm = (wq_hbm, wk_hbm, wv_hbm, wo_hbm)
 
     def attn_place(index, owner, part=None):
@@ -680,21 +704,26 @@
             return wqkv.at[rows, pl.ds(index * DC, DC)]
         return wo.at[rows, :]
 
+    def weight_send(*copy):
+        weight_sends.append(send(*copy))
+
     def attn_send(index):
-        send(attn_base + index, attn_hbm[index], attn_place(index, row), dev_x)
-        send(attn_base + 4 + index, attn_hbm[index], attn_place(index, row), dev_y)
+        weight_send(attn_base + index, attn_hbm[index], attn_place(index, row), dev_x)
+        weight_send(attn_base + 4 + index, attn_hbm[index], attn_place(index, row), dev_y)
 
     def attn_relay(index):
         arrived(attn_base + index, attn_place(index, row_x))
-        part = attn_place(index, row_x, 0)
-        send(attn_base + 8 + index, part, part, dev_y)
+        part = attn_place(index, row_x, 0 if index < 3 else None)
+        weight_send(attn_base + 8 + index, part, part, dev_y)
         arrived(attn_base + 4 + index, attn_place(index, row_y))
-        part = attn_place(index, row_y, 1)
-        send(attn_base + 12 + index, part, part, dev_x)
+        if index < 3:
+            part = attn_place(index, row_y, 1)
+            weight_send(attn_base + 12 + index, part, part, dev_x)
 
     def attn_ready(index):
-        arrived(attn_base + 8 + index, attn_place(index, row_d, 0))
-        arrived(attn_base + 12 + index, attn_place(index, row_d, 1))
+        arrived(attn_base + 8 + index, attn_place(index, row_d, 0 if index < 3 else None))
+        if index < 3:
+            arrived(attn_base + 12 + index, attn_place(index, row_d, 1))
 
     mlp_base = counter.take(9)
     mlp_hbm = (wg_hbm, wu_hbm, wd_hbm)
@@ -706,19 +735,19 @@
         return wd.at[rows, :]
 
     def mlp_send(index):
-        send(mlp_base + index, mlp_hbm[index].at[:, half_mine], mlp_place(index, row), dev_x)
-        send(mlp_base + 3 + index, mlp_hbm[index].at[:, half_other], mlp_place(index, row), dev_y)
+        weight_send(mlp_base + index, mlp_hbm[index].at[:, half_mine], mlp_place(index, row), dev_x)
+        weight_send(mlp_base + 3 + index, mlp_hbm[index].at[:, half_other], mlp_place(index, row), dev_y)
 
     def mlp_relay(index):
         place = mlp_place(index, row_y)
         arrived(mlp_base + 3 + index, place)
-        send(mlp_base + 6 + index, place, place, dev_x)
+        weight_send(mlp_base + 6 + index, place, place, dev_x)
 
     def mlp_ready(index):
         arrived(mlp_base + index, mlp_place(index, row_x))
         arrived(mlp_base + 6 + index, mlp_place(index, row_d))
 
-    for index in range(3):
+    for index in range(2):
         attn_send(index)
 
     x_base = counter.take(7)
@@ -731,6 +760,7 @@
         send(x_base + pair - 1, x_hbm, x_block(z_at, core), dev_z[pair])
     send(x_base + 3, x_hbm, x_block(z_at, core), dev_c)
 
+    pos_copy.wait()
     position_rows = jnp.broadcast_to(pos_ref[...].astype(F32), (8, T))
     position = dot_tn(position_rows, first_row[:, :HD], EXACT)
     pos_s[...] = position.astype(jnp.int32)
@@ -742,14 +772,15 @@
     sine = jnp.sin(angles)
     sin_s[...] = jnp.where(lane_at < HD // 2, -sine, sine)
 
-    for index in range(3):
+    for index in range(2):
         attn_relay(index)
+    attn_send(2)
     attn_send(3)
-    for pair in (1, 2, 3):
+    for pair in (2, 1, 3):
         block = x_block(z_pair[pair], core)
         arrived(x_base + pair - 1, block)
         send(x_base + 3 + pair, block, block, dev_c)
-    for copy in local_copies:
+    for copy in local_copies + small_copies:
         copy.wait()
     for pair in range(4):
         arrived(x_base + 3 + pair, x_block(z_pair[pair], 1 - core))
@@ -765,6 +796,7 @@
     for half in HALVES:
         query, key = hat_s[0, tokens(half), :], hat_s[1, tokens(half), :]
         scal_send(0, half, query * query, key * key)
+    attn_relay(2)
     attn_relay(3)
     for index in range(3):
         mlp_send(index)
@@ -852,13 +884,16 @@
     branch_done(0)
     mlp_relay(1)
     branch_scaled(0)
+    mid_gathers[0].pass_on(0)
     branch_done(1)
+    mid_gathers[0].pass_on(2, 1, 3)
+    branch_scaled(1)
+    mid_gathers[1].pass_on(0)
+    mlp_relay(2)
+    mid_gathers[1].pass_on(2, 1, 3)
+    for pair in (2, 3, 1):
+        weight_send(cot_base + pair - 1, cot_z.at[z_at], cot_z.at[z_at], dev_z[pair])
     mid_gathers[0].finish_own()
-    branch_scaled(1)
-    mlp_relay(2)
-    mid_gathers[1].finish_own()
-    for pair in (2, 3, 1):
-        send(cot_base + pair - 1, cot_z.at[z_at], cot_z.at[z_at], dev_z[pair])
     mid_gathers[0].finish_other()
     mlp_ready(0)
     mlp_ready(1)
@@ -921,20 +956,24 @@
     forward_tiles(0)
     mlp_ready(2)
     ffn_sums[0].start()
+    mid_gathers[1].finish_own()
     mid_gathers[1].finish_other()
     forward_tiles(1)
     ffn_sums[1].start()
-    ffn_sums[0].planes()
-    ffn_sums[1].planes()
-    ffn_done(0)
+    ffn_sums[0].planes(0, 1, 2, 3)
+    ffn_sums[1].planes(0, 1)
     for pair in (1, 2, 3):
         arrived(cot_base + pair - 1, cot_z.at[z_pair[pair]])
+    ffn_done(0)
+    ffn_sums[1].planes(2, 3)
     mlp_gain_part = ffn_scaled(0)
+    gf_gathers[0].pass_on(0)
     ffn_done(1)
+    gf_gathers[0].pass_on(2, 1, 3)
+    gain_s[row, 3:4, :] = mlp_gain_part + ffn_scaled(1)
+    gf_gathers[1].pass_on(0, 2, 1, 3)
+    lo_copy = local(out_lo, layer_out)
     gf_gathers[0].finish_own()
-    gain_s[row, 3:4, :] = mlp_gain_part + ffn_scaled(1)
-    lo_copy = local(out_lo, layer_out)
-    gf_gathers[1].finish_own()
     gf_gathers[0].finish_other()
 
     def backward_tiles(half):
@@ -956,18 +995,46 @@
     def lanes_of(owner):
         return aligned(owner * DR, DR)
 
-    GU = pl.ds(0, 2 * FH)
-    DOWN = pl.ds(2 * FH, FH)
-
     def down_piece(owner):
         return dot_tn(gf_full[:, lanes_of(owner)], mixed_s[...])
 
     def gu_piece(owner, part):
         return dot_tn(mid_full[:, lanes_of(owner)], gu_s[:, pl.ds(part * FH, FH)])
 
-    def gu_stage(slot, owner):
-        for part in range(2):
-            stage_gu[slot, :, pl.ds(part * FH, FH)] = gu_piece(owner, part).astype(BF)
+    grad_base = counter.take(9)
+    grad_sends = {}
+
+    def grad_lanes(part):
+        return pl.ds(part * FH, FH)
+
+    def grad_stage(slot, part):
+        if part == 2:
+            return stage_down.at[slot]
+        return stage_gu.at[slot, :, grad_lanes(part)]
+
+    def grad_piece(slot, part, more=None):
+        owner = (row_d, row_x, row_y, row)[slot]
+        total = down_piece(owner) if part == 2 else gu_piece(owner, part)
+        if more is not None:
+            total = total + more
+        grad_stage(slot, part)[...] = total.astype(BF)
+
+    def grad_send(slot, part, landing, device):
+        index = grad_base + 3 * slot + part
+        grad_sends[slot, part] = send(index, grad_stage(slot, part), landing, device)
+
+    def grad_diagonal(part):
+        grad_piece(0, part)
+        grad_send(0, part, rel_mlp.at[:, grad_lanes(part)], dev_x)
+
+    def grad_near(part):
+        grad_piece(1, part)
+        grad_send(1, part, land_mlp.at[1, :, grad_lanes(part)], dev_x)
+
+    def grad_relay(part):
+        arrived(grad_base + part, rel_mlp.at[:, grad_lanes(part)])
+        grad_piece(2, part, rel_mlp[:, grad_lanes(part)].astype(F32))
+        grad_send(2, part, land_mlp.at[2, :, grad_lanes(part)], dev_y)
 
     mid_sums = [
         Reduce(lambda rows, start: dot_nt(gu_s[rows, :], wgu[pl.ds(start, DC), :]), True, half)
@@ -998,105 +1065,100 @@
         inner, _ = scal_get(3, half)
         inner_s[tokens(half), :] = inner / D
 
-    grad_base = counter.take(6)
     backward_tiles(0)
-    gf_gathers[0].finish_raw()
+    gf_gathers[0].finish_sends()
     mid_sums[0].start()
+    gf_gathers[1].finish_own()
     gf_gathers[1].finish_other()
-    stage_down[0] = down_piece(row_d).astype(BF)
-    down_sends = [send(grad_base, stage_down.at[0], rel_mlp.at[:, DOWN], dev_x)]
+    grad_diagonal(2)
     backward_tiles(1)
-    gf_gathers[1].finish_raw()
+    gf_gathers[1].finish_sends()
     mid_sums[1].start()
-    gu_stage(0, row_d)
-    gu_sends = [send(grad_base + 1, stage_gu.at[0], rel_mlp.at[:, GU], dev_x)]
-    mid_sums[0].planes()
-    mid_sums[1].planes()
-    stage_down[1] = down_piece(row_x).astype(BF)
-    down_sends.append(send(grad_base + 2, stage_down.at[1], land_mlp.at[1, :, DOWN], dev_x))
+    grad_diagonal(0)
+    grad_diagonal(1)
+    mid_sums[0].planes(0, 1, 2, 3)
+    mid_sums[1].planes(0, 1)
     mid_done(0)
-    arrived(grad_base, rel_mlp.at[:, DOWN])
-    stage_down[2] = (down_piece(row_y) + rel_mlp[:, DOWN].astype(F32)).astype(BF)
-    down_sends.append(send(grad_base + 4, stage_down.at[2], land_mlp.at[2, :, DOWN], dev_y))
-    gu_stage(1, row_x)
-    gu_sends.append(send(grad_base + 3, stage_gu.at[1], land_mlp.at[1, :, GU], dev_x))
+    mid_sums[1].planes(2, 3)
+    grad_relay(2)
+    grad_near(2)
     mid_scaled(0)
+    gb_gathers[0].pass_on(0)
     mid_done(1)
+    grad_near(0)
+    gb_gathers[0].pass_on(2, 1, 3)
+    mid_scaled(1)
+    gb_gathers[1].pass_on(0)
+    grad_relay(0)
+    grad_near(1)
+    gb_gathers[1].pass_on(2, 1, 3)
+    grad_relay(1)
+    gain_s[row, 2:3, :] = jnp.sum(middle_s[...] * bhat_s[...], axis=0, keepdims=True)
     gb_gathers[0].finish_own()
-    gain_s[row, 2:3, :] = jnp.sum(middle_s[...] * bhat_s[...], axis=0, keepdims=True)
-    mid_scaled(1)
-    arrived(grad_base + 1, rel_mlp.at[:, GU])
-    for part in range(2):
-        half_lanes = pl.ds(part * FH, FH)
-        stage_gu[2, :, half_lanes] = (
-            gu_piece(row_y, part) + rel_mlp[:, half_lanes].astype(F32)
-        ).astype(BF)
-    gu_sends.append(send(grad_base + 5, stage_gu.at[2], land_mlp.at[2, :, GU], dev_y))
     gb_gathers[1].finish_own()
 
     ga_s[...] = dot_nn(gb_full[...], wo[...]).astype(BF)
 
+    whole = pl.ds(0, DR)
     upper = pl.ds(0, DR // 2)
     lower = pl.ds(DR // 2, DR // 2)
+    BY_Y = ((whole, 2),)
+    BY_BOTH = ((upper, 1), (lower, 2))
+    neighbours = {1: dev_x, 2: dev_y}
     attn_grad_base = counter.take(3 * 6)
     late = []
 
     class AttnGrad:
-        def __init__(self, order, left, right, stage, stage_lanes, lanes):
+        def __init__(self, order, routes, left, right, start, size):
             self.base = attn_grad_base + 6 * order
+            self.routes = routes
             self.left, self.right = left, right
-            self.stage, self.stage_lanes, self.lanes = stage, stage_lanes, lanes
+            self.start_lane, self.size = start, size
+            self.lanes = pl.ds(start, size)
 
         def at(self, slot, rows):
-            return self.stage.at[slot, rows, self.stage_lanes]
+            rows = pl.ds(slot // 2 * DR + rows.start, rows.size)
+            return gf_full.at[rows, pl.ds(slot % 2 * 4 * DC + self.start_lane, self.size)]
+
+        def piece(self, slot):
+            owner = (row_d, row_x, row_y, row)[slot]
+            piece = dot_tn(self.left[:, lanes_of(owner)], self.right())
+            self.at(slot, whole)[...] = piece.astype(BF)
 
         def start(self):
-            for slot, owner in enumerate((row_d, row_x, row_y, row)):
-                self.stage[slot, :, self.stage_lanes] = dot_tn(
-                    self.left[:, lanes_of(owner)], self.right()
+            self.piece(0)
+            for step, (rows, first) in enumerate(self.routes):
+                landing = rel_attn.at[rows, self.lanes]
+                send(self.base + step, self.at(0, rows), landing, neighbours[first])
+            self.piece(1)
+            self.piece(2)
+            for step, (rows, first) in enumerate(self.routes):
+                landing = land_attn.at[first, rows, self.lanes]
+                send(self.base + 2 + step, self.at(first, rows), landing, neighbours[first])
+            self.piece(3)
+            late.append(local(self.at(3, whole), land_attn.at[0, :, self.lanes]))
+
+        def relay(self):
+            for step, (rows, first) in enumerate(self.routes):
+                slot = 3 - first
+                arrived(self.base + step, rel_attn.at[rows, self.lanes])
+                stage = self.at(slot, rows)
+                stage[...] = (
+                    stage[...].astype(F32) + rel_attn[rows, self.lanes].astype(F32)
                 ).astype(BF)
-                if slot == 0:
-                    send(self.base, self.at(0, upper), rel_attn.at[upper, self.lanes], dev_x)
-                    send(self.base + 1, self.at(0, lower), rel_attn.at[lower, self.lanes], dev_y)
-                elif slot == 1:
-                    landing = land_attn.at[1, upper, self.lanes]
-                    send(self.base + 2, self.at(1, upper), landing, dev_x)
-                elif slot == 2:
-                    landing = land_attn.at[2, lower, self.lanes]
-                    send(self.base + 3, self.at(2, lower), landing, dev_y)
-                else:
-                    whole = self.at(3, pl.ds(0, DR))
-                    late.append(local(whole, land_attn.at[0, :, self.lanes]))
-
-        def relay(self):
-            for step, (slot, rows, device) in enumerate(((2, upper, dev_y), (1, lower, dev_x))):
-                arrived(self.base + step, rel_attn.at[rows, self.lanes])
-                self.stage[slot, rows, self.stage_lanes] = (
-                    self.stage[slot, rows, self.stage_lanes].astype(F32)
-                    + rel_attn[rows, self.lanes].astype(F32)
-                ).astype(BF)
-                send(
-                    self.base + 4 + step,
-                    self.at(slot, rows),
-                    land_attn.at[slot, rows, self.lanes],
-                    device,
-                )
+                landing = land_attn.at[slot, rows, self.lanes]
+                send(self.base + 4 + step, stage, landing, neighbours[slot])
 
         def finish(self):
-            arrived(self.base + 2, land_attn.at[1, upper, self.lanes])
-            arrived(self.base + 3, land_attn.at[2, lower, self.lanes])
-            arrived(self.base + 4, land_attn.at[2, upper, self.lanes])
-            arrived(self.base + 5, land_attn.at[1, lower, self.lanes])
-
-    stage_down[3] = down_piece(row).astype(BF)
-    own_copies = [local(stage_down.at[3], land_mlp.at[0, :, DOWN])]
-    for copy in down_sends:
-        sent(copy)
-    own_copies[0].wait()
-    first_lanes = pl.ds(0, DC)
-    o_grad = AttnGrad(
-        0, gb_full, lambda: att_s[...], stage_down, first_lanes, pl.ds(3 * DC, DC)
-    )
+            for step, (rows, first) in enumerate(self.routes):
+                arrived(self.base + 2 + step, land_attn.at[first, rows, self.lanes])
+                arrived(self.base + 4 + step, land_attn.at[3 - first, rows, self.lanes])
+
+    grad_piece(3, 2)
+    late.append(local(stage_down.at[3], land_mlp.at[0, :, grad_lanes(2)]))
+    for gather in gf_gathers:
+        gather.finish_sends()
+    o_grad = AttnGrad(0, BY_BOTH, gb_full, lambda: att_s[...], 3 * DC, DC)
     o_grad.start()
 
     def attend_back(half):
@@ -1152,14 +1214,7 @@
         gqkv_s[last, out_lanes] = dot_tn(
             probs_s[head, last, last].astype(BF), ga_s[last, lanes]
         ).astype(BF)
-    v_grad = AttnGrad(
-        1,
-        x_full,
-        lambda: gqkv_s[:, 2 * DC :],
-        stage_down,
-        pl.ds(DC, DC),
-        pl.ds(2 * DC, DC),
-    )
+    v_grad = AttnGrad(1, BY_BOTH, x_full, lambda: gqkv_s[:, 2 * DC :], 2 * DC, DC)
     v_grad.start()
     for half in HALVES:
         rows = tokens(half)
@@ -1182,17 +1237,12 @@
     for half in HALVES:
         in_sums[half].start()
     o_grad.relay()
-    gu_stage(3, row)
-    own_copies.append(local(stage_gu.at[3], land_mlp.at[0, :, GU]))
-    for copy in gu_sends:
-        sent(copy)
-    own_copies[1].wait()
-    both_lanes = pl.ds(0, 2 * DC)
-    qk_grad = AttnGrad(
-        2, x_full, lambda: gqkv_s[:, : 2 * DC], stage_gu, both_lanes, both_lanes
-    )
+    qk_grad = AttnGrad(2, BY_BOTH, x_full, lambda: gqkv_s[:, : 2 * DC], 0, 2 * DC)
     qk_grad.start()
     v_grad.relay()
+    grad_piece(3, 0)
+    grad_piece(3, 1)
+    late.append(local(stage_gu.at[3], land_mlp.at[0, :, pl.ds(0, 2 * FH)]))
     for half in HALVES:
         rows = tokens(half)
         work_s[1, rows, :] = middle_s[rows, :] + in_sums[half].finish()
@@ -1203,14 +1253,16 @@
     for slot, owner in enumerate((row_x, row_y, row_d)):
         arrived(gain_base + slot, gain_s.at[owner])
     gains_out[...] = gain_s[0] + gain_s[1] + gain_s[2] + gain_s[3]
-    for index, (slot, lanes) in enumerate(((1, DOWN), (1, GU), (2, DOWN), (2, GU))):
-        arrived(grad_base + 2 + index, land_mlp.at[slot, :, lanes])
+    for slot in (1, 2):
+        for part in range(3):
+            arrived(grad_base + 3 * slot + part, land_mlp.at[slot, :, grad_lanes(part)])
     for grad in (o_grad, v_grad, qk_grad):
         grad.finish()
     for copy in late:
         copy.wait()
     for copy in list(pending):
         sent(copy)
+    assert counter.used <= send_sem.shape[0], counter.used
 
 
 def total_kernel(
@@ -1255,7 +1307,7 @@
     hbm = pl.BlockSpec(memory_space=pl.ANY)
     vmem = pl.BlockSpec(memory_space=pltpu.VMEM)
     sds = jax.ShapeDtypeStruct
-    copies = 320
+    copies = 150
     landed = pl.pallas_call(
         block_kernel,
         out_shape=[
@@ -1265,7 +1317,7 @@
             sds((3, DR, 3 * FH), BF),
             sds((3, DR, 4 * DC), BF),
         ],
-        in_specs=[hbm] * 9 + [vmem] * 5,
+        in_specs=[hbm] * 14,
         out_specs=[hbm, hbm, vmem, hbm, hbm],
         scratch_shapes=[
             pltpu.VMEM((D, 3 * DC), BF),
@@ -1311,9 +1363,14 @@
             pltpu.VMEM((DR, 3 * FH), BF),
             pltpu.VMEM((DR, 4 * DC), BF),
             pltpu.VMEM((T, DC), BF),
+            pltpu.VMEM((1, D), F32),
+            pltpu.VMEM((1, D), F32),
+            pltpu.VMEM((1, D), F32),
+            pltpu.VMEM((1, D), F32),
+            pltpu.VMEM((1, T), jnp.int32),
             pltpu.SemaphoreType.DMA((copies,)),
             pltpu.SemaphoreType.DMA((copies,)),
-            pltpu.SemaphoreType.DMA((32,)),
+            pltpu.SemaphoreType.DMA((24,)),
         ],
         compiler_params=pltpu.CompilerParams(
             collective_id=0, has_side_effects=True, vmem_limit_bytes=64 * MIB
@@ -1337,7 +1394,7 @@
         mlp_gain[None, :],
         positions[None, :],
     )
-    step = 64
+    step = 256
 
     def rows_of(width):
         return pl.BlockSpec((step, width), lambda at: (at, 0))
@@ -1358,6 +1415,7 @@
             pl.BlockSpec((3, step, 4 * DC), lambda at: (0, at, 0)),
         ],
         out_specs=[rows_of(DC)] * 6 + [rows_of(2 * FH)] * 3 + [gain_spec] * 4,
+        compiler_params=pltpu.CompilerParams(vmem_limit_bytes=64 * MIB),
     )(*landed)
     return (*results[:9], *[gain[0] for gain in results[9:]])
 

time: 312 us -> 302 us (0.968)
  Pallas kernels: 306 us -> 297 us
    pallas_call x1, Pallas kernels: 297 us -> 290 us  [on_device_kernel(): pl.pallas_call(block_kernel, out_shape=[sds((T, DC), BF), sds((T, DC), F3...]
where the time goes in v4:
time: 302 us; the launch traced here: 298 us
  Pallas kernels  297 us (98%)
    pallas_call x1, Pallas kernels, on_device_kernel(): pl.pallas_call(block_kernel, out_shape=[sds((T, DC), BF), sds((T, DC), F3...  290 us
    pallas_call x1, Pallas kernels, on_device_kernel(): pl.pallas_call(total_kernel, grid=(DR // step,), out_shape=[sds((T, DC),...  6.21 us

profile of v4, /device:TPU:0, one launch (start us, length us, event | category | flops | bytes accessed | tf_op | source)
XLA Modules:
  0.0 297.6 jit_solution(15762932830147178035)
XLA Ops:
  0.7 290.3 %shard_map.237 = (bf16[512,256]{1,0:T(8,128)(2,1)}, f32[512,256]{1,0:T(8,128)}, f32[8,256]{1,0:T(8,128)}, bf16[3,512,1536]{2,1,0:T(8,128)(2,1)}, bf16[3,512,1024]{2,1,0:T(8,128)(2,1)}) custom-call(bf16[512,256]{1,0:T(8,128)(2,1)} %x_hbm.1, bf16[512,256]{1,0:T(8,128)(2,1)} %wq_hbm.1, bf16[512,256]{1,0:T(8,128)(2,1)} %wk_hbm.1, bf16[512,256]{1,0:T(8,128)(2,1)} %wv_hbm.1, ...), custom_call_target="tpu_custom_call" | custom-call | flops 26800001024 | bytes 16000000 | tf_op jit(solution)/shard_map/pallas_call | solution.py:1311
  290.9 6.2 %shard_map.238 = (bf16[512,256]{1,0:T(8,128)(2,1)}, f32[512,256]{1,0:T(8,128)}, f32[512,256]{1,0:T(8,128)}, f32[512,256]{1,0:T(8,128)}, f32[512,256]{1,0:T(8,128...) custom-call(bf16[512,256]{1,0:T(8,128)(2,1)} %get-tuple-element.31.l, ...), custom_call_target="tpu_custom_call" | custom-call | tf_op jit(solution)/shard_map/pallas_call | solution.py:1403

commit v5 on v4

--- a/solution.py
+++ b/solution.py
@@ -713,16 +713,16 @@
 
     def attn_relay(index):
         arrived(attn_base + index, attn_place(index, row_x))
-        part = attn_place(index, row_x, 0 if index < 3 else None)
+        part = attn_place(index, row_x, 0 if index < 2 else None)
         weight_send(attn_base + 8 + index, part, part, dev_y)
         arrived(attn_base + 4 + index, attn_place(index, row_y))
-        if index < 3:
+        if index < 2:
             part = attn_place(index, row_y, 1)
             weight_send(attn_base + 12 + index, part, part, dev_x)
 
     def attn_ready(index):
-        arrived(attn_base + 8 + index, attn_place(index, row_d, 0 if index < 3 else None))
-        if index < 3:
+        arrived(attn_base + 8 + index, attn_place(index, row_d, 0 if index < 2 else None))
+        if index < 2:
             arrived(attn_base + 12 + index, attn_place(index, row_d, 1))
 
     mlp_base = counter.take(9)
@@ -886,10 +886,10 @@
     branch_scaled(0)
     mid_gathers[0].pass_on(0)
     branch_done(1)
+    mlp_relay(2)
     mid_gathers[0].pass_on(2, 1, 3)
     branch_scaled(1)
     mid_gathers[1].pass_on(0)
-    mlp_relay(2)
     mid_gathers[1].pass_on(2, 1, 3)
     for pair in (2, 3, 1):
         weight_send(cot_base + pair - 1, cot_z.at[z_at], cot_z.at[z_at], dev_z[pair])
@@ -1077,22 +1077,23 @@
     grad_diagonal(0)
     grad_diagonal(1)
     mid_sums[0].planes(0, 1, 2, 3)
+    grad_relay(2)
     mid_sums[1].planes(0, 1)
     mid_done(0)
     mid_sums[1].planes(2, 3)
-    grad_relay(2)
+    grad_relay(0)
     grad_near(2)
     mid_scaled(0)
     gb_gathers[0].pass_on(0)
     mid_done(1)
+    grad_relay(1)
     grad_near(0)
     gb_gathers[0].pass_on(2, 1, 3)
     mid_scaled(1)
     gb_gathers[1].pass_on(0)
-    grad_relay(0)
     grad_near(1)
+    late = []
     gb_gathers[1].pass_on(2, 1, 3)
-    grad_relay(1)
     gain_s[row, 2:3, :] = jnp.sum(middle_s[...] * bhat_s[...], axis=0, keepdims=True)
     gb_gathers[0].finish_own()
     gb_gathers[1].finish_own()
@@ -1106,7 +1107,6 @@
     BY_BOTH = ((upper, 1), (lower, 2))
     neighbours = {1: dev_x, 2: dev_y}
     attn_grad_base = counter.take(3 * 6)
-    late = []
 
     class AttnGrad:
         def __init__(self, order, routes, left, right, start, size):
@@ -1125,16 +1125,20 @@
             piece = dot_tn(self.left[:, lanes_of(owner)], self.right())
             self.at(slot, whole)[...] = piece.astype(BF)
 
-        def start(self):
+        def diagonal(self):
             self.piece(0)
             for step, (rows, first) in enumerate(self.routes):
                 landing = rel_attn.at[rows, self.lanes]
                 send(self.base + step, self.at(0, rows), landing, neighbours[first])
+
+        def near(self):
             self.piece(1)
             self.piece(2)
             for step, (rows, first) in enumerate(self.routes):
                 landing = land_attn.at[first, rows, self.lanes]
                 send(self.base + 2 + step, self.at(first, rows), landing, neighbours[first])
+
+        def own(self):
             self.piece(3)
             late.append(local(self.at(3, whole), land_attn.at[0, :, self.lanes]))
 
@@ -1159,7 +1163,8 @@
     for gather in gf_gathers:
         gather.finish_sends()
     o_grad = AttnGrad(0, BY_BOTH, gb_full, lambda: att_s[...], 3 * DC, DC)
-    o_grad.start()
+    o_grad.diagonal()
+    o_grad.near()
 
     def attend_back(half):
         count = (half + 1) * HT
@@ -1215,7 +1220,8 @@
             probs_s[head, last, last].astype(BF), ga_s[last, lanes]
         ).astype(BF)
     v_grad = AttnGrad(1, BY_BOTH, x_full, lambda: gqkv_s[:, 2 * DC :], 2 * DC, DC)
-    v_grad.start()
+    v_grad.diagonal()
+    v_grad.near()
     for half in HALVES:
         rows = tokens(half)
         totals = scal_get(4, half)
@@ -1234,12 +1240,16 @@
         )
         for half in HALVES
     ]
-    for half in HALVES:
-        in_sums[half].start()
+    qk_grad = AttnGrad(2, BY_BOTH, x_full, lambda: gqkv_s[:, : 2 * DC], 0, 2 * DC)
+    qk_grad.diagonal()
+    in_sums[0].start()
+    qk_grad.near()
+    in_sums[1].start()
     o_grad.relay()
-    qk_grad = AttnGrad(2, BY_BOTH, x_full, lambda: gqkv_s[:, : 2 * DC], 0, 2 * DC)
-    qk_grad.start()
     v_grad.relay()
+    qk_grad.relay()
+    for grad in (o_grad, v_grad, qk_grad):
+        grad.own()
     grad_piece(3, 0)
     grad_piece(3, 1)
     late.append(local(stage_gu.at[3], land_mlp.at[0, :, pl.ds(0, 2 * FH)]))
@@ -1248,7 +1258,6 @@
         work_s[1, rows, :] = middle_s[rows, :] + in_sums[half].finish()
     late.append(local(work_s.at[1], grad_in))
     late.append(lo_copy)
-    qk_grad.relay()
 
     for slot, owner in enumerate((row_x, row_y, row_d)):
         arrived(gain_base + slot, gain_s.at[owner])

time: 302 us -> 293 us (0.970)
  Pallas kernels: 297 us -> 287 us
    pallas_call x1, Pallas kernels: 290 us -> 281 us  [on_device_kernel(): pl.pallas_call(block_kernel, out_shape=[sds((T, DC), BF), sds((T, DC), F3...]
where the time goes in v5:
time: 293 us; the launch traced here: 289 us
  Pallas kernels  287 us (98%)
    pallas_call x1, Pallas kernels, on_device_kernel(): pl.pallas_call(block_kernel, out_shape=[sds((T, DC), BF), sds((T, DC), F3...  281 us
    pallas_call x1, Pallas kernels, on_device_kernel(): pl.pallas_call(total_kernel, grid=(DR // step,), out_shape=[sds((T, DC),...  6.21 us

profile of v5, /device:TPU:0, one launch (start us, length us, event | category | flops | bytes accessed | tf_op | source)
XLA Modules:
  0.0 288.6 jit_solution(4765077353978478679)
XLA Ops:
  0.7 281.3 %shard_map.237 = (bf16[512,256]{1,0:T(8,128)(2,1)}, f32[512,256]{1,0:T(8,128)}, f32[8,256]{1,0:T(8,128)}, bf16[3,512,1536]{2,1,0:T(8,128)(2,1)}, bf16[3,512,1024]{2,1,0:T(8,128)(2,1)}) custom-call(bf16[512,256]{1,0:T(8,128)(2,1)} %x_hbm.1, bf16[512,256]{1,0:T(8,128)(2,1)} %wq_hbm.1, bf16[512,256]{1,0:T(8,128)(2,1)} %wk_hbm.1, bf16[512,256]{1,0:T(8,128)(2,1)} %wv_hbm.1, ...), custom_call_target="tpu_custom_call" | custom-call | flops 26800001024 | bytes 16000000 | tf_op jit(solution)/shard_map/pallas_call | solution.py:1320
  281.9 6.2 %shard_map.238 = (bf16[512,256]{1,0:T(8,128)(2,1)}, f32[512,256]{1,0:T(8,128)}, f32[512,256]{1,0:T(8,128)}, f32[512,256]{1,0:T(8,128)}, f32[512,256]{1,0:T(8,128...) custom-call(bf16[512,256]{1,0:T(8,128)(2,1)} %get-tuple-element.31.l, ...), custom_call_target="tpu_custom_call" | custom-call | tf_op jit(solution)/shard_map/pallas_call | solution.py:1412

commit v6 on v5

--- a/solution.py
+++ b/solution.py
@@ -948,10 +948,6 @@
         scale = lax.rsqrt(total / D + EPS)
         work_s[2, rows, 128:] = scale
         inner_s[rows, :] = inner * scale / D
-        ffn_hat = work_s[1, rows, :] * wide(scale)
-        out_lo[rows, :] = (middle_s[rows, :] + ffn_hat * mlp_gain).astype(BF)
-        cot = cot_z[z_at, rows, :].astype(F32)
-        return jnp.sum(cot * ffn_hat, axis=0, keepdims=True)
 
     forward_tiles(0)
     mlp_ready(2)
@@ -959,19 +955,23 @@
     mid_gathers[1].finish_own()
     mid_gathers[1].finish_other()
     forward_tiles(1)
+    ffn_sums[0].planes(0, 1)
     ffn_sums[1].start()
-    ffn_sums[0].planes(0, 1, 2, 3)
+    ffn_sums[0].planes(2, 3)
     ffn_sums[1].planes(0, 1)
     for pair in (1, 2, 3):
         arrived(cot_base + pair - 1, cot_z.at[z_pair[pair]])
     ffn_done(0)
     ffn_sums[1].planes(2, 3)
-    mlp_gain_part = ffn_scaled(0)
+    ffn_scaled(0)
     gf_gathers[0].pass_on(0)
     ffn_done(1)
     gf_gathers[0].pass_on(2, 1, 3)
-    gain_s[row, 3:4, :] = mlp_gain_part + ffn_scaled(1)
+    ffn_scaled(1)
     gf_gathers[1].pass_on(0, 2, 1, 3)
+    ffn_hat = work_s[1] * wide(work_s[2, :, 128:])
+    out_lo[...] = (middle_s[...] + ffn_hat * mlp_gain).astype(BF)
+    gain_s[row, 3:4, :] = jnp.sum(cot_z[z_at].astype(F32) * ffn_hat, axis=0, keepdims=True)
     lo_copy = local(out_lo, layer_out)
     gf_gathers[0].finish_own()
     gf_gathers[0].finish_other()
@@ -1064,6 +1064,25 @@
     def mid_scaled(half):
         inner, _ = scal_get(3, half)
         inner_s[tokens(half), :] = inner / D
+
+    def attend_back(half):
+        count = (half + 1) * HT
+        keys = pl.ds(0, count)
+
+        def attend_back_chunk(at, carry):
+            rows = aligned(at * chunk, chunk)
+            for head in range(2):
+                lanes = pl.ds(head * HD, HD)
+                grad_probs = dot_nt(ga_s[rows, lanes], low_s[2, keys, lanes])
+                probs = probs_s[head, rows, keys]
+                inner = jnp.sum(probs * grad_probs, axis=1, keepdims=True)
+                grad_scores = (probs * (grad_probs - inner)).astype(BF)
+                gs_s[head, rows, keys] = grad_scores
+                gqk_s[0, rows, lanes] = dot_nn(grad_scores, low_s[1, keys, lanes])
+            return carry
+
+        first = half * (HT // chunk)
+        lax.fori_loop(first, first + HT // chunk, attend_back_chunk, 0)
 
     backward_tiles(0)
     gf_gathers[0].finish_sends()
@@ -1093,12 +1112,14 @@
     gb_gathers[1].pass_on(0)
     grad_near(1)
     late = []
+    gb_gathers[0].finish_own()
+    ga_s[tokens(0), :] = dot_nn(gb_full[tokens(0), :], wo[...]).astype(BF)
     gb_gathers[1].pass_on(2, 1, 3)
+    attend_back(0)
     gain_s[row, 2:3, :] = jnp.sum(middle_s[...] * bhat_s[...], axis=0, keepdims=True)
-    gb_gathers[0].finish_own()
     gb_gathers[1].finish_own()
 
-    ga_s[...] = dot_nn(gb_full[...], wo[...]).astype(BF)
+    ga_s[tokens(1), :] = dot_nn(gb_full[tokens(1), :], wo[...]).astype(BF)
 
     whole = pl.ds(0, DR)
     upper = pl.ds(0, DR // 2)
@@ -1166,27 +1187,7 @@
     o_grad.diagonal()
     o_grad.near()
 
-    def attend_back(half):
-        count = (half + 1) * HT
-        keys = pl.ds(0, count)
-
-        def attend_back_chunk(at, carry):
-            rows = aligned(at * chunk, chunk)
-            for head in range(2):
-                lanes = pl.ds(head * HD, HD)
-                grad_probs = dot_nt(ga_s[rows, lanes], low_s[2, keys, lanes])
-                probs = probs_s[head, rows, keys]
-                inner = jnp.sum(probs * grad_probs, axis=1, keepdims=True)
-                grad_scores = (probs * (grad_probs - inner)).astype(BF)
-                gs_s[head, rows, keys] = grad_scores
-                gqk_s[0, rows, lanes] = dot_nn(grad_scores, low_s[1, keys, lanes])
-            return carry
-
-        first = half * (HT // chunk)
-        lax.fori_loop(first, first + HT // chunk, attend_back_chunk, 0)
-
-    for half in HALVES:
-        attend_back(half)
+    attend_back(1)
     early, last = pl.ds(0, HT), pl.ds(HT, HT)
     for head in range(2):
         lanes = pl.ds(head * HD, HD)

time: 293 us -> 289 us (0.986)
  Pallas kernels: 287 us -> 283 us
    pallas_call x1, Pallas kernels: 281 us -> 277 us  [on_device_kernel(): pl.pallas_call(block_kernel, out_shape=[sds((T, DC), BF), sds((T, DC), F3...]
where the time goes in v6:
time: 289 us; the launch traced here: 284 us
  Pallas kernels  283 us (98%)
    pallas_call x1, Pallas kernels, on_device_kernel(): pl.pallas_call(block_kernel, out_shape=[sds((T, DC), BF), sds((T, DC), F3...  277 us
    pallas_call x1, Pallas kernels, on_device_kernel(): pl.pallas_call(total_kernel, grid=(DR // step,), out_shape=[sds((T, DC),...  6.21 us

profile of v6, /device:TPU:0, one launch (start us, length us, event | category | flops | bytes accessed | tf_op | source)
XLA Modules:
  0.0 284.4 jit_solution(5119854788849728041)
XLA Ops:
  0.7 277.0 %shard_map.237 = (bf16[512,256]{1,0:T(8,128)(2,1)}, f32[512,256]{1,0:T(8,128)}, f32[8,256]{1,0:T(8,128)}, bf16[3,512,1536]{2,1,0:T(8,128)(2,1)}, bf16[3,512,1024]{2,1,0:T(8,128)(2,1)}) custom-call(bf16[512,256]{1,0:T(8,128)(2,1)} %x_hbm.1, bf16[512,256]{1,0:T(8,128)(2,1)} %wq_hbm.1, bf16[512,256]{1,0:T(8,128)(2,1)} %wk_hbm.1, bf16[512,256]{1,0:T(8,128)(2,1)} %wv_hbm.1, ...), custom_call_target="tpu_custom_call" | custom-call | flops 26800001024 | bytes 16000000 | tf_op jit(solution)/shard_map/pallas_call | solution.py:1321
  277.7 6.2 %shard_map.238 = (bf16[512,256]{1,0:T(8,128)(2,1)}, f32[512,256]{1,0:T(8,128)}, f32[512,256]{1,0:T(8,128)}, f32[512,256]{1,0:T(8,128)}, f32[512,256]{1,0:T(8,128...) custom-call(bf16[512,256]{1,0:T(8,128)(2,1)} %get-tuple-element.31.l, ...), custom_call_target="tpu_custom_call" | custom-call | tf_op jit(solution)/shard_map/pallas_call | solution.py:1413

commit v7 on v6

--- a/solution.py
+++ b/solution.py
@@ -796,6 +796,8 @@
     for half in HALVES:
         query, key = hat_s[0, tokens(half), :], hat_s[1, tokens(half), :]
         scal_send(0, half, query * query, key * key)
+    for pair in (2, 3, 1):
+        weight_send(cot_base + pair - 1, cot_z.at[z_at], cot_z.at[z_at], dev_z[pair])
     attn_relay(2)
     attn_relay(3)
     for index in range(3):
@@ -891,8 +893,6 @@
     branch_scaled(1)
     mid_gathers[1].pass_on(0)
     mid_gathers[1].pass_on(2, 1, 3)
-    for pair in (2, 3, 1):
-        weight_send(cot_base + pair - 1, cot_z.at[z_at], cot_z.at[z_at], dev_z[pair])
     mid_gathers[0].finish_own()
     mid_gathers[0].finish_other()
     mlp_ready(0)

time: 289 us -> 289 us (level)
  no operation moved by 1% of the time
where the time goes in v7:
time: 289 us; the launch traced here: 284 us
  Pallas kernels  283 us (98%)
    pallas_call x1, Pallas kernels, on_device_kernel(): pl.pallas_call(block_kernel, out_shape=[sds((T, DC), BF), sds((T, DC), F3...  277 us
    pallas_call x1, Pallas kernels, on_device_kernel(): pl.pallas_call(total_kernel, grid=(DR // step,), out_shape=[sds((T, DC),...  6.21 us

profile of v7, /device:TPU:0, one launch (start us, length us, event | category | flops | bytes accessed | tf_op | source)
XLA Modules:
  0.0 284.4 jit_solution(15253514301690356156)
XLA Ops:
  0.7 277.0 %shard_map.237 = (bf16[512,256]{1,0:T(8,128)(2,1)}, f32[512,256]{1,0:T(8,128)}, f32[8,256]{1,0:T(8,128)}, bf16[3,512,1536]{2,1,0:T(8,128)(2,1)}, bf16[3,512,1024]{2,1,0:T(8,128)(2,1)}) custom-call(bf16[512,256]{1,0:T(8,128)(2,1)} %x_hbm.1, bf16[512,256]{1,0:T(8,128)(2,1)} %wq_hbm.1, bf16[512,256]{1,0:T(8,128)(2,1)} %wk_hbm.1, bf16[512,256]{1,0:T(8,128)(2,1)} %wv_hbm.1, ...), custom_call_target="tpu_custom_call" | custom-call | flops 26800001024 | bytes 16000000 | tf_op jit(solution)/shard_map/pallas_call | solution.py:1321
  277.7 6.2 %shard_map.238 = (bf16[512,256]{1,0:T(8,128)(2,1)}, f32[512,256]{1,0:T(8,128)}, f32[512,256]{1,0:T(8,128)}, f32[512,256]{1,0:T(8,128)}, f32[512,256]{1,0:T(8,128...) custom-call(bf16[512,256]{1,0:T(8,128)(2,1)} %get-tuple-element.31.l, ...), custom_call_target="tpu_custom_call" | custom-call | tf_op jit(solution)/shard_map/pallas_call | solution.py:1413
